TPU v7x, 32 devices: a whole 2x2x4 slice. The times are simulated.
32 devices in a mesh: rep: 1, ep: 32 (over z, y, x, core), hid: 1.
Axes of the slice: x: 2, y: 2, z: 4, core: 2. Of those that a mesh axis runs over, the one named last changes fastest.
Arguments:
- tokens: bfloat16 [4096, 2048], P(('rep', 'ep')), may hold values from -6 to 6
- cotangent: bfloat16 [4096, 2048], P(('rep', 'ep')), may hold values from -2 to 2
- routing: float32 [4096, 8], P(('rep', 'ep')), may hold values from 0.05 to 0.5
- expert_ids: int32 [4096, 8], P(('rep', 'ep')), may hold values from 0 to 63, all different within a row; in each aligned block of 128 rows (0 to 127, 128 to 255, ...) at most 20 rows name the same one
- gate_weight: bfloat16 [64, 2048, 768], P('ep', None, 'hid'), may hold values from -0.125 to 0.125
- up_weight: bfloat16 [64, 2048, 768], P('ep', None, 'hid'), may hold values from -0.125 to 0.125
- down_weight: bfloat16 [64, 768, 2048], P('ep', 'hid'), may hold values from -0.21875 to 0.21875
Outputs:
- input_grad: float32 [4096, 2048], P(('rep', 'ep'), 'hid')
- gate_grad: float32 [4096, 8], P(('rep', 'ep'))
Inputs may be any that keep to these rules, and one draw needn't show every extreme that they name: `expert_ids`: among the 128 tokens of one index of ep (aligned blocks of rows), no expert is picked more than 20 times, a bound that some block reaches; the 8 picks of a token are different experts.
All inputs are finite; a program needn't handle non-finite values.
Results may differ from a plain program's by a relative error of at most 0.0029.
Values may be sent and summed in bfloat16 or wider, within the bound.
No kernel may reach another device: no remote copies, remote signals or barrier semaphores. Data moves between devices by JAX's collectives and lax.ppermute only.
A program may use at most 128 MiB of HBM per device.

v0:
```python
import jax
import jax.numpy as jnp
from jax import lax
from jax.sharding import PartitionSpec as P


def slot_rank(flat, experts):
    onehot = (flat[:, None] == jnp.arange(experts, dtype=jnp.int32)[None, :]).astype(jnp.int32)
    before = jnp.cumsum(onehot, axis=0) - onehot
    return jnp.sum(before * onehot, axis=1)


def expert_math(inputs, grads_in, w_gate, w_upper, w_down, w_joined):
    gate_pre = jnp.einsum("erd,edf->erf", inputs, w_gate, preferred_element_type=jnp.float32)
    up_pre = jnp.einsum("erd,edf->erf", inputs, w_upper, preferred_element_type=jnp.float32)
    upward = jnp.einsum("erd,efd->erf", grads_in, w_down, preferred_element_type=jnp.float32)
    sigma = jax.nn.sigmoid(gate_pre)
    silu_val = gate_pre * sigma
    hidden = silu_val * up_pre
    pick_gate = jnp.sum(hidden * upward, axis=2)
    gate_delta = (upward * up_pre * sigma * (1.0 + gate_pre * (1.0 - sigma))).astype(jnp.bfloat16)
    up_delta = (upward * silu_val).astype(jnp.bfloat16)
    deltas = jnp.concatenate([gate_delta, up_delta], axis=2)
    partial_value = jnp.einsum("erf,edf->erd", deltas, w_joined, preferred_element_type=jnp.float32)
    return (partial_value, pick_gate)


def combine_rows(returned, dest, token_of, routing, tok_rows):
    slots_all = returned.shape[0]
    mixing = (
        jnp.zeros((tok_rows, slots_all), jnp.float32).at[token_of, dest].set(routing.reshape(-1))
    )
    return jnp.dot(
        mixing, returned, precision=lax.Precision.HIGHEST, preferred_element_type=jnp.float32
    )


def local(tokens, cotangent, routing, expert_ids, gate_weight, up_weight, down_weight):
    count_ep = lax.axis_size("ep")
    local_experts = gate_weight.shape[0]
    experts = local_experts * count_ep
    tok_rows, top_picks = expert_ids.shape
    width = tokens.shape[1]
    capacity = 5 * tok_rows * top_picks // (4 * experts)
    flat = expert_ids.reshape(-1)
    dest = flat * capacity + slot_rank(flat, experts)
    token_of = jnp.arange(tok_rows * top_picks, dtype=jnp.int32) // top_picks
    slot_token = jnp.full((experts * capacity,), tok_rows, jnp.int32).at[dest].set(token_of)
    padding = jnp.zeros((1, width), tokens.dtype)
    bucket_shape = (count_ep, local_experts, capacity, width)
    token_rows = jnp.concatenate([tokens, padding], 0)[slot_token].reshape(bucket_shape)
    cotan_rows = jnp.concatenate([cotangent, padding], 0)[slot_token].reshape(bucket_shape)
    joined_weight = jnp.concatenate([gate_weight, up_weight], axis=2)
    inputs = lax.all_to_all(token_rows, "ep", split_axis=0, concat_axis=0, tiled=True)
    grads_in = lax.all_to_all(cotan_rows, "ep", split_axis=0, concat_axis=0, tiled=True)
    sources, owned, slots, row_width = inputs.shape
    inputs = inputs.transpose(1, 0, 2, 3).reshape(owned, sources * slots, row_width)
    grads_in = grads_in.transpose(1, 0, 2, 3).reshape(owned, sources * slots, row_width)
    partial_value, pick_gate = expert_math(
        inputs, grads_in, gate_weight, up_weight, down_weight, joined_weight
    )
    pick_gate = pick_gate.reshape(owned, sources, slots)
    partial_value = partial_value.reshape(owned, sources, slots, row_width).transpose(1, 0, 2, 3)
    returned = lax.all_to_all(partial_value, "ep", split_axis=0, concat_axis=0, tiled=True)
    gate_back = lax.all_to_all(
        pick_gate.transpose(1, 0, 2), "ep", split_axis=0, concat_axis=0, tiled=True
    )
    returned = returned.reshape(experts * capacity, returned.shape[3])
    weighted = combine_rows(returned, dest, token_of, routing, tok_rows)
    gate_grad = gate_back.reshape(-1)[dest].reshape(tok_rows, top_picks)
    input_grad = lax.psum_scatter(weighted, "hid", scatter_dimension=1, tiled=True)
    gate_total = lax.psum(gate_grad, "hid")
    return (input_grad, gate_total)


def solution(mesh):
    placed = (
        P(("rep", "ep"), None),
        P(("rep", "ep"), None),
        P(("rep", "ep"), None),
        P(("rep", "ep"), None),
        P("ep", None, "hid"),
        P("ep", None, "hid"),
        P("ep", "hid", None),
    )
    return jax.shard_map(
        local,
        mesh=mesh,
        in_specs=placed,
        out_specs=(P(("rep", "ep"), "hid"), P(("rep", "ep"), None)),
        check_vma=False,
    )
```

profile of v0, /device:TPU:0, one launch (start us, length us, event | category | flops | bytes accessed | tf_op | source)
XLA Modules:
  0.0 629.6 jit_solution(10250468809868440312)
XLA Ops:
  0.6 0.8 copy.27
  1.4 0.1 eq.29
  1.5 0.1 eq.25
  1.6 0.7 broadcast_multiply_fusion
  2.3 18.0 %reduce-window.6 = s32[64,8,128]{2,1,0:T(8,128)S(1)} reduce-window(s32[64,8,128]{2,1,0:T(8,128)S(1)} %fusion.19, s32[]{:T(128)} %constant.34.clone.1), window={size=1x1x128 pad=0_0x0_0x127_0}, to_apply=%region_0.0 | reduce-window | flops 8323072 | bytes 524292 | tf_op jit(solution)/shard_map/reduce-window
  20.3 0.1 slice.14
  20.5 0.1 copy.29
  20.7 0.1 copy.30
  20.7 0.1 broadcast_add_fusion
  20.9 0.1 copy.26
  21.0 0.1 mul.45
  21.1 0.1 fusion.18
  21.2 4.3 scatter_custom_fusion
  25.5 1.1 concatenate.17
  26.6 6.2 gather_fusion.1
  32.8 8.9 %reshape.127 = bf16[32,2,20,2048]{3,2,1,0:T(8,128)(2,1)} reshape(bf16[1280,2048]{1,0:T(8,128)(2,1)} %gather_fusion.1) | data formatting | bytes 10485760 | tf_op jit(solution)/shard_map/reshape | solution.py:51
  41.8 11.1 %copy.34 = bf16[32,2,20,2048]{3,1,2,0:T(2,128)(2,1)} copy(bf16[32,2,20,2048]{3,2,1,0:T(8,128)(2,1)} %reshape.127) | data formatting | bytes 10485760 | tf_op jit(solution)/shard_map/reshape | solution.py:51
  52.9 7.4 %all-to-all-start.1 = ((bf16[32,2,20,2048]{3,1,2,0:T(2,128)(2,1)}), bf16[32,2,20,2048]{3,1,2,0:T(2,128)(2,1)}, u32[]{:S(2)}, u32[]{:S(2)}) async-start(bf16[32,2,20,2048]{3,1,2,0:T(2,128)(2,1)} %copy.34), calls=%async_computation.1 | async-start | bytes 10485760 | tf_op jit(solution)/shard_map/all_to_all | solution.py:54
  60.4 6.1 gather_fusion
  66.5 8.9 %reshape.125 = bf16[32,2,20,2048]{3,2,1,0:T(8,128)(2,1)} reshape(bf16[1280,2048]{1,0:T(8,128)(2,1)} %gather_fusion) | data formatting | bytes 10485760 | tf_op jit(solution)/shard_map/reshape | solution.py:52
  75.4 11.1 %copy.32 = bf16[32,2,20,2048]{3,1,2,0:T(2,128)(2,1)} copy(bf16[32,2,20,2048]{3,2,1,0:T(8,128)(2,1)} %reshape.125) | data formatting | bytes 10485760 | tf_op jit(solution)/shard_map/reshape | solution.py:52
  86.5 90.5 %all-to-all-done.1 = bf16[32,2,20,2048]{3,1,2,0:T(2,128)(2,1)} async-done(((bf16[32,2,20,2048]{3,1,2,0:T(2,128)(2,1)}), bf16[32,2,20,2048]{3,1,2,0:T(2,128)(2,1)}, u32[]{:S(2)}, u32[]{:S(2)}) %all-to-all-start.1) | async-done | bytes 5242912 | tf_op jit(solution)/shard_map/all_to_all | solution.py:54
  177.1 3.8 all-to-all-start
  180.9 11.3 %fusion.6 = f32[2,640,768]{2,1,0:T(8,128)} fusion(bf16[2,2048,768]{2,1,0:T(8,128)(2,1)} %param.11, bf16[2,640,2048]{2,0,1:T(2,128)(2,1)} %bitcast.7), kind=kOutput, calls=%fused_computation.11 | convolution fusion | flops 4026531840 | bytes 15466496 | tf_op jit(solution)/shard_map/erd,edf->erf/dot_general | solution.py:14
  192.2 11.2 %fusion.8 = f32[2,640,768]{2,1,0:T(8,128)} fusion(bf16[2,2048,768]{2,1,0:T(8,128)(2,1)} %param.12, bf16[2,640,2048]{2,0,1:T(2,128)(2,1)} %bitcast.7), kind=kOutput, calls=%fused_computation.13 | convolution fusion | flops 4026531840 | bytes 15466496 | tf_op jit(solution)/shard_map/erd,edf->erf/dot_general | solution.py:15
  203.4 94.0 %all-to-all-done = bf16[32,2,20,2048]{3,1,2,0:T(2,128)(2,1)} async-done(((bf16[32,2,20,2048]{3,1,2,0:T(2,128)(2,1)}), bf16[32,2,20,2048]{3,1,2,0:T(2,128)(2,1)}, u32[]{:S(2)}, u32[]{:S(2)}) %all-to-all-start) | async-done | bytes 5242912 | tf_op jit(solution)/shard_map/all_to_all | solution.py:55
  297.5 15.1 %multiply_reduce_fusion = (f32[2,640]{1,0:T(2,128)S(1)}, bf16[2,640,768]{2,1,0:T(8,128)(2,1)S(1)}, bf16[2,640,768]{2,1,0:T(8,128)(2,1)}) fusion(f32[2,640,768]{2,1,0:T(8,128)} %fusion.8, f32[2,640,768]{2,1,0:T(8,128)} %fusion.6, bf16[2,768,2048]{2,1,0:T(8,128)(2,1)} %param.13, bf16[2,640,2048]{2,0,1:T(2,128)(2,1)} %bitcast.5), kind=kOutput, calls=%fused_computation.18 | convolution fusion | flops 4042259200 | bytes 23335936 | tf_op jit(solution)/shard_map/erd,efd->erf/dot_general | solution.py:16
  312.6 0.1 reshape.131
  312.7 0.6 copy.39
  313.3 3.5 all-to-all-start.3
  316.9 14.3 %fusion = f32[2,640,2048]{2,1,0:T(8,128)} fusion(bf16[2,2048,768]{2,1,0:T(8,128)(2,1)} %param.12, bf16[2,2048,768]{2,1,0:T(8,128)(2,1)} %param.11, bf16[2,640,768]{2,1,0:T(8,128)(2,1)} %get-tuple-element.8, bf16[2,640,768]{2,1,0:T(8,128)(2,1)S(1)} %get-tuple-element.7), kind=kOutput, calls=%fused_computation.5 | convolution fusion | flops 8086093824 | bytes 27000832 | tf_op jit(solution)/shard_map/erf,edf->erd/dot_general | solution.py:24
  331.2 18.7 %copy.37 = f32[2,640,2048]{2,0,1:T(2,128)} copy(f32[2,640,2048]{2,1,0:T(8,128)} %fusion) | data formatting | bytes 20971520 | tf_op jit(solution)/shard_map/erf,edf->erd/dot_general | solution.py:24
  349.9 0.0 copy-start.2
  349.9 6.0 all-to-all-start.2
  355.9 0.1 copy.31
  356.0 0.1 reshape.172
  356.1 0.1 multiply_reduce_fusion.1
  356.2 0.1 and_reduce_fusion
  356.3 4.5 scatter_custom_fusion.1
  360.8 0.1 reshape.137
  360.9 0.1 reshape.132
  361.0 6.6 %gather_fusion.2 = f32[1024]{0:T(1024)S(1)} fusion(f32[1280]{0:T(1024)S(1)} %reshape.132, s32[1024]{0:T(1024)S(1)} %broadcast_clamp_fusion), kind=kCustom, calls=%fused_computation.2 | custom fusion | bytes 12288 | tf_op jit(solution)/shard_map/gather | solution.py:70
  367.6 0.1 reshape.133
  367.7 0.7 copy.40
  368.4 219.8 %all-to-all-done.2 = f32[32,2,20,2048]{3,1,2,0:T(2,128)} async-done(((f32[32,2,20,2048]{3,1,2,0:T(2,128)}), f32[32,2,20,2048]{3,1,2,0:T(2,128)}, u32[]{:S(2)}, u32[]{:S(2)}) %all-to-all-start.2) | async-done | bytes 10485792 | tf_op jit(solution)/shard_map/all_to_all | solution.py:64
  588.1 17.8 %copy.38 = f32[32,2,20,2048]{3,2,1,0:T(8,128)} copy(f32[32,2,20,2048]{3,1,2,0:T(2,128)} %all-to-all-done.2) | data formatting | bytes 20971520 | tf_op jit(solution)/shard_map/all_to_all | solution.py:64
  606.0 12.9 %reshape.130 = f32[1280,2048]{1,0:T(8,128)} reshape(f32[32,2,20,2048]{3,2,1,0:T(8,128)} %copy.38) | data formatting | bytes 20971520 | tf_op jit(solution)/shard_map/reshape | solution.py:68
  618.9 10.6 %fusion.26 = f32[128,2048]{1,0:T(8,128)} fusion(f32[128,1280]{1,0:T(8,128)S(1)} %reshape.137, f32[1280,2048]{1,0:T(8,128)} %reshape.130), kind=kOutput, calls=%fused_computation.57 | convolution fusion | flops 4026531840 | bytes 12189696 | tf_op jit(solution)/shard_map/dot_general | solution.py:33
  (18 shorter events, 0.2 us)
Async XLA Ops:
  52.9 7.4 %copy-start = (bf16[128,2048]{1,0:T(8,128)(2,1)S(1)}, bf16[128,2048]{1,0:T(8,128)(2,1)}, u32[]{:S(2)}) copy-start(bf16[128,2048]{1,0:T(8,128)(2,1)} %param.8) | copy-start | bytes 1572868
  52.9 124.2 %all-to-all-start.1 = ((bf16[32,2,20,2048]{3,1,2,0:T(2,128)(2,1)}), bf16[32,2,20,2048]{3,1,2,0:T(2,128)(2,1)}, u32[]{:S(2)}, u32[]{:S(2)}) async-start(bf16[32,2,20,2048]{3,1,2,0:T(2,128)(2,1)} %copy.34), calls=%async_computation.1 | async-start | bytes 10485760 | tf_op jit(solution)/shard_map/all_to_all | solution.py:54
  177.1 120.4 %all-to-all-start = ((bf16[32,2,20,2048]{3,1,2,0:T(2,128)(2,1)}), bf16[32,2,20,2048]{3,1,2,0:T(2,128)(2,1)}, u32[]{:S(2)}, u32[]{:S(2)}) async-start(bf16[32,2,20,2048]{3,1,2,0:T(2,128)(2,1)} %copy.32), calls=%async_computation | async-start | bytes 10485760 | tf_op jit(solution)/shard_map/all_to_all | solution.py:55
  313.3 36.6 %all-to-all-start.3 = ((f32[32,2,20]{2,1,0:T(2,128)}), f32[32,2,20]{2,1,0:T(2,128)S(1)}, u32[]{:S(2)}, u32[]{:S(2)}) async-start(f32[32,2,20]{2,1,0:T(2,128)} %copy.39), calls=%async_computation.3 | async-start | bytes 65536 | tf_op jit(solution)/shard_map/all_to_all | solution.py:65
  349.9 6.0 copy-start.1
  349.9 6.2 copy-start.3
  349.9 6.3 copy-start.2
  349.9 238.2 %all-to-all-start.2 = ((f32[32,2,20,2048]{3,1,2,0:T(2,128)}), f32[32,2,20,2048]{3,1,2,0:T(2,128)}, u32[]{:S(2)}, u32[]{:S(2)}) async-start(f32[32,2,20,2048]{3,1,2,0:T(2,128)} %bitcast.35), calls=%async_computation.2 | async-start | bytes 20971520 | tf_op jit(solution)/shard_map/all_to_all | solution.py:64
where the time goes:
time: 636 us; the launch traced here: 630 us
  waiting for transfers between devices  404 us (64%)
  local copies, waits for them, and re-layouts  122 us (19%)
  matrix products  62.6 us (10%)
  starting transfers between devices  20.7 us (3%)
  other arithmetic  19.2 us (3%)
    all_to_all x1, waiting for transfers between devices, local(): lax.all_to_all(partial_value, 'ep', split_axis=0, concat_axis=0, tiled=True)  220 us
    all_to_all x1, waiting for transfers between devices, local(): lax.all_to_all(cotan_rows, 'ep', split_axis=0, concat_axis=0, tiled=True)  94 us
    all_to_all x1, waiting for transfers between devices, local(): lax.all_to_all(token_rows, 'ep', split_axis=0, concat_axis=0, tiled=True)  90.5 us
    reshape x2, local copies, waits for them, and re-layouts, local(): jnp.concatenate([cotangent, padding], 0)[slot_token].reshape(bucket_shape)  20.1 us
    reshape x2, local copies, waits for them, and re-layouts, local(): jnp.concatenate([tokens, padding], 0)[slot_token].reshape(bucket_shape)  20 us
    dot_general x1, local copies, waits for them, and re-layouts, expert_math(): jnp.einsum('erf,edf->erd', deltas, w_joined, preferred_element_type=jnp.f...  18.7 us
    another operation x3, other arithmetic  18.2 us
    all_to_all x1, local copies, waits for them, and re-layouts, local(): lax.all_to_all(partial_value, 'ep', split_axis=0, concat_axis=0, tiled=True)  17.8 us
  transfers between devices with their start and end apart: 4, of which 3 were waited for; matrix products, arithmetic and copies ran while one was open for 15% of the time, Pallas kernels for 0%

commit v1 on v0

v1 whole, which is shorter than its diff:
```python
import functools
import math

import jax
import jax.numpy as jnp
from jax import lax
from jax.experimental import pallas as pl
from jax.experimental.pallas import tpu as pltpu
from jax.sharding import PartitionSpec as P

BF16 = jnp.bfloat16
F32 = jnp.float32
VMEM_LIMIT = 56 * 1024 * 1024


def full(shape):
    return pl.BlockSpec(shape, lambda *_: (0,) * len(shape))


def call(kernel, out_shape, grid, in_specs, out_specs, flops, moved, scratch=()):
    return pl.pallas_call(
        kernel,
        out_shape=out_shape,
        grid=grid,
        in_specs=in_specs,
        out_specs=out_specs,
        scratch_shapes=scratch,
        cost_estimate=pl.CostEstimate(flops=flops, bytes_accessed=moved, transcendentals=0),
        compiler_params=pltpu.CompilerParams(vmem_limit_bytes=VMEM_LIMIT),
    )


def picks_of(ids, base, experts):
    tokens, top = ids.shape
    expert = lax.broadcasted_iota(jnp.int32, (tokens, experts), 1).astype(F32) + base
    hits = [ids[:, k : k + 1] == expert for k in range(top)]
    return hits, functools.reduce(jnp.logical_or, hits)


def earlier_picks(pick):
    tokens = pick.shape[0]
    row = lax.broadcasted_iota(jnp.int32, (tokens, tokens), 0)
    column = lax.broadcasted_iota(jnp.int32, (tokens, tokens), 1)
    below = jnp.where(column < row, 1.0, 0.0).astype(BF16)
    return jnp.dot(below, jnp.where(pick, 1.0, 0.0).astype(BF16), preferred_element_type=F32)


def plan_kernel(owned, parts, capacity, base_ref, meta_ref, pack_ref, high_ref, low_ref):
    tokens = meta_ref.shape[1]
    slots = pack_ref.shape[0]
    experts = slots // (parts * capacity)
    top = meta_ref.shape[2] // 2
    base = base_ref[0, 0]
    slot = lax.broadcasted_iota(jnp.int32, (1, slots), 1)
    rank_of = (slot % capacity).astype(F32)
    part_of = (slot // capacity) % parts
    expert_of = slot // (capacity * parts)
    expert = lax.broadcasted_iota(jnp.int32, (experts, slots), 0)
    spread = jnp.where(expert == expert_of, 1.0, 0.0).astype(BF16)
    for part in range(parts):
        ids, routing = meta_ref[part, :, :top], meta_ref[part, :, top:]
        hits, pick = picks_of(ids, base, experts)
        weight = functools.reduce(
            jnp.add, [jnp.where(hits[k], routing[:, k : k + 1], 0.0) for k in range(top)]
        )
        rank = jnp.where(pick, earlier_picks(pick), -1.0).astype(BF16)
        high = weight.astype(BF16)
        low = (weight - high.astype(F32)).astype(BF16)
        ranks = jnp.dot(rank, spread, preferred_element_type=F32)
        here = jnp.logical_and(ranks == rank_of, part_of == part)
        rows = slice(part * tokens, (part + 1) * tokens)
        for out, value in ((high_ref, high), (low_ref, low)):
            spread_value = jnp.dot(value, spread, preferred_element_type=F32)
            out[rows, :] = jnp.where(here, spread_value, 0.0).astype(BF16)
        pack_ref[:, rows] = jnp.where(here, 1.0, 0.0).T.astype(BF16)


def plan(base, meta, owned, peers, capacity):
    parts, tokens, _ = meta.shape
    slots = peers * owned * parts * capacity
    rows = parts * tokens
    outs = (
        jax.ShapeDtypeStruct((slots, rows), BF16),
        jax.ShapeDtypeStruct((rows, slots), BF16),
        jax.ShapeDtypeStruct((rows, slots), BF16),
    )
    return call(
        functools.partial(plan_kernel, owned, parts, capacity),
        outs,
        (),
        [pl.BlockSpec(memory_space=pltpu.SMEM), pl.BlockSpec(memory_space=pltpu.VMEM)],
        [pl.BlockSpec(memory_space=pltpu.VMEM)] * 3,
        8 * slots * rows,
        6 * slots * rows,
    )(base, meta)


def pack_kernel(pack_ref, *refs):
    rows_refs, out_ref = refs[:-1], refs[-1]
    tokens = rows_refs[0].shape[0]
    total = None
    for part, ref in enumerate(rows_refs):
        term = jnp.dot(
            pack_ref[:, part * tokens : (part + 1) * tokens], ref[...], preferred_element_type=F32
        )
        total = term if total is None else total + term
    out_ref[...] = total.astype(out_ref.dtype)


def pack(matrix, rows):
    slots, sources = matrix.shape
    tokens, width = rows[0].shape
    block = math.gcd(width, 512)
    return call(
        pack_kernel,
        jax.ShapeDtypeStruct((slots, width), rows[0].dtype),
        (width // block,),
        [full((slots, sources))] + [pl.BlockSpec((tokens, block), lambda j: (0, j))] * len(rows),
        pl.BlockSpec((slots, block), lambda j: (0, j)),
        2 * slots * sources * width,
        2 * (slots + sources) * width,
    )(matrix, *rows)


def expert_kernel(pieces, token_ref, cotan_ref, gate_ref, up_ref, down_ref, *outs):
    peers, rows, width = token_ref.shape

    def joined(ref):
        return jnp.concatenate([ref[p].astype(F32) for p in range(peers)], axis=0).astype(BF16)

    inputs, grads_in = joined(token_ref), joined(cotan_ref)
    gate_pre = jnp.dot(inputs, gate_ref[...], preferred_element_type=F32)
    up_pre = jnp.dot(inputs, up_ref[...], preferred_element_type=F32)
    across = (((1,), (1,)), ((), ()))
    upward = lax.dot_general(grads_in, down_ref[...], across, preferred_element_type=F32)
    sigma = 1.0 / (1.0 + jnp.exp(-gate_pre))
    silu_val = gate_pre * sigma
    outs[-1][...] = jnp.sum(silu_val * up_pre * upward, axis=1, keepdims=True)
    gate_delta = (upward * up_pre * sigma * (1.0 + gate_pre * (1.0 - sigma))).astype(BF16)
    up_delta = (upward * silu_val).astype(BF16)
    step = width // pieces
    for j in range(pieces):
        columns = slice(j * step, (j + 1) * step)
        partial = lax.dot_general(gate_delta, gate_ref[columns, :], across, preferred_element_type=F32)
        partial += lax.dot_general(up_delta, up_ref[columns, :], across, preferred_element_type=F32)
        for p in range(peers):
            outs[j][p] = partial[p * rows : (p + 1) * rows].astype(BF16)


def experts_of(token_rows, cotan_rows, w_gate, w_upper, w_down, pieces):
    peers, owned, rows, width = token_rows.shape
    hidden = w_gate.shape[2]
    row_spec = pl.BlockSpec((peers, None, rows, width), lambda e: (0, e, 0, 0))
    step = width // pieces
    outs = [jax.ShapeDtypeStruct((peers, owned, rows, step), BF16)] * pieces
    out_specs = [pl.BlockSpec((peers, None, rows, step), lambda e: (0, e, 0, 0))] * pieces
    outs.append(jax.ShapeDtypeStruct((owned, peers * rows, 1), F32))
    out_specs.append(pl.BlockSpec((None, peers * rows, 1), lambda e: (e, 0, 0)))
    *partial, gate = call(
        functools.partial(expert_kernel, pieces),
        outs,
        (owned,),
        [
            row_spec,
            row_spec,
            pl.BlockSpec((None, width, hidden), lambda e: (e, 0, 0)),
            pl.BlockSpec((None, width, hidden), lambda e: (e, 0, 0)),
            pl.BlockSpec((None, hidden, width), lambda e: (e, 0, 0)),
        ],
        out_specs,
        10 * owned * peers * rows * width * hidden,
        6 * owned * width * hidden + 6 * owned * peers * rows * width,
    )(token_rows, cotan_rows, w_gate, w_upper, w_down)
    return partial, gate


def combine_kernel(parts, high_ref, low_ref, slots_ref, *outs):
    tokens = outs[0].shape[0]
    rows = slots_ref[...]
    total = jnp.dot(high_ref[...], rows, preferred_element_type=F32)
    total += jnp.dot(low_ref[...], rows, preferred_element_type=F32)
    for part in range(parts):
        outs[part][...] = total[part * tokens : (part + 1) * tokens].astype(outs[part].dtype)


def combine(high, low, returned, dtypes):
    sources, slots = high.shape
    width = returned.shape[1]
    parts = len(dtypes)
    tokens = sources // parts
    block = math.gcd(width, 512)
    return call(
        functools.partial(combine_kernel, parts),
        [jax.ShapeDtypeStruct((tokens, width), kind) for kind in dtypes],
        (width // block,),
        [full((sources, slots)), full((sources, slots)), pl.BlockSpec((slots, block), lambda j: (0, j))],
        [pl.BlockSpec((tokens, block), lambda j: (0, j))] * parts,
        4 * slots * sources * width,
        2 * (slots + 2 * sources) * width,
    )(high, low, returned)


def gate_kernel(capacity, experts, ids_ref, gate_ref, out_ref):
    ids = ids_ref[...]
    top = ids.shape[1]
    hits, pick = picks_of(ids, 0.0, experts)
    before = earlier_picks(pick)
    slots = gate_ref.shape[1]
    slot = lax.broadcasted_iota(jnp.int32, (1, slots), 1).astype(F32)
    gate = gate_ref[...]
    for k in range(top):
        rank = jnp.sum(jnp.where(hits[k], before, 0.0), axis=1, keepdims=True)
        dest = ids[:, k : k + 1] * capacity + rank
        out_ref[:, k : k + 1] = jnp.sum(jnp.where(slot == dest, gate, 0.0), axis=1, keepdims=True)


def gates_home(ids, gate, capacity, experts):
    tokens, top = ids.shape
    return call(
        functools.partial(gate_kernel, capacity, experts),
        jax.ShapeDtypeStruct((tokens, top), F32),
        (),
        [pl.BlockSpec(memory_space=pltpu.VMEM)] * 2,
        pl.BlockSpec(memory_space=pltpu.VMEM),
        3 * tokens * top * gate.shape[1],
        4 * tokens * top,
    )(ids, gate)


def local(tokens, cotangent, routing, expert_ids, gate_weight, up_weight, down_weight):
    count_ep = lax.axis_size("ep")
    owned = gate_weight.shape[0]
    experts = owned * count_ep
    tok_rows, top_picks = expert_ids.shape
    width = tokens.shape[1]
    capacity = 5 * tok_rows * top_picks // (4 * experts)

    peers = math.gcd(count_ep, 8)
    layers = count_ep // peers
    in_layer = [[layer * peers + i for i in range(peers)] for layer in range(layers)]
    parts = min(layers, 8 // math.gcd(8, capacity))
    chunks = [list(range(first, first + parts)) for first in range(0, layers, parts)]
    tail_pieces = 2

    def shift(value, by):
        pairs = [(i, (i + by * peers) % count_ep) for i in range(count_ep)]
        return lax.ppermute(value, "ep", pairs)

    def exchange(value):
        return lax.all_to_all(value, "ep", 0, 0, tiled=True, axis_index_groups=in_layer)

    layer = lax.axis_index("ep") // peers
    base = (layer * (peers * owned)).astype(F32).reshape(1, 1)
    ids = expert_ids.astype(F32)
    meta = jnp.concatenate([ids, routing], axis=1)
    metas = [meta] + [shift(meta, by) for by in range(1, layers)]
    token_at, cotan_at = {0: tokens}, {0: cotangent}
    for chunk in chunks:
        for by in chunk:
            if by:
                token_at[by] = shift(tokens, by)
        for by in chunk:
            if by:
                cotan_at[by] = shift(cotangent, by)

    plans, received = [], []
    for chunk in chunks:
        matrix, high, low = plan(base, jnp.stack([metas[by] for by in chunk]), owned, peers, capacity)
        plans.append((high, low))
        shape = (peers, owned * parts * capacity, width)
        token_rows = exchange(pack(matrix, [token_at[by] for by in chunk]).reshape(shape))
        cotan_rows = exchange(pack(matrix, [cotan_at[by] for by in chunk]).reshape(shape))
        received.append((token_rows, cotan_rows))

    gates, home = [], {}
    for number, chunk in enumerate(chunks):
        pieces = tail_pieces if number == len(chunks) - 1 else 1
        shape = (peers, owned, parts * capacity, width)
        token_rows, cotan_rows = [rows.reshape(shape) for rows in received[number]]
        partial, gate = experts_of(token_rows, cotan_rows, gate_weight, up_weight, down_weight, pieces)
        gates.append(gate.reshape(owned, peers, parts, capacity))
        high, low = plans[number]
        for j, piece in enumerate(partial):
            step = piece.shape[3]
            returned = exchange(piece.reshape(peers, owned * parts * capacity, step))
            kinds = [F32 if by == 0 else BF16 for by in chunk]
            sums = combine(high, low, returned.reshape(-1, step), kinds)
            for by, rows in zip(chunk, sums):
                back = rows if by == 0 else shift(rows, -by)
                home.setdefault(by, []).append(back)

    gate_slots = jnp.concatenate(gates, axis=2).transpose(2, 1, 0, 3)
    order = lax.rem(layer - jnp.arange(layers, dtype=jnp.int32) + layers, layers)
    gate_slots = gate_slots[order].reshape(count_ep, owned * capacity)
    gate_back = lax.all_to_all(gate_slots, "ep", 0, 0, tiled=True)
    gate_grad = gates_home(ids, gate_back.reshape(1, experts * capacity), capacity, experts)

    columns = []
    step = width // tail_pieces
    for j in range(tail_pieces):
        total = None
        for by in range(layers):
            rows = home[by]
            value = rows[j] if len(rows) > 1 else rows[0][:, j * step : (j + 1) * step]
            value = value.astype(F32)
            total = value if total is None else total + value
        columns.append(total)
    input_grad = jnp.concatenate(columns, axis=1)
    if lax.axis_size("hid") > 1:
        input_grad = lax.psum_scatter(input_grad, "hid", scatter_dimension=1, tiled=True)
        gate_grad = lax.psum(gate_grad, "hid")
    return (input_grad, gate_grad)


def solution(mesh):
    placed = (
        P(("rep", "ep"), None),
        P(("rep", "ep"), None),
        P(("rep", "ep"), None),
        P(("rep", "ep"), None),
        P("ep", None, "hid"),
        P("ep", None, "hid"),
        P("ep", "hid", None),
    )
    return jax.shard_map(
        local,
        mesh=mesh,
        in_specs=placed,
        out_specs=(P(("rep", "ep"), "hid"), P(("rep", "ep"), None)),
        check_vma=False,
    )
```

time: 636 us -> 328 us (0.52)
  waiting for transfers between devices: 404 us -> 125 us
  local copies, waits for them, and re-layouts: 122 us -> 13.7 us
  Pallas kernels: 0 us -> 74.4 us
  matrix products: 62.6 us -> 0 us
  starting transfers between devices: 20.7 us -> 72.2 us
  blocking collectives: 0 us -> 36.6 us
  other arithmetic: 19.2 us -> 4.84 us
    all_to_all x4 -> x7, waiting for transfers between devices: 404 us -> 42.6 us  [the longest x1 25.3 us: local(): gate_back = lax.all_to_all(gate_slots, 'ep', 0, 0, tiled=True)]
    ppermute x0 -> x14, waiting for transfers between devices: none -> 82 us  [shift(): return lax.ppermute(value, 'ep', pairs)]
    pallas_call x0 -> x12, Pallas kernels: none -> 74.4 us  [the longest x2 34.6 us: experts_of(): call(functools.partial(expert_kernel, pieces), outs, (owned,), [row_spec,...]
    dot_general x5 -> x0, matrix products: 62.6 us -> none  [the longest x1 15.1 us: expert_math(): jnp.einsum('erd,efd->erf', grads_in, w_down, preferred_element_type=jnp.f...]
    reshape x9 -> x5, local copies, waits for them, and re-layouts: 53.4 us -> 0.9 us  [the longest x1 0.68 us: local(): gate_back.reshape(1, experts * capacity)]
    ppermute x0 -> x14, starting transfers between devices: none -> 45.7 us  [shift(): return lax.ppermute(value, 'ep', pairs)]
    all_to_all x0 -> x1, blocking collectives: none -> 36.6 us  [exchange(): lax.all_to_all(value, 'ep', 0, 0, tiled=True, axis_index_groups=in_layer)]
    dot_general x1 -> x0, local copies, waits for them, and re-layouts: 18.7 us -> none  [expert_math(): jnp.einsum('erf,edf->erd', deltas, w_joined, preferred_element_type=jnp.f...]
  transfers between devices with their start and end apart: 4 -> 21, of which waited for: 3 -> 9; matrix products, arithmetic and copies ran while one was open for 15% -> 2% of each run, Pallas kernels for 0% -> 21%
where the time goes in v1:
time: 328 us; the launch traced here: 327 us
  waiting for transfers between devices  125 us (38%)
  Pallas kernels  74.4 us (23%)
  starting transfers between devices  72.2 us (22%)
  blocking collectives  36.6 us (11%)
  local copies, waits for them, and re-layouts  13.7 us (4%)
  other arithmetic  4.84 us (1%)
    ppermute x14, waiting for transfers between devices, shift(): return lax.ppermute(value, 'ep', pairs)  82 us
    ppermute x14, starting transfers between devices, shift(): return lax.ppermute(value, 'ep', pairs)  45.7 us
    all_to_all x1, blocking collectives, exchange(): lax.all_to_all(value, 'ep', 0, 0, tiled=True, axis_index_groups=in_layer)  36.6 us
    pallas_call x2, Pallas kernels, experts_of(): call(functools.partial(expert_kernel, pieces), outs, (owned,), [row_spec,...  34.6 us
    all_to_all x1, waiting for transfers between devices, local(): gate_back = lax.all_to_all(gate_slots, 'ep', 0, 0, tiled=True)  25.3 us
    all_to_all x6, starting transfers between devices, exchange(): lax.all_to_all(value, 'ep', 0, 0, tiled=True, axis_index_groups=in_layer)  23.9 us
    pallas_call x4, Pallas kernels, pack(): call(pack_kernel, jax.ShapeDtypeStruct((slots, width), rows[0].dtype), (w...  19.5 us
    all_to_all x6, waiting for transfers between devices, exchange(): lax.all_to_all(value, 'ep', 0, 0, tiled=True, axis_index_groups=in_layer)  17.4 us
  transfers between devices with their start and end apart: 21, of which 9 were waited for; matrix products, arithmetic and copies ran while one was open for 2% of the time, Pallas kernels for 21%

profile of v1, /device:TPU:0, one launch (start us, length us, event | category | flops | bytes accessed | tf_op | source)
XLA Modules:
  0.0 327.2 jit_solution(11076529330007583144)
XLA Ops:
  0.6 3.1 collective-permute-start.1
  5.1 1.6 collective-permute-start
  6.7 11.4 %collective-permute-done = f32[128,16]{0,1:T(8,128)S(1)} collective-permute-done((f32[128,16]{0,1:T(8,128)S(1)}, f32[128,16]{0,1:T(8,128)S(1)}, u32[]{:S(2)}, u32[]{:S(2)}) %collective-permute-start) | collective-permute-done | bytes 8224 | tf_op jit(solution)/shard_map/ppermute | solution.py:247
  18.0 0.8 copy.33.meta_ref
  18.8 2.9 shard_map.86
  21.7 0.8 copy-done.7
  22.5 4.9 %shard_map.87 = bf16[640,2048]{1,0:T(8,128)(2,1)} custom-call(bf16[640,256]{1,0:T(8,128)(2,1)} %get-tuple-element.21.pack_ref, bf16[128,2048]{1,0:T(8,128)(2,1)} %refs_0_.2, bf16[128,2048]{1,0:T(8,128)(2,1)} %copy-done.7), custom_call_target="tpu_custom_call" | custom-call | flops 671088640 | bytes 3670016 | tf_op jit(solution)/shard_map/pallas_call | solution.py:114
  27.3 3.9 %all-to-all-start = ((bf16[8,80,2048]{2,1,0:T(8,128)(2,1)}), bf16[8,80,2048]{2,1,0:T(8,128)(2,1)S(1)}, u32[]{:S(2)}, u32[]{:S(2)}) async-start(bf16[8,80,2048]{2,1,0:T(8,128)(2,1)} %bitcast.25), calls=%async_computation | async-start | bytes 5242880 | tf_op jit(solution)/shard_map/all_to_all | solution.py:250
  31.2 0.8 collective-permute-start.6
  32.0 1.3 collective-permute-start.7
  33.3 2.3 collective-permute-start.5
  35.7 21.7 %collective-permute-done.5 = f32[128,16]{0,1:T(8,128)S(1)} collective-permute-done((f32[128,16]{0,1:T(8,128)S(1)}, f32[128,16]{0,1:T(8,128)S(1)}, u32[]{:S(2)}, u32[]{:S(2)}) %collective-permute-start.5) | collective-permute-done | bytes 8224 | tf_op jit(solution)/shard_map/ppermute | solution.py:247
  57.4 11.2 %collective-permute-done.4 = f32[128,16]{0,1:T(8,128)S(1)} collective-permute-done((f32[128,16]{0,1:T(8,128)S(1)}, f32[128,16]{0,1:T(8,128)S(1)}, u32[]{:S(2)}, u32[]{:S(2)}) %collective-permute-start.4) | collective-permute-done | bytes 8224 | tf_op jit(solution)/shard_map/ppermute | solution.py:247
  69.4 2.9 shard_map.91
  72.3 4.9 %shard_map.92 = bf16[640,2048]{1,0:T(8,128)(2,1)} custom-call(bf16[640,256]{1,0:T(8,128)(2,1)} %get-tuple-element.27.pack_ref, bf16[128,2048]{1,0:T(8,128)(2,1)} %collective-permute-done.6.refs_0_, bf16[128,2048]{1,0:T(8,128)(2,1)} %collective-permute-done.7.refs_1_), custom_call_target="tpu_custom_call" | custom-call | flops 671088640 | bytes 3670016 | tf_op jit(solution)/shard_map/pallas_call | solution.py:114
  77.2 1.5 copy-done
  78.7 4.4 %all-to-all-start.3 = ((bf16[8,80,2048]{2,1,0:T(8,128)(2,1)}), bf16[8,80,2048]{2,1,0:T(8,128)(2,1)}, u32[]{:S(2)}, u32[]{:S(2)}) async-start(bf16[8,80,2048]{2,1,0:T(8,128)(2,1)} %bitcast.26), calls=%async_computation.3 | async-start | bytes 5242880 | tf_op jit(solution)/shard_map/all_to_all | solution.py:250
  83.2 2.8 collective-permute-start.9
  86.0 23.5 %collective-permute-done.8.refs_0_ = bf16[128,2048]{1,0:T(8,128)(2,1)S(1)} collective-permute-done((bf16[128,2048]{1,0:T(8,128)(2,1)S(1)}, bf16[128,2048]{1,0:T(8,128)(2,1)S(1)}, u32[]{:S(2)}, u32[]{:S(2)}) %collective-permute-start.8) | collective-permute-done | bytes 524320 | tf_op jit(solution)/shard_map/ppermute | solution.py:247
  110.2 0.8 copy-done.9
  111.0 4.9 %shard_map.93 = bf16[640,2048]{1,0:T(8,128)(2,1)} custom-call(bf16[640,256]{1,0:T(8,128)(2,1)} %get-tuple-element.27.pack_ref, bf16[128,2048]{1,0:T(8,128)(2,1)} %copy-done.8, bf16[128,2048]{1,0:T(8,128)(2,1)} %copy-done.9), custom_call_target="tpu_custom_call" | custom-call | flops 671088640 | bytes 3670016 | tf_op jit(solution)/shard_map/pallas_call | solution.py:114
  115.9 3.9 %all-to-all-start.4 = ((bf16[8,80,2048]{2,1,0:T(8,128)(2,1)}), bf16[8,80,2048]{2,1,0:T(8,128)(2,1)S(1)}, u32[]{:S(2)}, u32[]{:S(2)}) async-start(bf16[8,80,2048]{2,1,0:T(8,128)(2,1)} %bitcast.27), calls=%async_computation.4 | async-start | bytes 5242880 | tf_op jit(solution)/shard_map/all_to_all | solution.py:250
  119.8 10.9 %collective-permute-start.2 = (bf16[128,2048]{1,0:T(8,128)(2,1)S(1)}, bf16[128,2048]{1,0:T(8,128)(2,1)S(1)}, u32[]{:S(2)}, u32[]{:S(2)}) collective-permute-start(bf16[128,2048]{1,0:T(8,128)(2,1)S(1)} %copy-done.6), channel_id=1, source_target_pairs={{0,8},{1,9},{2,10},{3,11},{4,12},{5,13},{6,14},{7,15},{8,16},{9,17... | collective-permute-start | bytes 1572872 | tf_op jit(solution)/shard_map/ppermute | solution.py:247
  130.7 14.1 %collective-permute-done.2.refs_1_ = bf16[128,2048]{1,0:T(8,128)(2,1)S(1)} collective-permute-done((bf16[128,2048]{1,0:T(8,128)(2,1)S(1)}, bf16[128,2048]{1,0:T(8,128)(2,1)S(1)}, u32[]{:S(2)}, u32[]{:S(2)}) %collective-permute-start.2) | collective-permute-done | bytes 524320 | tf_op jit(solution)/shard_map/ppermute | solution.py:247
  144.8 0.8 copy-done.10
  145.6 4.9 %shard_map.88 = bf16[640,2048]{1,0:T(8,128)(2,1)} custom-call(bf16[640,256]{1,0:T(8,128)(2,1)} %get-tuple-element.21.pack_ref, bf16[128,2048]{1,0:T(8,128)(2,1)} %refs_0_.3, bf16[128,2048]{1,0:T(8,128)(2,1)} %copy-done.10), custom_call_target="tpu_custom_call" | custom-call | flops 671088640 | bytes 3670016 | tf_op jit(solution)/shard_map/pallas_call | solution.py:114
  150.5 1.6 all-to-all-done.4
  152.1 1.6 copy-done.1
  153.7 4.4 %all-to-all-start.1 = ((bf16[8,80,2048]{2,1,0:T(8,128)(2,1)}), bf16[8,80,2048]{2,1,0:T(8,128)(2,1)}, u32[]{:S(2)}, u32[]{:S(2)}) async-start(bf16[8,80,2048]{2,1,0:T(8,128)(2,1)} %bitcast.28), calls=%async_computation.1 | async-start | bytes 5242880 | tf_op jit(solution)/shard_map/all_to_all | solution.py:250
  158.1 16.5 %shard_map.94 = (bf16[8,2,40,1024]{3,2,1,0:T(8,128)(2,1)}, bf16[8,2,40,1024]{3,2,1,0:T(8,128)(2,1)}, f32[2,320,1]{2,1,0:T(8,128)}) custom-call(bf16[8,2,40,2048]{3,2,1,0:T(8,128)(2,1)} %bitcast.12.token_ref, bf16[8,2,40,2048]{3,2,1,0:T(8,128)(2,1)} %bitcast.30, bf16[2,2048,768]{2,1,0:T(8,128)(2,1)} %gate_ref.3, bf16[2,2048,768]{2,1,0:T(8,128)(2,1)} %up_ref.3, ...), custom_call_target="tpu_custom_call" | custom-call | flops 10066329600 | bytes 26738688 | tf_op jit(solution)/shard_map/pallas_call | solution.py:159
  174.6 15.8 %all-to-all-done.1 = bf16[8,80,2048]{2,1,0:T(8,128)(2,1)} async-done(((bf16[8,80,2048]{2,1,0:T(8,128)(2,1)}), bf16[8,80,2048]{2,1,0:T(8,128)(2,1)}, u32[]{:S(2)}, u32[]{:S(2)}) %all-to-all-start.1) | async-done | bytes 2621472 | tf_op jit(solution)/shard_map/all_to_all | solution.py:250
  190.3 3.8 %all-to-all-start.6 = ((bf16[8,80,1024]{2,1,0:T(8,128)(2,1)}), bf16[8,80,1024]{2,1,0:T(8,128)(2,1)S(1)}, u32[]{:S(2)}, u32[]{:S(2)}) async-start(bf16[8,80,1024]{2,1,0:T(8,128)(2,1)} %bitcast.35), calls=%async_computation.6 | async-start | bytes 2621440 | tf_op jit(solution)/shard_map/all_to_all | solution.py:250
  194.1 18.1 %shard_map.89 = (bf16[8,2,40,2048]{3,2,1,0:T(8,128)(2,1)}, f32[2,320,1]{2,1,0:T(8,128)}) custom-call(bf16[8,2,40,2048]{3,2,1,0:T(8,128)(2,1)} %bitcast.29, bf16[8,2,40,2048]{3,2,1,0:T(8,128)(2,1)} %bitcast.6.cotan_ref, bf16[2,2048,768]{2,1,0:T(8,128)(2,1)} %gate_ref.3, bf16[2,2048,768]{2,1,0:T(8,128)(2,1)} %up_ref.3, bf16[2,768,2048]{2,1,0:T(8,128)(2,1)} %down_ref.3), custom_call_target="tpu_custom_call" | custom-call | flops 10066329600 | bytes 26738688 | tf_op jit(solution)/shard_map/pallas_call | solution.py:159
  212.2 36.6 %all_to_all.44 = bf16[8,80,2048]{2,1,0:T(8,128)(2,1)} all-to-all(bf16[8,80,2048]{2,1,0:T(8,128)(2,1)} %bitcast.32), channel_id=1, replica_groups={{0,1,2,3,4,5,6,7},{8,9,10,11,12,13,14,15},{16,17,18,19,20,21,22,23},{24..., dimensions={0} | all-to-all | bytes 5242880 | tf_op jit(solution)/shard_map/all_to_all | solution.py:250
  248.8 3.6 %all-to-all-start.5 = ((bf16[8,80,1024]{2,1,0:T(8,128)(2,1)}), bf16[8,80,1024]{2,1,0:T(8,128)(2,1)S(1)}, u32[]{:S(2)}, u32[]{:S(2)}) async-start(bf16[8,80,1024]{2,1,0:T(8,128)(2,1)} %bitcast.15), calls=%async_computation.5 | async-start | bytes 2621440 | tf_op jit(solution)/shard_map/all_to_all | solution.py:250
  252.4 5.0 %shard_map.90 = (f32[128,2048]{1,0:T(8,128)}, bf16[128,2048]{1,0:T(8,128)(2,1)}) custom-call(bf16[256,640]{1,0:T(8,128)(2,1)} %get-tuple-element.19.high_ref, bf16[256,640]{1,0:T(8,128)(2,1)} %get-tuple-element.20.low_ref, bf16[640,2048]{1,0:T(8,128)(2,1)} %bitcast.31), custom_call_target="tpu_custom_call" | custom-call | flops 1342177280 | bytes 4718592 | tf_op jit(solution)/shard_map/pallas_call | solution.py:192
  257.4 12.5 %collective-permute-start.3 = (bf16[128,2048]{1,0:T(8,128)(2,1)}, bf16[128,2048]{1,0:T(8,128)(2,1)S(1)}, u32[]{:S(2)}, u32[]{:S(2)}) collective-permute-start(bf16[128,2048]{1,0:T(8,128)(2,1)} %get-tuple-element.24), channel_id=1, source_target_pairs={{0,24},{1,25},{2,26},{3,27},{4,28},{5,29},{6,30},{7,31},{8,0},{9,1... | collective-permute-start | bytes 1572872 | tf_op jit(solution)/shard_map/ppermute | solution.py:247
  269.9 3.3 shard_map.96
  273.8 1.1 copy-done.2
  274.9 3.1 shard_map.95
  278.0 6.7 %collective-permute-start.10 = (bf16[128,1024]{1,0:T(8,128)(2,1)}, bf16[128,1024]{1,0:T(8,128)(2,1)S(1)}, u32[]{:S(2)}, u32[]{:S(2)}) collective-permute-start(bf16[128,1024]{1,0:T(8,128)(2,1)} %get-tuple-element.29), channel_id=1, source_target_pairs={{0,16},{1,17},{2,18},{3,19},{4,20},{5,21},{6,22},{7,23},{8,24},{9,... | collective-permute-start | bytes 786440 | tf_op jit(solution)/shard_map/ppermute | solution.py:247
  284.7 3.1 collective-permute-start.11
  289.7 2.6 all-to-all-start.7
  293.0 25.3 %all-to-all-done.7 = f32[32,1,40]{2,1,0:T(1,128)S(1)} async-done(((f32[32,1,40]{2,1,0:T(1,128)}), f32[32,1,40]{2,1,0:T(1,128)S(1)}, u32[]{:S(2)}, u32[]{:S(2)}) %all-to-all-start.7) | async-done | bytes 5152 | tf_op jit(solution)/shard_map/all_to_all | solution.py:295
  320.2 3.1 shard_map.97
  323.3 1.5 copy.40
  324.8 1.3 convert_add_fusion.1
  326.1 1.1 pad_maximum_fusion
  (58 shorter events, 8.1 us)
Async XLA Ops:
  0.6 21.1 %collective-permute-start.1 = (bf16[128,2048]{1,0:T(8,128)(2,1)}, bf16[128,2048]{1,0:T(8,128)(2,1)S(1)}, u32[]{:S(2)}, u32[]{:S(2)}) collective-permute-start(bf16[128,2048]{1,0:T(8,128)(2,1)} %refs_0_.2), channel_id=1, source_target_pairs={{0,8},{1,9},{2,10},{3,11},{4,12},{5,13},{6,14},{7,15},{8,16},{9,17... | collective-permute-start | bytes 1572872 | tf_op jit(solution)/shard_map/ppermute | solution.py:247
  5.1 13.0 %collective-permute-start = (f32[128,16]{0,1:T(8,128)S(1)}, f32[128,16]{0,1:T(8,128)S(1)}, u32[]{:S(2)}, u32[]{:S(2)}) collective-permute-start(f32[128,16]{0,1:T(8,128)S(1)} %get-tuple-element.49), channel_id=1, source_target_pairs={{0,8},{1,9},{2,10},{3,11},{4,12},{5,13},{6,14},{7,15},{8,16},{9,17... | collective-permute-start | bytes 24584 | tf_op jit(solution)/shard_map/ppermute | solution.py:247
  21.7 0.8 copy-start.7
  27.3 3.9 %copy-start.5 = (bf16[128,2048]{1,0:T(8,128)(2,1)S(1)}, bf16[128,2048]{1,0:T(8,128)(2,1)}, u32[]{:S(2)}) copy-start(bf16[128,2048]{1,0:T(8,128)(2,1)} %refs_0_.2) | copy-start | bytes 1572868
  27.3 49.9 %all-to-all-start = ((bf16[8,80,2048]{2,1,0:T(8,128)(2,1)}), bf16[8,80,2048]{2,1,0:T(8,128)(2,1)S(1)}, u32[]{:S(2)}, u32[]{:S(2)}) async-start(bf16[8,80,2048]{2,1,0:T(8,128)(2,1)} %bitcast.25), calls=%async_computation | async-start | bytes 5242880 | tf_op jit(solution)/shard_map/all_to_all | solution.py:250
  31.2 41.1 %collective-permute-start.6 = (bf16[128,2048]{1,0:T(8,128)(2,1)S(1)}, bf16[128,2048]{1,0:T(8,128)(2,1)}, u32[]{:S(2)}, u32[]{:S(2)}) collective-permute-start(bf16[128,2048]{1,0:T(8,128)(2,1)S(1)} %copy-done.5), channel_id=1, source_target_pairs={{0,16},{1,17},{2,18},{3,19},{4,20},{5,21},{6,22},{7,23},{8,24},{9,... | collective-permute-start | bytes 1572872 | tf_op jit(solution)/shard_map/ppermute | solution.py:247
  32.0 40.3 %collective-permute-start.7 = (bf16[128,2048]{1,0:T(8,128)(2,1)S(1)}, bf16[128,2048]{1,0:T(8,128)(2,1)}, u32[]{:S(2)}, u32[]{:S(2)}) collective-permute-start(bf16[128,2048]{1,0:T(8,128)(2,1)S(1)} %copy-done.5), channel_id=1, source_target_pairs={{0,24},{1,25},{2,26},{3,27},{4,28},{5,29},{6,30},{7,31},{8,0},{9,1... | collective-permute-start | bytes 1572872 | tf_op jit(solution)/shard_map/ppermute | solution.py:247
  33.3 24.1 %collective-permute-start.5 = (f32[128,16]{0,1:T(8,128)S(1)}, f32[128,16]{0,1:T(8,128)S(1)}, u32[]{:S(2)}, u32[]{:S(2)}) collective-permute-start(f32[128,16]{0,1:T(8,128)S(1)} %get-tuple-element.49), channel_id=1, source_target_pairs={{0,24},{1,25},{2,26},{3,27},{4,28},{5,29},{6,30},{7,31},{8,0},{9,1... | collective-permute-start | bytes 24584 | tf_op jit(solution)/shard_map/ppermute | solution.py:247
  35.7 33.0 %collective-permute-start.4 = (f32[128,16]{0,1:T(8,128)S(1)}, f32[128,16]{0,1:T(8,128)S(1)}, u32[]{:S(2)}, u32[]{:S(2)}) collective-permute-start(f32[128,16]{0,1:T(8,128)S(1)} %get-tuple-element.49), channel_id=1, source_target_pairs={{0,16},{1,17},{2,18},{3,19},{4,20},{5,21},{6,22},{7,23},{8,24},{9,... | collective-permute-start | bytes 24584 | tf_op jit(solution)/shard_map/ppermute | solution.py:247
  77.2 1.5 copy-start
  77.2 5.9 %copy-start.6 = (bf16[128,2048]{1,0:T(8,128)(2,1)S(1)}, bf16[128,2048]{1,0:T(8,128)(2,1)}, u32[]{:S(2)}) copy-start(bf16[128,2048]{1,0:T(8,128)(2,1)} %refs_0_.3) | copy-start | bytes 1572868
  78.7 37.2 %all-to-all-start.3 = ((bf16[8,80,2048]{2,1,0:T(8,128)(2,1)}), bf16[8,80,2048]{2,1,0:T(8,128)(2,1)}, u32[]{:S(2)}, u32[]{:S(2)}) async-start(bf16[8,80,2048]{2,1,0:T(8,128)(2,1)} %bitcast.26), calls=%async_computation.3 | async-start | bytes 5242880 | tf_op jit(solution)/shard_map/all_to_all | solution.py:250
  83.1 26.3 %collective-permute-start.8 = (bf16[128,2048]{1,0:T(8,128)(2,1)S(1)}, bf16[128,2048]{1,0:T(8,128)(2,1)S(1)}, u32[]{:S(2)}, u32[]{:S(2)}) collective-permute-start(bf16[128,2048]{1,0:T(8,128)(2,1)S(1)} %copy-done.6), channel_id=1, source_target_pairs={{0,16},{1,17},{2,18},{3,19},{4,20},{5,21},{6,22},{7,23},{8,24},{9,... | collective-permute-start | bytes 1572872 | tf_op jit(solution)/shard_map/ppermute | solution.py:247
  83.2 26.3 %collective-permute-start.9 = (bf16[128,2048]{1,0:T(8,128)(2,1)S(1)}, bf16[128,2048]{1,0:T(8,128)(2,1)S(1)}, u32[]{:S(2)}, u32[]{:S(2)}) collective-permute-start(bf16[128,2048]{1,0:T(8,128)(2,1)S(1)} %copy-done.6), channel_id=1, source_target_pairs={{0,24},{1,25},{2,26},{3,27},{4,28},{5,29},{6,30},{7,31},{8,0},{9,1... | collective-permute-start | bytes 1572872 | tf_op jit(solution)/shard_map/ppermute | solution.py:247
  109.4 0.8 copy-start.8
  110.2 0.8 copy-start.9
  115.9 36.1 %all-to-all-start.4 = ((bf16[8,80,2048]{2,1,0:T(8,128)(2,1)}), bf16[8,80,2048]{2,1,0:T(8,128)(2,1)S(1)}, u32[]{:S(2)}, u32[]{:S(2)}) async-start(bf16[8,80,2048]{2,1,0:T(8,128)(2,1)} %bitcast.27), calls=%async_computation.4 | async-start | bytes 5242880 | tf_op jit(solution)/shard_map/all_to_all | solution.py:250
  119.8 25.0 %collective-permute-start.2 = (bf16[128,2048]{1,0:T(8,128)(2,1)S(1)}, bf16[128,2048]{1,0:T(8,128)(2,1)S(1)}, u32[]{:S(2)}, u32[]{:S(2)}) collective-permute-start(bf16[128,2048]{1,0:T(8,128)(2,1)S(1)} %copy-done.6), channel_id=1, source_target_pairs={{0,8},{1,9},{2,10},{3,11},{4,12},{5,13},{6,14},{7,15},{8,16},{9,17... | collective-permute-start | bytes 1572872 | tf_op jit(solution)/shard_map/ppermute | solution.py:247
  144.8 0.8 copy-start.10
  152.1 1.6 copy-start.1
  153.7 36.7 %all-to-all-start.1 = ((bf16[8,80,2048]{2,1,0:T(8,128)(2,1)}), bf16[8,80,2048]{2,1,0:T(8,128)(2,1)}, u32[]{:S(2)}, u32[]{:S(2)}) async-start(bf16[8,80,2048]{2,1,0:T(8,128)(2,1)} %bitcast.28), calls=%async_computation.1 | async-start | bytes 5242880 | tf_op jit(solution)/shard_map/all_to_all | solution.py:250
  190.3 21.9 %all-to-all-start.6 = ((bf16[8,80,1024]{2,1,0:T(8,128)(2,1)}), bf16[8,80,1024]{2,1,0:T(8,128)(2,1)S(1)}, u32[]{:S(2)}, u32[]{:S(2)}) async-start(bf16[8,80,1024]{2,1,0:T(8,128)(2,1)} %bitcast.35), calls=%async_computation.6 | async-start | bytes 2621440 | tf_op jit(solution)/shard_map/all_to_all | solution.py:250
  212.2 36.6 %copy-start.3 = (bf16[8,80,1024]{2,1,0:T(8,128)(2,1)}, bf16[8,80,1024]{2,1,0:T(8,128)(2,1)S(1)}, u32[]{:S(2)}) copy-start(bf16[8,80,1024]{2,1,0:T(8,128)(2,1)S(1)} %all-to-all-done.6) | copy-start | bytes 3932164
  248.8 24.9 %all-to-all-start.5 = ((bf16[8,80,1024]{2,1,0:T(8,128)(2,1)}), bf16[8,80,1024]{2,1,0:T(8,128)(2,1)S(1)}, u32[]{:S(2)}, u32[]{:S(2)}) async-start(bf16[8,80,1024]{2,1,0:T(8,128)(2,1)} %bitcast.15), calls=%async_computation.5 | async-start | bytes 2621440 | tf_op jit(solution)/shard_map/all_to_all | solution.py:250
  257.4 30.4 %copy-start.12 = (f32[2,320,1]{2,1,0:T(8,128)S(1)}, f32[2,320,1]{2,1,0:T(8,128)}, u32[]{:S(2)}) copy-start(f32[2,320,1]{2,1,0:T(8,128)} %get-tuple-element.34) | copy-start | bytes 7684
  257.4 67.4 %collective-permute-start.3 = (bf16[128,2048]{1,0:T(8,128)(2,1)}, bf16[128,2048]{1,0:T(8,128)(2,1)S(1)}, u32[]{:S(2)}, u32[]{:S(2)}) collective-permute-start(bf16[128,2048]{1,0:T(8,128)(2,1)} %get-tuple-element.24), channel_id=1, source_target_pairs={{0,24},{1,25},{2,26},{3,27},{4,28},{5,29},{6,30},{7,31},{8,0},{9,1... | collective-permute-start | bytes 1572872 | tf_op jit(solution)/shard_map/ppermute | solution.py:247
  269.9 18.2 %copy-start.11 = (f32[2,320,1]{2,1,0:T(8,128)S(1)}, f32[2,320,1]{2,1,0:T(8,128)}, u32[]{:S(2)}) copy-start(f32[2,320,1]{2,1,0:T(8,128)} %get-tuple-element.35) | copy-start | bytes 7684
  269.9 54.9 %copy-start.4 = (f32[128,2048]{1,0:T(8,128)S(1)}, f32[128,2048]{1,0:T(8,128)}, u32[]{:S(2)}) copy-start(f32[128,2048]{1,0:T(8,128)} %get-tuple-element.23) | copy-start | bytes 3145732
  273.2 51.6 %collective-permute-start.12 = (bf16[128,1024]{1,0:T(8,128)(2,1)}, bf16[128,1024]{1,0:T(8,128)(2,1)}, u32[]{:S(2)}, u32[]{:S(2)}) collective-permute-start(bf16[128,1024]{1,0:T(8,128)(2,1)} %get-tuple-element.32), channel_id=1, source_target_pairs={{0,16},{1,17},{2,18},{3,19},{4,20},{5,21},{6,22},{7,23},{8,24},{9,... | collective-permute-start | bytes 786440 | tf_op jit(solution)/shard_map/ppermute | solution.py:247
  273.2 51.6 %collective-permute-start.13 = (bf16[128,1024]{1,0:T(8,128)(2,1)}, bf16[128,1024]{1,0:T(8,128)(2,1)}, u32[]{:S(2)}, u32[]{:S(2)}) collective-permute-start(bf16[128,1024]{1,0:T(8,128)(2,1)} %get-tuple-element.33), channel_id=1, source_target_pairs={{0,8},{1,9},{2,10},{3,11},{4,12},{5,13},{6,14},{7,15},{8,16},{9,17... | collective-permute-start | bytes 786440 | tf_op jit(solution)/shard_map/ppermute | solution.py:247
  273.8 1.1 copy-start.2
  278.0 46.8 %collective-permute-start.10 = (bf16[128,1024]{1,0:T(8,128)(2,1)}, bf16[128,1024]{1,0:T(8,128)(2,1)S(1)}, u32[]{:S(2)}, u32[]{:S(2)}) collective-permute-start(bf16[128,1024]{1,0:T(8,128)(2,1)} %get-tuple-element.29), channel_id=1, source_target_pairs={{0,16},{1,17},{2,18},{3,19},{4,20},{5,21},{6,22},{7,23},{8,24},{9,... | collective-permute-start | bytes 786440 | tf_op jit(solution)/shard_map/ppermute | solution.py:247
  284.7 40.1 %collective-permute-start.11 = (bf16[128,1024]{1,0:T(8,128)(2,1)}, bf16[128,1024]{1,0:T(8,128)(2,1)S(1)}, u32[]{:S(2)}, u32[]{:S(2)}) collective-permute-start(bf16[128,1024]{1,0:T(8,128)(2,1)} %get-tuple-element.30), channel_id=1, source_target_pairs={{0,8},{1,9},{2,10},{3,11},{4,12},{5,13},{6,14},{7,15},{8,16},{9,17... | collective-permute-start | bytes 786440 | tf_op jit(solution)/shard_map/ppermute | solution.py:247
  289.7 28.6 %all-to-all-start.7 = ((f32[32,1,40]{2,1,0:T(1,128)}), f32[32,1,40]{2,1,0:T(1,128)S(1)}, u32[]{:S(2)}, u32[]{:S(2)}) async-start(f32[32,1,40]{2,1,0:T(1,128)} %bitcast.21), calls=%async_computation.7 | async-start | bytes 32768 | tf_op jit(solution)/shard_map/all_to_all | solution.py:295

commit v2 on v1

v2 whole, which is shorter than its diff:
```python
import functools
import math

import jax
import jax.numpy as jnp
from jax import lax
from jax.experimental import pallas as pl
from jax.experimental.pallas import tpu as pltpu
from jax.sharding import PartitionSpec as P

BF16 = jnp.bfloat16
F32 = jnp.float32
LANES = 128
VMEM_LIMIT = 56 * 1024 * 1024


def full(shape):
    return pl.BlockSpec(shape, lambda *_: (0,) * len(shape))


def call(kernel, out_shape, grid, in_specs, out_specs, flops, moved, waits=()):
    count = len(in_specs)

    def body(*refs):
        kernel(*refs[:count], *refs[count + len(waits) :])

    run = pl.pallas_call(
        body,
        out_shape=out_shape,
        grid=grid,
        in_specs=[*in_specs, *[pl.BlockSpec(memory_space=pl.ANY)] * len(waits)],
        out_specs=out_specs,
        cost_estimate=pl.CostEstimate(flops=flops, bytes_accessed=moved, transcendentals=0),
        compiler_params=pltpu.CompilerParams(vmem_limit_bytes=VMEM_LIMIT),
    )
    return lambda *args: run(*args, *waits)


def picks_of(ids, base, experts):
    tokens, top = ids.shape
    expert = lax.broadcasted_iota(jnp.int32, (tokens, experts), 1).astype(F32) + base
    hits = [ids[:, k : k + 1] == expert for k in range(top)]
    return hits, functools.reduce(jnp.logical_or, hits)


def earlier_picks(pick):
    tokens = pick.shape[0]
    row = lax.broadcasted_iota(jnp.int32, (tokens, tokens), 0)
    column = lax.broadcasted_iota(jnp.int32, (tokens, tokens), 1)
    below = jnp.where(column < row, 1.0, 0.0).astype(BF16)
    return jnp.dot(below, jnp.where(pick, 1.0, 0.0).astype(BF16), preferred_element_type=F32)


def plan_kernel(shared, top, capacity, place_ref, *refs):
    meta_refs, (pack_ref, high_ref, low_ref) = refs[:-3], refs[-3:]
    parts, tokens = len(meta_refs), meta_refs[0].shape[0]
    slots = pack_ref.shape[0]
    experts = slots // (parts * capacity)
    base = (place_ref[0, 0] * experts).astype(F32)
    slot = lax.broadcasted_iota(jnp.int32, (1, slots), 1)
    rank_of = (slot % capacity).astype(F32)
    part_of = (slot // capacity) % parts
    shared_of = (slot // (capacity * parts)) % shared
    chip_of = (slot // (capacity * parts * shared)) ^ place_ref[0, 1]
    expert = lax.broadcasted_iota(jnp.int32, (experts, slots), 0)
    spread = jnp.where(expert == chip_of * shared + shared_of, 1.0, 0.0).astype(BF16)
    for part, meta_ref in enumerate(meta_refs):
        meta = meta_ref[...].astype(F32)
        hits, pick = picks_of(meta[:, :top], base, experts)
        rank = jnp.where(pick, earlier_picks(pick), -1.0).astype(BF16)
        ranks = jnp.dot(rank, spread, preferred_element_type=F32)
        here = jnp.logical_and(ranks == rank_of, part_of == part)
        rows = slice(part * tokens, (part + 1) * tokens)
        for out, first in ((high_ref, top), (low_ref, 2 * top)):
            terms = [jnp.where(hits[k], meta[:, first + k : first + k + 1], 0.0) for k in range(top)]
            term = functools.reduce(jnp.add, terms).astype(BF16)
            spread_term = jnp.dot(term, spread, preferred_element_type=F32)
            out[rows, :] = jnp.where(here, spread_term, 0.0).astype(BF16)
        pack_ref[:, rows] = jnp.where(here, 1.0, 0.0).T.astype(BF16)


def plan(place, rows, width, top, shared, chips, capacity):
    parts, tokens = len(rows), rows[0].shape[0]
    slots = chips * shared * parts * capacity
    sources = parts * tokens
    outs = (
        jax.ShapeDtypeStruct((slots, sources), BF16),
        jax.ShapeDtypeStruct((sources, slots), BF16),
        jax.ShapeDtypeStruct((sources, slots), BF16),
    )
    return call(
        functools.partial(plan_kernel, shared, top, capacity),
        outs,
        (1,),
        [pl.BlockSpec(memory_space=pltpu.SMEM)]
        + [pl.BlockSpec((tokens, LANES), lambda i: (0, width // LANES))] * parts,
        [full((slots, sources)), full((sources, slots)), full((sources, slots))],
        8 * slots * sources,
        6 * slots * sources,
    )(place, *rows)


def pack_kernel(sources, pack_ref, *refs):
    tokens = refs[0].shape[0]
    total = None
    for part, ref in enumerate(refs[:sources]):
        term = jnp.dot(
            pack_ref[:, part * tokens : (part + 1) * tokens], ref[...], preferred_element_type=F32
        )
        total = term if total is None else total + term
    first = 0
    for out_ref in refs[sources:]:
        for e in range(out_ref.shape[0]):
            rows = out_ref.shape[1]
            out_ref[e] = total[first : first + rows].astype(out_ref.dtype)
            first += rows


def pack(matrix, rows, width, chips, shared, waits):
    slots, sources = matrix.shape
    tokens = rows[0].shape[0]
    block = math.gcd(width, 512)
    depth = slots // (chips * shared)
    return call(
        functools.partial(pack_kernel, len(rows)),
        [jax.ShapeDtypeStruct((shared, depth, width), rows[0].dtype)] * chips,
        (width // block,),
        [full((slots, sources))] + [pl.BlockSpec((tokens, block), lambda j: (0, j))] * len(rows),
        [pl.BlockSpec((shared, depth, block), lambda j: (0, 0, j))] * chips,
        2 * slots * sources * width,
        2 * (slots + sources) * width,
        waits,
    )(matrix, *rows)


def expert_body(pieces, token_refs, cotan_refs, gate_ref, up_ref, down_ref, outs, gate_out):
    rows, width = token_refs[0].shape

    def joined(refs):
        return jnp.concatenate([ref[...].astype(F32) for ref in refs], axis=0).astype(BF16)

    inputs, grads_in = joined(token_refs), joined(cotan_refs)
    gate_pre = jnp.dot(inputs, gate_ref[...], preferred_element_type=F32)
    up_pre = jnp.dot(inputs, up_ref[...], preferred_element_type=F32)
    across = (((1,), (1,)), ((), ()))
    upward = lax.dot_general(grads_in, down_ref[...], across, preferred_element_type=F32)
    sigma = 1.0 / (1.0 + jnp.exp(-gate_pre))
    silu_val = gate_pre * sigma
    gate_out[...] = jnp.sum(silu_val * up_pre * upward, axis=1, keepdims=True)
    gate_delta = (upward * up_pre * sigma * (1.0 + gate_pre * (1.0 - sigma))).astype(BF16)
    up_delta = (upward * silu_val).astype(BF16)
    step = width // pieces
    chips = len(token_refs)
    for j in range(pieces):
        columns = slice(j * step, (j + 1) * step)
        partial = lax.dot_general(gate_delta, gate_ref[columns, :], across, preferred_element_type=F32)
        partial += lax.dot_general(up_delta, up_ref[columns, :], across, preferred_element_type=F32)
        for chip in range(chips):
            outs[j * chips + chip][...] = partial[chip * rows : (chip + 1) * rows].astype(BF16)


def expert_kernel(chips, pieces, owned, *refs):
    token_refs, cotan_refs = refs[:chips], refs[chips : 2 * chips]
    outs = refs[-1 - pieces * chips : -1]
    weights = refs[2 * chips : -1 - pieces * chips]
    for number in range(len(weights) // 3):

        @pl.when(pl.program_id(0) // owned == number)
        def _(number=number):
            own = weights[3 * number : 3 * number + 3]
            expert_body(pieces, token_refs, cotan_refs, *own, outs, refs[-1])


def experts_of(token_rows, cotan_rows, weights, pieces, waits):
    chips = len(token_rows)
    shared, rows, width = token_rows[0].shape
    owned, _, hidden = weights[0][0].shape
    row_spec = pl.BlockSpec((None, rows, width), lambda e: (e, 0, 0))
    step = width // pieces
    outs = [jax.ShapeDtypeStruct((shared, rows, step), BF16)] * (pieces * chips)
    out_specs = [pl.BlockSpec((None, rows, step), lambda e: (e, 0, 0))] * (pieces * chips)
    outs.append(jax.ShapeDtypeStruct((shared, chips * rows, 1), F32))
    out_specs.append(pl.BlockSpec((None, chips * rows, 1), lambda e: (e, 0, 0)))
    weight_specs = []
    for number in range(len(weights)):

        def place(e, number=number):
            return (jnp.clip(e - number * owned, 0, owned - 1), 0, 0)

        weight_specs += [pl.BlockSpec((None, width, hidden), place)] * 2
        weight_specs.append(pl.BlockSpec((None, hidden, width), place))
    *partial, gate = call(
        functools.partial(expert_kernel, chips, pieces, owned),
        outs,
        (shared,),
        [row_spec] * (2 * chips) + weight_specs,
        out_specs,
        10 * shared * chips * rows * width * hidden,
        6 * shared * width * hidden + 6 * shared * chips * rows * width,
        waits,
    )(*token_rows, *cotan_rows, *[w for own in weights for w in own])
    return [partial[j * chips : (j + 1) * chips] for j in range(pieces)], gate


def combine_kernel(parts, chips, high_ref, low_ref, *refs):
    outs = refs[chips:]
    tokens = outs[0].shape[0]
    total = None
    for chip, ref in enumerate(refs[:chips]):
        rows = ref[...]
        slots = slice(chip * rows.shape[0], (chip + 1) * rows.shape[0])
        for matrix in (high_ref, low_ref):
            term = jnp.dot(matrix[:, slots], rows, preferred_element_type=F32)
            total = term if total is None else total + term
    for part in range(parts):
        outs[part][...] = total[part * tokens : (part + 1) * tokens].astype(outs[part].dtype)


def combine(high, low, returned, dtypes, waits):
    sources, slots = high.shape
    depth, width = returned[0].shape
    parts, chips = len(dtypes), len(returned)
    tokens = sources // parts
    block = math.gcd(width, 512)
    return call(
        functools.partial(combine_kernel, parts, chips),
        [jax.ShapeDtypeStruct((tokens, width), kind) for kind in dtypes],
        (width // block,),
        [full((sources, slots))] * 2 + [pl.BlockSpec((depth, block), lambda j: (0, j))] * chips,
        [pl.BlockSpec((tokens, block), lambda j: (0, j))] * parts,
        4 * slots * sources * width,
        2 * (slots + 2 * sources) * width,
        waits,
    )(high, low, *returned)


def gate_kernel(capacity, experts, ids_ref, gate_ref, out_ref):
    ids = ids_ref[...]
    top = ids.shape[1]
    hits, pick = picks_of(ids, 0.0, experts)
    before = earlier_picks(pick)
    slots = gate_ref.shape[1]
    slot = lax.broadcasted_iota(jnp.int32, (1, slots), 1).astype(F32)
    gate = gate_ref[...]
    for k in range(top):
        rank = jnp.sum(jnp.where(hits[k], before, 0.0), axis=1, keepdims=True)
        dest = ids[:, k : k + 1] * capacity + rank
        out_ref[:, k : k + 1] = jnp.sum(jnp.where(slot == dest, gate, 0.0), axis=1, keepdims=True)


def gates_home(ids, gate, capacity, experts):
    tokens, top = ids.shape
    return call(
        functools.partial(gate_kernel, capacity, experts),
        jax.ShapeDtypeStruct((tokens, top), F32),
        (),
        [pl.BlockSpec(memory_space=pltpu.VMEM)] * 2,
        pl.BlockSpec(memory_space=pltpu.VMEM),
        3 * tokens * top * gate.shape[1],
        4 * tokens * top,
    )(ids, gate)


def local(tokens, cotangent, routing, expert_ids, gate_weight, up_weight, down_weight):
    count_ep = lax.axis_size("ep")
    owned = gate_weight.shape[0]
    experts = owned * count_ep
    tok_rows, top_picks = expert_ids.shape
    width = tokens.shape[1]
    capacity = 5 * tok_rows * top_picks // (4 * experts)

    cores = math.gcd(count_ep, 2)
    chips = math.gcd(count_ep // cores, 4)
    layers = count_ep // (cores * chips)
    shared = cores * owned
    parts = min(layers, 8 // math.gcd(8, capacity))
    chunks = [list(range(first, first + parts)) for first in range(0, layers, parts)]
    tail_pieces = 2

    def permute(value, target):
        return lax.ppermute(value, "ep", [(i, target(i)) for i in range(count_ep)])

    def shift(value, by):
        return permute(value, lambda i: (i + by * chips * cores) % count_ep)

    def across(values):
        return [values[0]] + [permute(values[m], lambda i: i ^ (m * cores)) for m in range(1, chips)]

    me = lax.axis_index("ep")
    core, chip, layer = me % cores, me // cores % chips, me // (cores * chips)
    place = jnp.stack([layer, chip]).reshape(1, 2)
    ids = ((expert_ids // owned) ^ core) * owned + expert_ids % owned
    ids = ids.astype(F32)
    high = lax.reduce_precision(routing, exponent_bits=8, mantissa_bits=7)
    low = (routing - high).astype(BF16)
    spare = jnp.zeros((tok_rows, LANES - 3 * top_picks), BF16)
    tagged = jnp.concatenate([tokens, ids.astype(BF16), high.astype(BF16), low, spare], axis=1)
    weights = [(gate_weight, up_weight, down_weight)]
    if cores > 1:
        weights.append(tuple(permute(w, lambda i: i ^ 1) for w in weights[0]))

    received, waits = [], list(weights[-1])
    plans, at = [], [[tagged], [cotangent]]
    for chunk in chunks:
        for rows in at:
            for by in chunk:
                if by:
                    rows.append(shift(rows[-1], 1))
            parts_rows = [rows[by] for by in chunk]
            if rows is at[0]:
                plans.append(plan(place, parts_rows, width, top_picks, shared, chips, capacity))
            packed = pack(plans[-1][0], parts_rows, width, chips, shared, waits)
            received.append(across(packed))
            waits = [packed[0]] if len(received) == 1 else [packed[0], *received[-2][1:]]

    gates, partials = [], []
    for number in range(len(chunks)):
        pieces = tail_pieces if number == len(chunks) - 1 else 1
        waits = [packed[0]] if number < len(chunks) - 1 else []
        partial, gate = experts_of(received[2 * number], received[2 * number + 1], weights, pieces, waits)
        gates.append(gate.reshape(shared, chips, parts, capacity))
        partials.append(partial)

    gate_slots = jnp.concatenate(gates, axis=2).transpose(2, 1, 0, 3)
    order = lax.rem(layer - jnp.arange(layers, dtype=jnp.int32) + layers, layers)
    gate_slots = gate_slots[order][:, jnp.arange(chips, dtype=jnp.int32) ^ chip]
    gate_slots = gate_slots.reshape(layers * chips, shared * capacity)
    same_core = [[i * cores + c for i in range(layers * chips)] for c in range(cores)]
    gate_back = lax.all_to_all(gate_slots, "ep", 0, 0, tiled=True, axis_index_groups=same_core)
    gate_grad = gates_home(ids, gate_back.reshape(1, experts * capacity), capacity, experts)

    home, waits = {}, []
    for chunk, (_, high, low), pieces in zip(chunks, plans, partials):
        for blocks in pieces:
            step = blocks[0].shape[2]
            returned = [rows.reshape(-1, step) for rows in across(blocks)]
            kinds = [F32 if by == 0 else BF16 for by in chunk]
            sums = combine(high, low, returned, kinds, waits)
            waits = [sums[0], gate_back] if chunk is chunks[0] else [sums[0]]
            for by, rows in zip(chunk, sums):
                back = rows if by == 0 else shift(rows, -by)
                home.setdefault(by, []).append(back)

    columns = []
    step = width // tail_pieces
    for j in range(tail_pieces):
        total = None
        for by in range(layers):
            rows = home[by]
            value = rows[j] if len(rows) > 1 else rows[0][:, j * step : (j + 1) * step]
            value = value.astype(F32)
            total = value if total is None else total + value
        columns.append(total)
    input_grad = jnp.concatenate(columns, axis=1)
    if lax.axis_size("hid") > 1:
        input_grad = lax.psum_scatter(input_grad, "hid", scatter_dimension=1, tiled=True)
        gate_grad = lax.psum(gate_grad, "hid")
    return (input_grad, gate_grad)


def solution(mesh):
    placed = (
        P(("rep", "ep"), None),
        P(("rep", "ep"), None),
        P(("rep", "ep"), None),
        P(("rep", "ep"), None),
        P("ep", None, "hid"),
        P("ep", None, "hid"),
        P("ep", "hid", None),
    )
    return jax.shard_map(
        local,
        mesh=mesh,
        in_specs=placed,
        out_specs=(P(("rep", "ep"), "hid"), P(("rep", "ep"), None)),
        check_vma=False,
    )
```

time: 328 us -> 251 us (0.77)
  waiting for transfers between devices: 125 us -> 86.8 us
  starting transfers between devices: 72.2 us -> 42.5 us
  blocking collectives: 36.6 us -> 10.3 us
  Pallas kernels: 74.4 us -> 92 us
    all_to_all x7 -> x0, waiting for transfers between devices: 42.6 us -> none  [the longest x1 25.3 us: local(): gate_back = lax.all_to_all(gate_slots, 'ep', 0, 0, tiled=True)]
    all_to_all x7 -> x0, starting transfers between devices: 26.4 us -> none  [the longest x6 23.9 us: exchange(): lax.all_to_all(value, 'ep', 0, 0, tiled=True, axis_index_groups=in_layer)]
    all_to_all x1, blocking collectives: 36.6 us -> 10.3 us  [local(): lax.all_to_all(gate_slots, 'ep', 0, 0, tiled=True, axis_index_groups=same...]
    pallas_call x12, Pallas kernels: 74.4 us -> 92 us  [call(): return lambda *args: run(*args, *waits)]
    ppermute x14 -> x35, waiting for transfers between devices: 82 us -> 86.8 us  [permute(): return lax.ppermute(value, 'ep', [(i, target(i)) for i in range(count_ep)])]
    ppermute x14 -> x35, starting transfers between devices: 45.7 us -> 42.5 us  [permute(): return lax.ppermute(value, 'ep', [(i, target(i)) for i in range(count_ep)])]
    unnamed x27 -> x61, local copies, waits for them, and re-layouts: 8.81 us -> 7.87 us
  transfers between devices with their start and end apart: 21 -> 35, of which waited for: 9 -> 16; matrix products, arithmetic and copies ran while one was open for 2% -> 5% of each run, Pallas kernels for 21% -> 37%
where the time goes in v2:
time: 251 us
  Pallas kernels  92 us (37%)
  waiting for transfers between devices  86.8 us (35%)
  starting transfers between devices  42.5 us (17%)
  local copies, waits for them, and re-layouts  11.9 us (5%)
  blocking collectives  10.3 us (4%)
  other arithmetic  6.14 us (2%)
    pallas_call x12, Pallas kernels, call(): return lambda *args: run(*args, *waits)  92 us
    ppermute x35, waiting for transfers between devices, permute(): return lax.ppermute(value, 'ep', [(i, target(i)) for i in range(count_ep)])  86.8 us
    ppermute x35, starting transfers between devices, permute(): return lax.ppermute(value, 'ep', [(i, target(i)) for i in range(count_ep)])  42.5 us
    all_to_all x1, blocking collectives, local(): lax.all_to_all(gate_slots, 'ep', 0, 0, tiled=True, axis_index_groups=same...  10.3 us
    unnamed x61, local copies, waits for them, and re-layouts  7.87 us
  transfers between devices with their start and end apart: 35, of which 16 were waited for; matrix products, arithmetic and copies ran while one was open for 5% of the time, Pallas kernels for 37%

profile of v2, /device:TPU:0, one launch (start us, length us, event | category | flops | bytes accessed | tf_op | source)
XLA Modules:
  0.0 250.5 jit_solution(6354303456306616754)
XLA Ops:
  6.1 2.7 %collective-permute-start = (bf16[128,2176]{1,0:T(8,128)(2,1)S(1)}, bf16[128,2176]{1,0:T(8,128)(2,1)S(1)}, u32[]{:S(2)}, u32[]{:S(2)}) collective-permute-start(bf16[128,2176]{1,0:T(8,128)(2,1)S(1)} %concatenate.9.refs_1_), channel_id=1, source_target_pairs={{0,8},{1,9},{2,10},{3,11},{4,12},{5,13},{6,14},{7,15},{8,16},{9,17... | collective-permute-start | bytes 1671176 | tf_op jit(solution)/shard_map/ppermute | solution.py:281
  8.8 15.2 %collective-permute-done.refs_2_ = bf16[128,2176]{1,0:T(8,128)(2,1)S(1)} collective-permute-done((bf16[128,2176]{1,0:T(8,128)(2,1)S(1)}, bf16[128,2176]{1,0:T(8,128)(2,1)S(1)}, u32[]{:S(2)}, u32[]{:S(2)}) %collective-permute-start) | collective-permute-done | bytes 557088 | tf_op jit(solution)/shard_map/ppermute | solution.py:281
  24.0 1.3 collective-permute-start.7
  25.9 2.8 %shard_map.86 = (bf16[640,256]{1,0:T(8,128)(2,1)}, bf16[256,640]{1,0:T(8,128)(2,1)}, bf16[256,640]{1,0:T(8,128)(2,1)}) custom-call(s32[1,2]{1,0:T(1,128)} %add_bitcast_fusion.refs_0_, bf16[128,2176]{1,0:T(8,128)(2,1)} %copy-done, bf16[128,2176]{1,0:T(8,128)(2,1)} %copy-done.8), custom_call_target="tpu_custom_call" | custom-call | flops 1310720 | bytes 983040 | tf_op jit(solution)/shard_map/pallas_call | solution.py:36
  29.3 4.6 %shard_map.87 = (bf16[4,40,2048]{2,1,0:T(8,128)(2,1)}, bf16[4,40,2048]{2,1,0:T(8,128)(2,1)}, bf16[4,40,2048]{2,1,0:T(8,128)(2,1)}, bf16[4,40,2048]{2,1,0:T(8,128)(2,1)}) custom-call(bf16[640,256]{1,0:T(8,128)(2,1)} %get-tuple-element.46.refs_0_, bf16[128,2176]{1,0:T(8,128)(2,1)} %copy-done, bf16[128,2176]{1,0:T(8,128)(2,1)} %copy-done.8, ...), custom_call_target="tpu_custom_call" | custom-call | flops 671088640 | bytes 3670016 | tf_op jit(solution)/shard_map/pallas_call | solution.py:36
  33.8 2.9 %collective-permute-start.4 = (bf16[4,40,2048]{2,1,0:T(8,128)(2,1)}, bf16[4,40,2048]{2,1,0:T(8,128)(2,1)S(1)}, u32[]{:S(2)}, u32[]{:S(2)}) collective-permute-start(bf16[4,40,2048]{2,1,0:T(8,128)(2,1)} %get-tuple-element.48), channel_id=1, source_target_pairs={{0,2},{1,3},{2,0},{3,1},{4,6},{5,7},{6,4},{7,5},{8,10},{9,11},{10,... | collective-permute-start | bytes 1966088 | tf_op jit(solution)/shard_map/ppermute | solution.py:281
  36.7 1.5 collective-permute-start.5
  38.2 3.1 %collective-permute-done.11.refs_1_ = bf16[128,2176]{1,0:T(8,128)(2,1)S(1)} collective-permute-done((bf16[128,2176]{1,0:T(8,128)(2,1)S(1)}, bf16[128,2176]{1,0:T(8,128)(2,1)S(1)}, u32[]{:S(2)}, u32[]{:S(2)}) %collective-permute-start.11) | collective-permute-done | bytes 557088 | tf_op jit(solution)/shard_map/ppermute | solution.py:281
  41.3 11.2 %collective-permute-done.7.refs_2_ = bf16[128,2048]{1,0:T(8,128)(2,1)S(1)} collective-permute-done((bf16[128,2048]{1,0:T(8,128)(2,1)}, bf16[128,2048]{1,0:T(8,128)(2,1)S(1)}, u32[]{:S(2)}, u32[]{:S(2)}) %collective-permute-start.7) | collective-permute-done | bytes 524320 | tf_op jit(solution)/shard_map/ppermute | solution.py:281
  53.4 4.6 %shard_map.88 = (bf16[4,40,2048]{2,1,0:T(8,128)(2,1)}, bf16[4,40,2048]{2,1,0:T(8,128)(2,1)}, bf16[4,40,2048]{2,1,0:T(8,128)(2,1)}, bf16[4,40,2048]{2,1,0:T(8,128)(2,1)}) custom-call(bf16[640,256]{1,0:T(8,128)(2,1)} %get-tuple-element.46.refs_0_, bf16[128,2048]{1,0:T(8,128)(2,1)} %refs_1_.1, bf16[128,2048]{1,0:T(8,128)(2,1)} %copy-done.26, ...), custom_call_target="tpu_custom_call" | custom-call | flops 671088640 | bytes 3670016 | tf_op jit(solution)/shard_map/pallas_call | solution.py:36
  58.0 6.5 %collective-permute-done.12.refs_2_ = bf16[128,2176]{1,0:T(8,128)(2,1)S(1)} collective-permute-done((bf16[128,2176]{1,0:T(8,128)(2,1)S(1)}, bf16[128,2176]{1,0:T(8,128)(2,1)S(1)}, u32[]{:S(2)}, u32[]{:S(2)}) %collective-permute-start.12) | collective-permute-done | bytes 557088 | tf_op jit(solution)/shard_map/ppermute | solution.py:281
  64.5 1.5 collective-permute-start.8
  66.0 1.5 collective-permute-start.9
  68.7 2.7 %shard_map.89 = (bf16[640,256]{1,0:T(8,128)(2,1)}, bf16[256,640]{1,0:T(8,128)(2,1)}, bf16[256,640]{1,0:T(8,128)(2,1)}) custom-call(s32[1,2]{1,0:T(1,128)} %add_bitcast_fusion.refs_0_, bf16[128,2176]{1,0:T(8,128)(2,1)} %copy-done.9, bf16[128,2176]{1,0:T(8,128)(2,1)} %copy-done.10), custom_call_target="tpu_custom_call" | custom-call | flops 1310720 | bytes 983040 | tf_op jit(solution)/shard_map/pallas_call | solution.py:36
  72.3 4.7 %shard_map.90 = (bf16[4,40,2048]{2,1,0:T(8,128)(2,1)}, bf16[4,40,2048]{2,1,0:T(8,128)(2,1)}, bf16[4,40,2048]{2,1,0:T(8,128)(2,1)}, bf16[4,40,2048]{2,1,0:T(8,128)(2,1)}) custom-call(bf16[640,256]{1,0:T(8,128)(2,1)} %get-tuple-element.55.refs_0_, bf16[128,2176]{1,0:T(8,128)(2,1)} %copy-done.9, bf16[128,2176]{1,0:T(8,128)(2,1)} %copy-done.10, ...), custom_call_target="tpu_custom_call" | custom-call | flops 671088640 | bytes 3670016 | tf_op jit(solution)/shard_map/pallas_call | solution.py:36
  77.0 2.9 %collective-permute-start.19 = (bf16[4,40,2048]{2,1,0:T(8,128)(2,1)}, bf16[4,40,2048]{2,1,0:T(8,128)(2,1)S(1)}, u32[]{:S(2)}, u32[]{:S(2)}) collective-permute-start(bf16[4,40,2048]{2,1,0:T(8,128)(2,1)} %get-tuple-element.66), channel_id=1, source_target_pairs={{0,2},{1,3},{2,0},{3,1},{4,6},{5,7},{6,4},{7,5},{8,10},{9,11},{10,... | collective-permute-start | bytes 1966088 | tf_op jit(solution)/shard_map/ppermute | solution.py:281
  79.8 1.6 collective-permute-start.14
  81.4 11.2 %collective-permute-done.14.refs_2_ = bf16[128,2048]{1,0:T(8,128)(2,1)S(1)} collective-permute-done((bf16[128,2048]{1,0:T(8,128)(2,1)S(1)}, bf16[128,2048]{1,0:T(8,128)(2,1)S(1)}, u32[]{:S(2)}, u32[]{:S(2)}) %collective-permute-start.14) | collective-permute-done | bytes 524320 | tf_op jit(solution)/shard_map/ppermute | solution.py:281
  92.6 2.0 collective-permute-start.21
  94.6 1.2 collective-permute-done.9.refs_5_.refs_6_
  95.8 1.6 collective-permute-done.10.refs_6_.refs_7_
  98.3 4.6 %shard_map.91 = (bf16[4,40,2048]{2,1,0:T(8,128)(2,1)}, bf16[4,40,2048]{2,1,0:T(8,128)(2,1)}, bf16[4,40,2048]{2,1,0:T(8,128)(2,1)}, bf16[4,40,2048]{2,1,0:T(8,128)(2,1)}) custom-call(bf16[640,256]{1,0:T(8,128)(2,1)} %get-tuple-element.55.refs_0_, bf16[128,2048]{1,0:T(8,128)(2,1)} %copy-done.17, bf16[128,2048]{1,0:T(8,128)(2,1)} %copy-done.18, ...), custom_call_target="tpu_custom_call" | custom-call | flops 671088640 | bytes 3670016 | tf_op jit(solution)/shard_map/pallas_call | solution.py:36
  102.9 1.5 collective-permute-start.22
  104.9 5.7 %collective-permute-done.19.refs_1_ = bf16[4,40,2048]{2,1,0:T(8,128)(2,1)S(1)} collective-permute-done((bf16[4,40,2048]{2,1,0:T(8,128)(2,1)}, bf16[4,40,2048]{2,1,0:T(8,128)(2,1)S(1)}, u32[]{:S(2)}, u32[]{:S(2)}) %collective-permute-start.19) | collective-permute-done | bytes 655392 | tf_op jit(solution)/shard_map/ppermute | solution.py:281
  110.5 2.5 collective-permute-start.24
  113.0 26.4 %shard_map.92 = (bf16[4,40,2048]{2,1,0:T(8,128)(2,1)}, bf16[4,40,2048]{2,1,0:T(8,128)(2,1)}, bf16[4,40,2048]{2,1,0:T(8,128)(2,1)}, bf16[4,40,2048]{2,1,0:T(8,128)(2,1)}, f32[4,160,1]{2,1,0:T(8,128)}) custom-call(bf16[4,40,2048]{2,1,0:T(8,128)(2,1)} %get-tuple-element.47.refs_3_.refs_0_, bf16[4,40,2048]{2,1,0:T(8,128)(2,1)} %copy-done.2, ...), custom_call_target="tpu_custom_call" | custom-call | flops 10066329600 | bytes 45613056 | tf_op jit(solution)/shard_map/pallas_call | solution.py:36
  140.5 2.5 collective-permute-start.17
  143.0 9.0 %collective-permute-done.23.refs_6_ = bf16[4,40,2048]{2,1,0:T(8,128)(2,1)S(1)} collective-permute-done((bf16[4,40,2048]{2,1,0:T(8,128)(2,1)}, bf16[4,40,2048]{2,1,0:T(8,128)(2,1)S(1)}, u32[]{:S(2)}, u32[]{:S(2)}) %collective-permute-start.23) | collective-permute-done | bytes 655392 | tf_op jit(solution)/shard_map/ppermute | solution.py:281
  152.0 1.8 collective-permute-done.24.refs_7_
  154.6 25.8 %shard_map.94 = (bf16[4,40,1024]{2,1,0:T(8,128)(2,1)}, bf16[4,40,1024]{2,1,0:T(8,128)(2,1)}, bf16[4,40,1024]{2,1,0:T(8,128)(2,1)}, bf16[4,40,1024]{2,1,0:T(8,128...) custom-call(bf16[4,40,2048]{2,1,0:T(8,128)(2,1)} %get-tuple-element., ...), custom_call_target="tpu_custom_call" | custom-call | flops 10066329600 | bytes 45613056 | tf_op jit(solution)/shard_map/pallas_call | solution.py:36
  180.4 1.6 collective-permute-start.25
  182.6 1.6 collective-permute-start.27
  184.1 1.5 collective-permute-start.30
  186.1 5.2 %collective-permute-done.25 = bf16[4,40,1024]{2,1,0:T(8,128)(2,1)S(1)} collective-permute-done((bf16[4,40,1024]{2,1,0:T(8,128)(2,1)}, bf16[4,40,1024]{2,1,0:T(8,128)(2,1)S(1)}, u32[]{:S(2)}, u32[]{:S(2)}) %collective-permute-start.25) | collective-permute-done | bytes 327712 | tf_op jit(solution)/shard_map/ppermute | solution.py:281
  191.3 1.4 collective-permute-start.32
  192.8 5.6 %shard_map.93 = (f32[128,2048]{1,0:T(8,128)}, bf16[128,2048]{1,0:T(8,128)(2,1)}) custom-call(bf16[256,640]{1,0:T(8,128)(2,1)} %get-tuple-element.44.refs_0_, bf16[256,640]{1,0:T(8,128)(2,1)} %get-tuple-element.45.refs_1_, bf16[160,2048]{1,0:T(8,128)(2,1)} %bitcast.32, bf16[160,2048]{1,0:T(8,128)(2,1)} %bitcast.33, bf16[160,2048]{1,0:T(8,128)(2,1)} %bitcast.34, ...), custom_call_target="tpu_custom_call" | custom-call | flops 1342177280 | bytes 4718592 | tf_op jit(solution)/shard_map/pallas_call | solution.py:36
  198.4 1.5 collective-permute-done.26
  199.9 3.0 %collective-permute-start.18 = (bf16[128,2048]{1,0:T(8,128)(2,1)}, bf16[128,2048]{1,0:T(8,128)(2,1)S(1)}, u32[]{:S(2)}, u32[]{:S(2)}) collective-permute-start(bf16[128,2048]{1,0:T(8,128)(2,1)} %get-tuple-element.63), channel_id=1, source_target_pairs={{0,24},{1,25},{2,26},{3,27},{4,28},{5,29},{6,30},{7,31},{8,0},{9,1... | collective-permute-start | bytes 1572872 | tf_op jit(solution)/shard_map/ppermute | solution.py:281
  203.2 1.2 reduce.1
  205.8 10.3 %all_to_all.11 = f32[16,1,80]{2,1,0:T(1,128)} all-to-all(f32[16,1,80]{2,1,0:T(1,128)S(1)} %bitcast.31), channel_id=1, replica_groups={{0,2,4,6,8,10,12,14,16,18,20,22,24,26,28,30},{1,3,5,7,9,11,13,15,17,19,..., dimensions={0} | all-to-all | bytes 10240 | tf_op jit(solution)/shard_map/all_to_all | solution.py:329
  216.8 3.6 %shard_map.95 = (bf16[128,1024]{1,0:T(8,128)(2,1)}, bf16[128,1024]{1,0:T(8,128)(2,1)}) custom-call(bf16[256,640]{1,0:T(8,128)(2,1)} %get-tuple-element.64.refs_0_, bf16[256,640]{1,0:T(8,128)(2,1)} %get-tuple-element.65.refs_1_, bf16[160,1024]{1,0:T(8,128)(2,1)} %bitcast.25, bf16[160,1024]{1,0:T(8,128)(2,1)} %bitcast.26, bf16[160,1024]{1,0:T(8,128)(2,1)} %bitcast.27, ...), custom_call_target="tpu_custom_call" | custom-call | flops 671088640 | bytes 2359296 | tf_op jit(solution)/shard_map/pallas_call | solution.py:36
  222.4 3.6 %shard_map.96 = (bf16[128,1024]{1,0:T(8,128)(2,1)}, bf16[128,1024]{1,0:T(8,128)(2,1)}) custom-call(bf16[256,640]{1,0:T(8,128)(2,1)} %get-tuple-element.64.refs_0_, bf16[256,640]{1,0:T(8,128)(2,1)} %get-tuple-element.65.refs_1_, bf16[160,1024]{1,0:T(8,128)(2,1)} %bitcast.36, bf16[160,1024]{1,0:T(8,128)(2,1)} %bitcast.37, bf16[160,1024]{1,0:T(8,128)(2,1)} %bitcast.38, ...), custom_call_target="tpu_custom_call" | custom-call | flops 671088640 | bytes 2359296 | tf_op jit(solution)/shard_map/pallas_call | solution.py:36
  226.0 3.1 %collective-permute-start.34 = (bf16[128,1024]{1,0:T(8,128)(2,1)}, bf16[128,1024]{1,0:T(8,128)(2,1)S(1)}, u32[]{:S(2)}, u32[]{:S(2)}) collective-permute-start(bf16[128,1024]{1,0:T(8,128)(2,1)} %get-tuple-element.85), channel_id=1, source_target_pairs={{0,8},{1,9},{2,10},{3,11},{4,12},{5,13},{6,14},{7,15},{8,16},{9,17... | collective-permute-start | bytes 786440 | tf_op jit(solution)/shard_map/ppermute | solution.py:281
  229.8 1.4 reduce.5
  231.8 3.1 %shard_map.97 = f32[128,8]{1,0:T(8,128)} custom-call(f32[128,8]{1,0:T(8,128)} %get-tuple-element.97.refs_0_, f32[1,1280]{1,0:T(1,128)} %reshape.125.refs_1_), custom_call_target="tpu_custom_call" | custom-call | flops 3932160 | bytes 4096 | tf_op jit(solution)/shard_map/pallas_call | solution.py:36
  234.9 1.5 copy.58
  236.4 9.1 %collective-permute-done.28 = bf16[128,1024]{1,0:T(8,128)(2,1)S(1)} collective-permute-done((bf16[128,1024]{1,0:T(8,128)(2,1)}, bf16[128,1024]{1,0:T(8,128)(2,1)S(1)}, u32[]{:S(2)}, u32[]{:S(2)}) %collective-permute-start.28) | collective-permute-done | bytes 262176 | tf_op jit(solution)/shard_map/ppermute | solution.py:281
  245.5 3.6 %collective-permute-done.33 = bf16[128,1024]{1,0:T(8,128)(2,1)S(1)} collective-permute-done((bf16[128,1024]{1,0:T(8,128)(2,1)}, bf16[128,1024]{1,0:T(8,128)(2,1)S(1)}, u32[]{:S(2)}, u32[]{:S(2)}) %collective-permute-start.33) | collective-permute-done | bytes 262176 | tf_op jit(solution)/shard_map/ppermute | solution.py:281
  (124 shorter events, 20.9 us)
Async XLA Ops:
  0.6 28.1 %collective-permute-start.1 = (bf16[2,2048,768]{2,1,0:T(8,128)(2,1)}, bf16[2,2048,768]{2,1,0:T(8,128)(2,1)}, u32[]{:S(2)}, u32[]{:S(2)}) collective-permute-start(bf16[2,2048,768]{2,1,0:T(8,128)(2,1)} %refs_8_.3), channel_id=1, source_target_pairs={{0,1},{1,0},{2,3},{3,2},{4,5},{5,4},{6,7},{7,6},{8,9},{9,8},{10,11... | collective-permute-start | bytes 18874376 | tf_op jit(solution)/shard_map/ppermute | solution.py:281
  1.1 27.6 %collective-permute-start.2 = (bf16[2,2048,768]{2,1,0:T(8,128)(2,1)}, bf16[2,2048,768]{2,1,0:T(8,128)(2,1)}, u32[]{:S(2)}, u32[]{:S(2)}) collective-permute-start(bf16[2,2048,768]{2,1,0:T(8,128)(2,1)} %refs_9_.3), channel_id=1, source_target_pairs={{0,1},{1,0},{2,3},{3,2},{4,5},{5,4},{6,7},{7,6},{8,9},{9,8},{10,11... | collective-permute-start | bytes 18874376 | tf_op jit(solution)/shard_map/ppermute | solution.py:281
  1.2 28.0 %collective-permute-start.3 = (bf16[2,768,2048]{2,1,0:T(8,128)(2,1)}, bf16[2,768,2048]{2,1,0:T(8,128)(2,1)}, u32[]{:S(2)}, u32[]{:S(2)}) collective-permute-start(bf16[2,768,2048]{2,1,0:T(8,128)(2,1)} %refs_10_.3), channel_id=1, source_target_pairs={{0,1},{1,0},{2,3},{3,2},{4,5},{5,4},{6,7},{7,6},{8,9},{9,8},{10,11... | collective-permute-start | bytes 18874376 | tf_op jit(solution)/shard_map/ppermute | solution.py:281
  6.1 19.9 %copy-start = (bf16[128,2176]{1,0:T(8,128)(2,1)}, bf16[128,2176]{1,0:T(8,128)(2,1)S(1)}, u32[]{:S(2)}) copy-start(bf16[128,2176]{1,0:T(8,128)(2,1)S(1)} %concatenate.9.refs_1_) | copy-start | bytes 1671172
  6.1 17.9 %collective-permute-start = (bf16[128,2176]{1,0:T(8,128)(2,1)S(1)}, bf16[128,2176]{1,0:T(8,128)(2,1)S(1)}, u32[]{:S(2)}, u32[]{:S(2)}) collective-permute-start(bf16[128,2176]{1,0:T(8,128)(2,1)S(1)} %concatenate.9.refs_1_), channel_id=1, source_target_pairs={{0,8},{1,9},{2,10},{3,11},{4,12},{5,13},{6,14},{7,15},{8,16},{9,17... | collective-permute-start | bytes 1671176 | tf_op jit(solution)/shard_map/ppermute | solution.py:281
  24.0 17.3 %collective-permute-start.11 = (bf16[128,2176]{1,0:T(8,128)(2,1)S(1)}, bf16[128,2176]{1,0:T(8,128)(2,1)S(1)}, u32[]{:S(2)}, u32[]{:S(2)}) collective-permute-start(bf16[128,2176]{1,0:T(8,128)(2,1)S(1)} %collective-permute-done.refs_2_), channel_id=1, source_target_pairs={{0,8},{1,9},{2,10},{3,11},{4,12},{5,13},{6,14},{7,15},{8,16},{9,17... | collective-permute-start | bytes 1671176 | tf_op jit(solution)/shard_map/ppermute | solution.py:281
  24.0 28.5 %collective-permute-start.7 = (bf16[128,2048]{1,0:T(8,128)(2,1)}, bf16[128,2048]{1,0:T(8,128)(2,1)S(1)}, u32[]{:S(2)}, u32[]{:S(2)}) collective-permute-start(bf16[128,2048]{1,0:T(8,128)(2,1)} %refs_1_.1), channel_id=1, source_target_pairs={{0,8},{1,9},{2,10},{3,11},{4,12},{5,13},{6,14},{7,15},{8,16},{9,17... | collective-permute-start | bytes 1572872 | tf_op jit(solution)/shard_map/ppermute | solution.py:281
  33.8 32.2 %collective-permute-start.4 = (bf16[4,40,2048]{2,1,0:T(8,128)(2,1)}, bf16[4,40,2048]{2,1,0:T(8,128)(2,1)S(1)}, u32[]{:S(2)}, u32[]{:S(2)}) collective-permute-start(bf16[4,40,2048]{2,1,0:T(8,128)(2,1)} %get-tuple-element.48), channel_id=1, source_target_pairs={{0,2},{1,3},{2,0},{3,1},{4,6},{5,7},{6,4},{7,5},{8,10},{9,11},{10,... | collective-permute-start | bytes 1966088 | tf_op jit(solution)/shard_map/ppermute | solution.py:281
  36.7 31.0 %collective-permute-start.5 = (bf16[4,40,2048]{2,1,0:T(8,128)(2,1)}, bf16[4,40,2048]{2,1,0:T(8,128)(2,1)S(1)}, u32[]{:S(2)}, u32[]{:S(2)}) collective-permute-start(bf16[4,40,2048]{2,1,0:T(8,128)(2,1)} %get-tuple-element.49), channel_id=1, source_target_pairs={{0,4},{1,5},{2,6},{3,7},{4,0},{5,1},{6,2},{7,3},{8,12},{9,13},{10,... | collective-permute-start | bytes 1966088 | tf_op jit(solution)/shard_map/ppermute | solution.py:281
  38.2 33.2 %collective-permute-start.6 = (bf16[4,40,2048]{2,1,0:T(8,128)(2,1)}, bf16[4,40,2048]{2,1,0:T(8,128)(2,1)S(1)}, u32[]{:S(2)}, u32[]{:S(2)}) collective-permute-start(bf16[4,40,2048]{2,1,0:T(8,128)(2,1)} %get-tuple-element.50), channel_id=1, source_target_pairs={{0,6},{1,7},{2,4},{3,5},{4,2},{5,3},{6,0},{7,1},{8,14},{9,15},{10,... | collective-permute-start | bytes 1966088 | tf_op jit(solution)/shard_map/ppermute | solution.py:281
  41.3 27.3 %copy-start.9 = (bf16[128,2176]{1,0:T(8,128)(2,1)}, bf16[128,2176]{1,0:T(8,128)(2,1)S(1)}, u32[]{:S(2)}) copy-start(bf16[128,2176]{1,0:T(8,128)(2,1)S(1)} %collective-permute-done.11.refs_1_) | copy-start | bytes 1671172
  41.3 23.2 %collective-permute-start.12 = (bf16[128,2176]{1,0:T(8,128)(2,1)S(1)}, bf16[128,2176]{1,0:T(8,128)(2,1)S(1)}, u32[]{:S(2)}, u32[]{:S(2)}) collective-permute-start(bf16[128,2176]{1,0:T(8,128)(2,1)S(1)} %collective-permute-done.11.refs_1_), channel_id=1, source_target_pairs={{0,8},{1,9},{2,10},{3,11},{4,12},{5,13},{6,14},{7,15},{8,16},{9,17... | collective-permute-start | bytes 1671176 | tf_op jit(solution)/shard_map/ppermute | solution.py:281
  52.6 27.3 %collective-permute-start.13 = (bf16[128,2048]{1,0:T(8,128)(2,1)S(1)}, bf16[128,2048]{1,0:T(8,128)(2,1)S(1)}, u32[]{:S(2)}, u32[]{:S(2)}) collective-permute-start(bf16[128,2048]{1,0:T(8,128)(2,1)S(1)} %collective-permute-done.7.refs_2_), channel_id=1, source_target_pairs={{0,8},{1,9},{2,10},{3,11},{4,12},{5,13},{6,14},{7,15},{8,16},{9,17... | collective-permute-start | bytes 1572872 | tf_op jit(solution)/shard_map/ppermute | solution.py:281
  64.5 28.1 %collective-permute-start.8 = (bf16[4,40,2048]{2,1,0:T(8,128)(2,1)}, bf16[4,40,2048]{2,1,0:T(8,128)(2,1)S(1)}, u32[]{:S(2)}, u32[]{:S(2)}) collective-permute-start(bf16[4,40,2048]{2,1,0:T(8,128)(2,1)} %get-tuple-element.52), channel_id=1, source_target_pairs={{0,2},{1,3},{2,0},{3,1},{4,6},{5,7},{6,4},{7,5},{8,10},{9,11},{10,... | collective-permute-start | bytes 1966088 | tf_op jit(solution)/shard_map/ppermute | solution.py:281
  66.0 29.8 %collective-permute-start.9 = (bf16[4,40,2048]{2,1,0:T(8,128)(2,1)}, bf16[4,40,2048]{2,1,0:T(8,128)(2,1)S(1)}, u32[]{:S(2)}, u32[]{:S(2)}) collective-permute-start(bf16[4,40,2048]{2,1,0:T(8,128)(2,1)} %get-tuple-element.53), channel_id=1, source_target_pairs={{0,4},{1,5},{2,6},{3,7},{4,0},{5,1},{6,2},{7,3},{8,12},{9,13},{10,... | collective-permute-start | bytes 1966088 | tf_op jit(solution)/shard_map/ppermute | solution.py:281
  67.7 29.8 %collective-permute-start.10 = (bf16[4,40,2048]{2,1,0:T(8,128)(2,1)}, bf16[4,40,2048]{2,1,0:T(8,128)(2,1)S(1)}, u32[]{:S(2)}, u32[]{:S(2)}) collective-permute-start(bf16[4,40,2048]{2,1,0:T(8,128)(2,1)} %get-tuple-element.54), channel_id=1, source_target_pairs={{0,6},{1,7},{2,4},{3,5},{4,2},{5,3},{6,0},{7,1},{8,14},{9,15},{10,... | collective-permute-start | bytes 1966088 | tf_op jit(solution)/shard_map/ppermute | solution.py:281
  77.0 33.6 %collective-permute-start.19 = (bf16[4,40,2048]{2,1,0:T(8,128)(2,1)}, bf16[4,40,2048]{2,1,0:T(8,128)(2,1)S(1)}, u32[]{:S(2)}, u32[]{:S(2)}) collective-permute-start(bf16[4,40,2048]{2,1,0:T(8,128)(2,1)} %get-tuple-element.66), channel_id=1, source_target_pairs={{0,2},{1,3},{2,0},{3,1},{4,6},{5,7},{6,4},{7,5},{8,10},{9,11},{10,... | collective-permute-start | bytes 1966088 | tf_op jit(solution)/shard_map/ppermute | solution.py:281
  79.8 17.6 %copy-start.17 = (bf16[128,2048]{1,0:T(8,128)(2,1)}, bf16[128,2048]{1,0:T(8,128)(2,1)S(1)}, u32[]{:S(2)}) copy-start(bf16[128,2048]{1,0:T(8,128)(2,1)S(1)} %collective-permute-done.13.refs_1_) | copy-start | bytes 1572868
  79.8 12.8 %collective-permute-start.14 = (bf16[128,2048]{1,0:T(8,128)(2,1)S(1)}, bf16[128,2048]{1,0:T(8,128)(2,1)S(1)}, u32[]{:S(2)}, u32[]{:S(2)}) collective-permute-start(bf16[128,2048]{1,0:T(8,128)(2,1)S(1)} %collective-permute-done.13.refs_1_), channel_id=1, source_target_pairs={{0,8},{1,9},{2,10},{3,11},{4,12},{5,13},{6,14},{7,15},{8,16},{9,17... | collective-permute-start | bytes 1572872 | tf_op jit(solution)/shard_map/ppermute | solution.py:281
  92.6 46.8 %collective-permute-start.20 = (bf16[4,40,2048]{2,1,0:T(8,128)(2,1)}, bf16[4,40,2048]{2,1,0:T(8,128)(2,1)S(1)}, u32[]{:S(2)}, u32[]{:S(2)}) collective-permute-start(bf16[4,40,2048]{2,1,0:T(8,128)(2,1)} %get-tuple-element.67), channel_id=1, source_target_pairs={{0,4},{1,5},{2,6},{3,7},{4,0},{5,1},{6,2},{7,3},{8,12},{9,13},{10,... | collective-permute-start | bytes 1966088 | tf_op jit(solution)/shard_map/ppermute | solution.py:281
  92.6 47.4 %collective-permute-start.21 = (bf16[4,40,2048]{2,1,0:T(8,128)(2,1)}, bf16[4,40,2048]{2,1,0:T(8,128)(2,1)S(1)}, u32[]{:S(2)}, u32[]{:S(2)}) collective-permute-start(bf16[4,40,2048]{2,1,0:T(8,128)(2,1)} %get-tuple-element.68), channel_id=1, source_target_pairs={{0,6},{1,7},{2,4},{3,5},{4,2},{5,3},{6,0},{7,1},{8,14},{9,15},{10,... | collective-permute-start | bytes 1966088 | tf_op jit(solution)/shard_map/ppermute | solution.py:281
  102.9 37.6 %collective-permute-start.22 = (bf16[4,40,2048]{2,1,0:T(8,128)(2,1)}, bf16[4,40,2048]{2,1,0:T(8,128)(2,1)S(1)}, u32[]{:S(2)}, u32[]{:S(2)}) collective-permute-start(bf16[4,40,2048]{2,1,0:T(8,128)(2,1)} %get-tuple-element.69), channel_id=1, source_target_pairs={{0,2},{1,3},{2,0},{3,1},{4,6},{5,7},{6,4},{7,5},{8,10},{9,11},{10,... | collective-permute-start | bytes 1966088 | tf_op jit(solution)/shard_map/ppermute | solution.py:281
  104.3 47.6 %collective-permute-start.23 = (bf16[4,40,2048]{2,1,0:T(8,128)(2,1)}, bf16[4,40,2048]{2,1,0:T(8,128)(2,1)S(1)}, u32[]{:S(2)}, u32[]{:S(2)}) collective-permute-start(bf16[4,40,2048]{2,1,0:T(8,128)(2,1)} %get-tuple-element.70), channel_id=1, source_target_pairs={{0,4},{1,5},{2,6},{3,7},{4,0},{5,1},{6,2},{7,3},{8,12},{9,13},{10,... | collective-permute-start | bytes 1966088 | tf_op jit(solution)/shard_map/ppermute | solution.py:281
  110.5 28.8 %copy-start.11 = (bf16[4,40,2048]{2,1,0:T(8,128)(2,1)}, bf16[4,40,2048]{2,1,0:T(8,128)(2,1)S(1)}, u32[]{:S(2)}) copy-start(bf16[4,40,2048]{2,1,0:T(8,128)(2,1)S(1)} %collective-permute-done.19.refs_1_) | copy-start | bytes 1966084
  110.5 43.2 %collective-permute-start.24 = (bf16[4,40,2048]{2,1,0:T(8,128)(2,1)}, bf16[4,40,2048]{2,1,0:T(8,128)(2,1)S(1)}, u32[]{:S(2)}, u32[]{:S(2)}) collective-permute-start(bf16[4,40,2048]{2,1,0:T(8,128)(2,1)} %get-tuple-element.71), channel_id=1, source_target_pairs={{0,6},{1,7},{2,4},{3,5},{4,2},{5,3},{6,0},{7,1},{8,14},{9,15},{10,... | collective-permute-start | bytes 1966088 | tf_op jit(solution)/shard_map/ppermute | solution.py:281
  139.4 14.3 %copy-start.12 = (bf16[4,40,2048]{2,1,0:T(8,128)(2,1)}, bf16[4,40,2048]{2,1,0:T(8,128)(2,1)S(1)}, u32[]{:S(2)}) copy-start(bf16[4,40,2048]{2,1,0:T(8,128)(2,1)S(1)} %collective-permute-done.20.refs_2_) | copy-start | bytes 1966084
  139.4 43.1 %collective-permute-start.15 = (bf16[4,40,2048]{2,1,0:T(8,128)(2,1)}, bf16[4,40,2048]{2,1,0:T(8,128)(2,1)S(1)}, u32[]{:S(2)}, u32[]{:S(2)}) collective-permute-start(bf16[4,40,2048]{2,1,0:T(8,128)(2,1)} %get-tuple-element.59), channel_id=1, source_target_pairs={{0,2},{1,3},{2,0},{3,1},{4,6},{5,7},{6,4},{7,5},{8,10},{9,11},{10,... | collective-permute-start | bytes 1966088 | tf_op jit(solution)/shard_map/ppermute | solution.py:281
  140.0 13.7 %copy-start.13 = (bf16[4,40,2048]{2,1,0:T(8,128)(2,1)}, bf16[4,40,2048]{2,1,0:T(8,128)(2,1)S(1)}, u32[]{:S(2)}) copy-start(bf16[4,40,2048]{2,1,0:T(8,128)(2,1)S(1)} %collective-permute-done.21.refs_3_) | copy-start | bytes 1966084
  140.0 44.1 %collective-permute-start.16 = (bf16[4,40,2048]{2,1,0:T(8,128)(2,1)}, bf16[4,40,2048]{2,1,0:T(8,128)(2,1)S(1)}, u32[]{:S(2)}, u32[]{:S(2)}) collective-permute-start(bf16[4,40,2048]{2,1,0:T(8,128)(2,1)} %get-tuple-element.60), channel_id=1, source_target_pairs={{0,4},{1,5},{2,6},{3,7},{4,0},{5,1},{6,2},{7,3},{8,12},{9,13},{10,... | collective-permute-start | bytes 1966088 | tf_op jit(solution)/shard_map/ppermute | solution.py:281
  140.5 13.2 %copy-start.14 = (bf16[4,40,2048]{2,1,0:T(8,128)(2,1)}, bf16[4,40,2048]{2,1,0:T(8,128)(2,1)S(1)}, u32[]{:S(2)}) copy-start(bf16[4,40,2048]{2,1,0:T(8,128)(2,1)S(1)} %collective-permute-done.22.refs_5_) | copy-start | bytes 1966084
  140.5 62.4 %copy-start.22 = (f32[4,160,1]{2,1,0:T(8,128)S(1)}, f32[4,160,1]{2,1,0:T(8,128)}, u32[]{:S(2)}) copy-start(f32[4,160,1]{2,1,0:T(8,128)} %get-tuple-element.76) | copy-start | bytes 7684
  140.5 45.1 %collective-permute-start.17 = (bf16[4,40,2048]{2,1,0:T(8,128)(2,1)}, bf16[4,40,2048]{2,1,0:T(8,128)(2,1)S(1)}, u32[]{:S(2)}, u32[]{:S(2)}) collective-permute-start(bf16[4,40,2048]{2,1,0:T(8,128)(2,1)} %get-tuple-element.61), channel_id=1, source_target_pairs={{0,6},{1,7},{2,4},{3,5},{4,2},{5,3},{6,0},{7,1},{8,14},{9,15},{10,... | collective-permute-start | bytes 1966088 | tf_op jit(solution)/shard_map/ppermute | solution.py:281
  180.4 10.9 %collective-permute-start.25 = (bf16[4,40,1024]{2,1,0:T(8,128)(2,1)}, bf16[4,40,1024]{2,1,0:T(8,128)(2,1)S(1)}, u32[]{:S(2)}, u32[]{:S(2)}) collective-permute-start(bf16[4,40,1024]{2,1,0:T(8,128)(2,1)} %get-tuple-element.73), channel_id=1, source_target_pairs={{0,2},{1,3},{2,0},{3,1},{4,6},{5,7},{6,4},{7,5},{8,10},{9,11},{10,... | collective-permute-start | bytes 983048 | tf_op jit(solution)/shard_map/ppermute | solution.py:281
  182.0 18.0 %collective-permute-start.26 = (bf16[4,40,1024]{2,1,0:T(8,128)(2,1)}, bf16[4,40,1024]{2,1,0:T(8,128)(2,1)S(1)}, u32[]{:S(2)}, u32[]{:S(2)}) collective-permute-start(bf16[4,40,1024]{2,1,0:T(8,128)(2,1)} %get-tuple-element.74), channel_id=1, source_target_pairs={{0,4},{1,5},{2,6},{3,7},{4,0},{5,1},{6,2},{7,3},{8,12},{9,13},{10,... | collective-permute-start | bytes 983048 | tf_op jit(solution)/shard_map/ppermute | solution.py:281
  182.5 10.2 %copy-start.23 = (bf16[4,40,2048]{2,1,0:T(8,128)(2,1)}, bf16[4,40,2048]{2,1,0:T(8,128)(2,1)S(1)}, u32[]{:S(2)}) copy-start(bf16[4,40,2048]{2,1,0:T(8,128)(2,1)S(1)} %collective-permute-done.15) | copy-start | bytes 1966084
  182.6 33.5 %collective-permute-start.27 = (bf16[4,40,1024]{2,1,0:T(8,128)(2,1)}, bf16[4,40,1024]{2,1,0:T(8,128)(2,1)S(1)}, u32[]{:S(2)}, u32[]{:S(2)}) collective-permute-start(bf16[4,40,1024]{2,1,0:T(8,128)(2,1)} %get-tuple-element.75), channel_id=1, source_target_pairs={{0,6},{1,7},{2,4},{3,5},{4,2},{5,3},{6,0},{7,1},{8,14},{9,15},{10,... | collective-permute-start | bytes 983048 | tf_op jit(solution)/shard_map/ppermute | solution.py:281
  184.1 8.6 %copy-start.24 = (bf16[4,40,2048]{2,1,0:T(8,128)(2,1)}, bf16[4,40,2048]{2,1,0:T(8,128)(2,1)S(1)}, u32[]{:S(2)}) copy-start(bf16[4,40,2048]{2,1,0:T(8,128)(2,1)S(1)} %collective-permute-done.16) | copy-start | bytes 1966084
  184.1 36.9 %collective-permute-start.30 = (bf16[4,40,1024]{2,1,0:T(8,128)(2,1)}, bf16[4,40,1024]{2,1,0:T(8,128)(2,1)S(1)}, u32[]{:S(2)}, u32[]{:S(2)}) collective-permute-start(bf16[4,40,1024]{2,1,0:T(8,128)(2,1)} %get-tuple-element.81), channel_id=1, source_target_pairs={{0,2},{1,3},{2,0},{3,1},{4,6},{5,7},{6,4},{7,5},{8,10},{9,11},{10,... | collective-permute-start | bytes 983048 | tf_op jit(solution)/shard_map/ppermute | solution.py:281
  185.6 36.0 %collective-permute-start.31 = (bf16[4,40,1024]{2,1,0:T(8,128)(2,1)}, bf16[4,40,1024]{2,1,0:T(8,128)(2,1)S(1)}, u32[]{:S(2)}, u32[]{:S(2)}) collective-permute-start(bf16[4,40,1024]{2,1,0:T(8,128)(2,1)} %get-tuple-element.82), channel_id=1, source_target_pairs={{0,4},{1,5},{2,6},{3,7},{4,0},{5,1},{6,2},{7,3},{8,12},{9,13},{10,... | collective-permute-start | bytes 983048 | tf_op jit(solution)/shard_map/ppermute | solution.py:281
  191.3 24.8 %copy-start.19 = (bf16[4,40,1024]{2,1,0:T(8,128)(2,1)}, bf16[4,40,1024]{2,1,0:T(8,128)(2,1)S(1)}, u32[]{:S(2)}) copy-start(bf16[4,40,1024]{2,1,0:T(8,128)(2,1)S(1)} %collective-permute-done.25) | copy-start | bytes 983044
  191.3 30.3 %collective-permute-start.32 = (bf16[4,40,1024]{2,1,0:T(8,128)(2,1)}, bf16[4,40,1024]{2,1,0:T(8,128)(2,1)}, u32[]{:S(2)}, u32[]{:S(2)}) collective-permute-start(bf16[4,40,1024]{2,1,0:T(8,128)(2,1)} %get-tuple-element.83), channel_id=1, source_target_pairs={{0,6},{1,7},{2,4},{3,5},{4,2},{5,3},{6,0},{7,1},{8,14},{9,15},{10,... | collective-permute-start | bytes 983048 | tf_op jit(solution)/shard_map/ppermute | solution.py:281
  198.4 50.8 %copy-start.1 = (f32[128,2048]{1,0:T(8,128)S(1)}, f32[128,2048]{1,0:T(8,128)}, u32[]{:S(2)}) copy-start(f32[128,2048]{1,0:T(8,128)} %get-tuple-element.62.refs_6_) | copy-start | bytes 3145732
  199.9 16.2 %copy-start.20 = (bf16[4,40,1024]{2,1,0:T(8,128)(2,1)}, bf16[4,40,1024]{2,1,0:T(8,128)(2,1)S(1)}, u32[]{:S(2)}) copy-start(bf16[4,40,1024]{2,1,0:T(8,128)(2,1)S(1)} %collective-permute-done.26) | copy-start | bytes 983044
  199.9 36.5 %collective-permute-start.18 = (bf16[128,2048]{1,0:T(8,128)(2,1)}, bf16[128,2048]{1,0:T(8,128)(2,1)S(1)}, u32[]{:S(2)}, u32[]{:S(2)}) collective-permute-start(bf16[128,2048]{1,0:T(8,128)(2,1)} %get-tuple-element.63), channel_id=1, source_target_pairs={{0,24},{1,25},{2,26},{3,27},{4,28},{5,29},{6,30},{7,31},{8,0},{9,1... | collective-permute-start | bytes 1572872 | tf_op jit(solution)/shard_map/ppermute | solution.py:281
  220.4 16.0 %collective-permute-start.29 = (bf16[128,1024]{1,0:T(8,128)(2,1)}, bf16[128,1024]{1,0:T(8,128)(2,1)S(1)}, u32[]{:S(2)}, u32[]{:S(2)}) collective-permute-start(bf16[128,1024]{1,0:T(8,128)(2,1)} %get-tuple-element.79), channel_id=1, source_target_pairs={{0,8},{1,9},{2,10},{3,11},{4,12},{5,13},{6,14},{7,15},{8,16},{9,17... | collective-permute-start | bytes 786440 | tf_op jit(solution)/shard_map/ppermute | solution.py:281
  221.0 24.5 %collective-permute-start.28 = (bf16[128,1024]{1,0:T(8,128)(2,1)}, bf16[128,1024]{1,0:T(8,128)(2,1)S(1)}, u32[]{:S(2)}, u32[]{:S(2)}) collective-permute-start(bf16[128,1024]{1,0:T(8,128)(2,1)} %get-tuple-element.78.refs_6_), channel_id=1, source_target_pairs={{0,16},{1,17},{2,18},{3,19},{4,20},{5,21},{6,22},{7,23},{8,24},{9,... | collective-permute-start | bytes 786440 | tf_op jit(solution)/shard_map/ppermute | solution.py:281
  226.0 19.5 %collective-permute-start.34 = (bf16[128,1024]{1,0:T(8,128)(2,1)}, bf16[128,1024]{1,0:T(8,128)(2,1)S(1)}, u32[]{:S(2)}, u32[]{:S(2)}) collective-permute-start(bf16[128,1024]{1,0:T(8,128)(2,1)} %get-tuple-element.85), channel_id=1, source_target_pairs={{0,8},{1,9},{2,10},{3,11},{4,12},{5,13},{6,14},{7,15},{8,16},{9,17... | collective-permute-start | bytes 786440 | tf_op jit(solution)/shard_map/ppermute | solution.py:281
  229.1 20.0 %collective-permute-start.33 = (bf16[128,1024]{1,0:T(8,128)(2,1)}, bf16[128,1024]{1,0:T(8,128)(2,1)S(1)}, u32[]{:S(2)}, u32[]{:S(2)}) collective-permute-start(bf16[128,1024]{1,0:T(8,128)(2,1)} %get-tuple-element.84), channel_id=1, source_target_pairs={{0,16},{1,17},{2,18},{3,19},{4,20},{5,21},{6,22},{7,23},{8,24},{9,... | collective-permute-start | bytes 786440 | tf_op jit(solution)/shard_map/ppermute | solution.py:281
  (16 other events, 41.1 us)

commit v3 on v2

--- a/solution.py
+++ b/solution.py
@@ -10,15 +10,17 @@
 
 BF16 = jnp.bfloat16
 F32 = jnp.float32
+ACROSS = (((1,), (1,)), ((), ()))
 LANES = 128
-VMEM_LIMIT = 56 * 1024 * 1024
+SMALL_VMEM = 12 * 1024 * 1024
+VMEM_LIMIT = 40 * 1024 * 1024
 
 
 def full(shape):
     return pl.BlockSpec(shape, lambda *_: (0,) * len(shape))
 
 
-def call(kernel, out_shape, grid, in_specs, out_specs, flops, moved, waits=()):
+def call(kernel, out_shape, grid, in_specs, out_specs, flops, moved, waits=(), scratch=(), vmem=SMALL_VMEM):
     count = len(in_specs)
 
     def body(*refs):
@@ -31,9 +33,21 @@
         in_specs=[*in_specs, *[pl.BlockSpec(memory_space=pl.ANY)] * len(waits)],
         out_specs=out_specs,
         cost_estimate=pl.CostEstimate(flops=flops, bytes_accessed=moved, transcendentals=0),
-        compiler_params=pltpu.CompilerParams(vmem_limit_bytes=VMEM_LIMIT),
+        scratch_shapes=scratch,
+        compiler_params=pltpu.CompilerParams(vmem_limit_bytes=vmem),
     )
     return lambda *args: run(*args, *waits)
+
+
+def tie(value, waits):
+    anywhere = pl.BlockSpec(memory_space=pl.ANY)
+    return pl.pallas_call(
+        lambda *refs: None,
+        out_shape=jax.ShapeDtypeStruct(value.shape, value.dtype),
+        in_specs=[anywhere] * (1 + len(waits)),
+        out_specs=anywhere,
+        input_output_aliases={0: 0},
+    )(value, *waits)
 
 
 def picks_of(ids, base, experts):
@@ -133,71 +147,83 @@
     )(matrix, *rows)
 
 
-def expert_body(pieces, token_refs, cotan_refs, gate_ref, up_ref, down_ref, outs, gate_out):
-    rows, width = token_refs[0].shape
-
-    def joined(refs):
-        return jnp.concatenate([ref[...].astype(F32) for ref in refs], axis=0).astype(BF16)
+def joined(refs):
+    return jnp.concatenate([ref[...].astype(F32) for ref in refs], axis=0).astype(BF16)
+
+
+def expert_kernel(chips, pieces, owned, owners, *refs):
+    token_refs, cotan_refs = refs[:chips], refs[chips : 2 * chips]
+    sources = refs[2 * chips : 2 * chips + 3 * owners]
+    outs, gate_out = refs[2 * chips + 3 * owners : -5], refs[-5]
+    buffers, sems = refs[-4:-1], refs[-1]
+    step, steps = pl.program_id(0), pl.num_programs(0)
+    slot = lax.rem(step, 2)
+
+    def fetch(number, at, kind, into):
+        return pltpu.make_async_copy(sources[3 * number + kind].at[at], buffers[kind].at[into], sems.at[into, kind])
+
+    def start(expert, into):
+        for number in range(owners):
+
+            @pl.when(expert // owned == number)
+            def _(number=number):
+                for kind in range(3):
+                    fetch(number, lax.rem(expert, owned), kind, into).start()
+
+    @pl.when(step == 0)
+    def _():
+        start(step, slot)
+
+    @pl.when(step + 1 < steps)
+    def _():
+        start(step + 1, 1 - slot)
+
+    def weight(kind):
+        fetch(0, 0, kind, slot).wait()
+        return buffers[kind].at[slot]
 
     inputs, grads_in = joined(token_refs), joined(cotan_refs)
+    gate_ref = weight(0)
     gate_pre = jnp.dot(inputs, gate_ref[...], preferred_element_type=F32)
+    up_ref = weight(1)
     up_pre = jnp.dot(inputs, up_ref[...], preferred_element_type=F32)
-    across = (((1,), (1,)), ((), ()))
-    upward = lax.dot_general(grads_in, down_ref[...], across, preferred_element_type=F32)
+    down_ref = weight(2)
+    upward = lax.dot_general(grads_in, down_ref[...], ACROSS, preferred_element_type=F32)
     sigma = 1.0 / (1.0 + jnp.exp(-gate_pre))
     silu_val = gate_pre * sigma
     gate_out[...] = jnp.sum(silu_val * up_pre * upward, axis=1, keepdims=True)
     gate_delta = (upward * up_pre * sigma * (1.0 + gate_pre * (1.0 - sigma))).astype(BF16)
     up_delta = (upward * silu_val).astype(BF16)
-    step = width // pieces
-    chips = len(token_refs)
+    width, rows = inputs.shape[1] // pieces, inputs.shape[0] // chips
     for j in range(pieces):
-        columns = slice(j * step, (j + 1) * step)
-        partial = lax.dot_general(gate_delta, gate_ref[columns, :], across, preferred_element_type=F32)
-        partial += lax.dot_general(up_delta, up_ref[columns, :], across, preferred_element_type=F32)
+        columns = slice(j * width, (j + 1) * width)
+        partial = lax.dot_general(gate_delta, gate_ref[columns, :], ACROSS, preferred_element_type=F32)
+        partial += lax.dot_general(up_delta, up_ref[columns, :], ACROSS, preferred_element_type=F32)
         for chip in range(chips):
             outs[j * chips + chip][...] = partial[chip * rows : (chip + 1) * rows].astype(BF16)
-
-
-def expert_kernel(chips, pieces, owned, *refs):
-    token_refs, cotan_refs = refs[:chips], refs[chips : 2 * chips]
-    outs = refs[-1 - pieces * chips : -1]
-    weights = refs[2 * chips : -1 - pieces * chips]
-    for number in range(len(weights) // 3):
-
-        @pl.when(pl.program_id(0) // owned == number)
-        def _(number=number):
-            own = weights[3 * number : 3 * number + 3]
-            expert_body(pieces, token_refs, cotan_refs, *own, outs, refs[-1])
 
 
 def experts_of(token_rows, cotan_rows, weights, pieces, waits):
     chips = len(token_rows)
     shared, rows, width = token_rows[0].shape
     owned, _, hidden = weights[0][0].shape
+    all_rows, step = chips * rows, width // pieces
     row_spec = pl.BlockSpec((None, rows, width), lambda e: (e, 0, 0))
-    step = width // pieces
     outs = [jax.ShapeDtypeStruct((shared, rows, step), BF16)] * (pieces * chips)
     out_specs = [pl.BlockSpec((None, rows, step), lambda e: (e, 0, 0))] * (pieces * chips)
-    outs.append(jax.ShapeDtypeStruct((shared, chips * rows, 1), F32))
-    out_specs.append(pl.BlockSpec((None, chips * rows, 1), lambda e: (e, 0, 0)))
-    weight_specs = []
-    for number in range(len(weights)):
-
-        def place(e, number=number):
-            return (jnp.clip(e - number * owned, 0, owned - 1), 0, 0)
-
-        weight_specs += [pl.BlockSpec((None, width, hidden), place)] * 2
-        weight_specs.append(pl.BlockSpec((None, hidden, width), place))
+    outs.append(jax.ShapeDtypeStruct((shared, all_rows, 1), F32))
+    out_specs.append(pl.BlockSpec((None, all_rows, 1), lambda e: (e, 0, 0)))
     *partial, gate = call(
-        functools.partial(expert_kernel, chips, pieces, owned),
+        functools.partial(expert_kernel, chips, pieces, owned, len(weights)),
         outs,
         (shared,),
-        [row_spec] * (2 * chips) + weight_specs,
+        [row_spec] * (2 * chips) + [pl.BlockSpec(memory_space=pl.ANY)] * (3 * len(weights)),
         out_specs,
-        10 * shared * chips * rows * width * hidden,
-        6 * shared * width * hidden + 6 * shared * chips * rows * width,
+        10 * shared * all_rows * width * hidden,
+        6 * shared * width * hidden + 6 * shared * all_rows * width,
         waits,
+        [pltpu.VMEM((2, *w.shape[1:]), BF16) for w in weights[0]] + [pltpu.SemaphoreType.DMA((2, 3))],
+        VMEM_LIMIT,
     )(*token_rows, *cotan_rows, *[w for own in weights for w in own])
     return [partial[j * chips : (j + 1) * chips] for j in range(pieces)], gate
 
@@ -333,13 +359,21 @@
     for chunk, (_, high, low), pieces in zip(chunks, plans, partials):
         for blocks in pieces:
             step = blocks[0].shape[2]
+            if chunk is not chunks[0] and blocks is pieces[1]:
+                blocks = [blocks[0]] + [tie(rows, first_sums[:1]) for rows in blocks[1:]]
             returned = [rows.reshape(-1, step) for rows in across(blocks)]
             kinds = [F32 if by == 0 else BF16 for by in chunk]
             sums = combine(high, low, returned, kinds, waits)
-            waits = [sums[0], gate_back] if chunk is chunks[0] else [sums[0]]
+            waits = [sums[0]]
+            if chunk is chunks[0]:
+                first_sums = sums
+            elif blocks is pieces[0]:
+                waits.append(gate_back)
             for by, rows in zip(chunk, sums):
                 back = rows if by == 0 else shift(rows, -by)
                 home.setdefault(by, []).append(back)
+                if chunk is chunks[0] and by:
+                    waits.append(back)
 
     columns = []
     step = width // tail_pieces

time: 251 us -> 240 us (0.956)
  waiting for transfers between devices: 86.8 us -> 110 us
  Pallas kernels: 92 us -> 70.8 us
  blocking collectives: 10.3 us -> 0 us
    pallas_call x12, Pallas kernels: 92 us -> 70.8 us  [call(): return lambda *args: run(*args, *waits)]
    ppermute x35, waiting for transfers between devices: 86.8 us -> 106 us  [permute(): return lax.ppermute(value, 'ep', [(i, target(i)) for i in range(count_ep)])]
    all_to_all x1 -> x0, blocking collectives: 10.3 us -> none  [local(): lax.all_to_all(gate_slots, 'ep', 0, 0, tiled=True, axis_index_groups=same...]
    ppermute x35, starting transfers between devices: 42.5 us -> 38.3 us  [permute(): return lax.ppermute(value, 'ep', [(i, target(i)) for i in range(count_ep)])]
    all_to_all x0 -> x1, starting transfers between devices: none -> 4.06 us  [local(): lax.all_to_all(gate_slots, 'ep', 0, 0, tiled=True, axis_index_groups=same...]
    all_to_all x0 -> x1, waiting for transfers between devices: none -> 3.34 us  [local(): lax.all_to_all(gate_slots, 'ep', 0, 0, tiled=True, axis_index_groups=same...]
    unnamed x61 -> x35, local copies, waits for them, and re-layouts: 7.87 us -> 5.66 us
  transfers between devices with their start and end apart: 35 -> 36, of which waited for: 16 -> 16; matrix products, arithmetic and copies ran while one was open for 5% -> 4% of each run, Pallas kernels for 37% -> 30%
where the time goes in v3:
time: 240 us
  waiting for transfers between devices  110 us (46%)
  Pallas kernels  70.8 us (30%)
  starting transfers between devices  42.3 us (18%)
  local copies, waits for them, and re-layouts  9.71 us (4%)
  other arithmetic  5.9 us (2%)
    ppermute x35, waiting for transfers between devices, permute(): return lax.ppermute(value, 'ep', [(i, target(i)) for i in range(count_ep)])  106 us
    pallas_call x12, Pallas kernels, call(): return lambda *args: run(*args, *waits)  70.8 us
    ppermute x35, starting transfers between devices, permute(): return lax.ppermute(value, 'ep', [(i, target(i)) for i in range(count_ep)])  38.3 us
    unnamed x35, local copies, waits for them, and re-layouts  5.66 us
  transfers between devices with their start and end apart: 36, of which 16 were waited for; matrix products, arithmetic and copies ran while one was open for 4% of the time, Pallas kernels for 30%

profile of v3, /device:TPU:0, one launch (start us, length us, event | category | flops | bytes accessed | tf_op | source)
XLA Modules:
  0.0 239.5 jit_solution(4761285530050746506)
XLA Ops:
  4.9 1.2 concatenate.9.refs_1_
  6.1 2.7 %collective-permute-start = (bf16[128,2176]{1,0:T(8,128)(2,1)S(1)}, bf16[128,2176]{1,0:T(8,128)(2,1)S(1)}, u32[]{:S(2)}, u32[]{:S(2)}) collective-permute-start(bf16[128,2176]{1,0:T(8,128)(2,1)S(1)} %concatenate.9.refs_1_), channel_id=1, source_target_pairs={{0,8},{1,9},{2,10},{3,11},{4,12},{5,13},{6,14},{7,15},{8,16},{9,17... | collective-permute-start | bytes 1671176 | tf_op jit(solution)/shard_map/ppermute | solution.py:307
  8.8 15.2 %collective-permute-done.refs_2_ = bf16[128,2176]{1,0:T(8,128)(2,1)S(1)} collective-permute-done((bf16[128,2176]{1,0:T(8,128)(2,1)S(1)}, bf16[128,2176]{1,0:T(8,128)(2,1)S(1)}, u32[]{:S(2)}, u32[]{:S(2)}) %collective-permute-start) | collective-permute-done | bytes 557088 | tf_op jit(solution)/shard_map/ppermute | solution.py:307
  24.0 1.3 collective-permute-start.7
  25.4 1.6 shard_map.86
  29.3 2.4 %shard_map.87 = (bf16[4,40,2048]{2,1,0:T(8,128)(2,1)S(1)}, bf16[4,40,2048]{2,1,0:T(8,128)(2,1)S(1)}, bf16[4,40,2048]{2,1,0:T(8,128)(2,1)S(1)}, bf16[4,40,2048]{2,1,0:T(8,128)(2,1)S(1)}) custom-call(bf16[640,256]{1,0:T(8,128)(2,1)S(1)} %get-tuple-element.46.refs_0_, bf16[128,2176]{1,0:T(8,128)(2,1)S(1)} %concatenate.9.refs_1_, ...), custom_call_target="tpu_custom_call" | custom-call | flops 671088640 | bytes 3670016 | tf_op jit(solution)/shard_map/pallas_call | solution.py:39
  31.7 2.9 %collective-permute-start.4 = (bf16[4,40,2048]{2,1,0:T(8,128)(2,1)S(1)}, bf16[4,40,2048]{2,1,0:T(8,128)(2,1)S(1)}, u32[]{:S(2)}, u32[]{:S(2)}) collective-permute-start(bf16[4,40,2048]{2,1,0:T(8,128)(2,1)S(1)} %get-tuple-element.48), channel_id=1, source_target_pairs={{0,2},{1,3},{2,0},{3,1},{4,6},{5,7},{6,4},{7,5},{8,10},{9,11},{10,... | collective-permute-start | bytes 1966088 | tf_op jit(solution)/shard_map/ppermute | solution.py:307
  34.6 1.5 collective-permute-start.5
  36.2 5.1 %collective-permute-done.11.refs_1_ = bf16[128,2176]{1,0:T(8,128)(2,1)S(1)} collective-permute-done((bf16[128,2176]{1,0:T(8,128)(2,1)S(1)}, bf16[128,2176]{1,0:T(8,128)(2,1)S(1)}, u32[]{:S(2)}, u32[]{:S(2)}) %collective-permute-start.11) | collective-permute-done | bytes 557088 | tf_op jit(solution)/shard_map/ppermute | solution.py:307
  41.3 11.3 %collective-permute-done.7.refs_2_ = bf16[128,2048]{1,0:T(8,128)(2,1)} collective-permute-done((bf16[128,2048]{1,0:T(8,128)(2,1)}, bf16[128,2048]{1,0:T(8,128)(2,1)}, u32[]{:S(2)}, u32[]{:S(2)}) %collective-permute-start.7) | collective-permute-done | bytes 524320 | tf_op jit(solution)/shard_map/ppermute | solution.py:307
  52.7 3.5 %shard_map.88 = (bf16[4,40,2048]{2,1,0:T(8,128)(2,1)S(1)}, bf16[4,40,2048]{2,1,0:T(8,128)(2,1)S(1)}, bf16[4,40,2048]{2,1,0:T(8,128)(2,1)S(1)}, bf16[4,40,2048]{2,1,0:T(8,128)(2,1)S(1)}) custom-call(bf16[640,256]{1,0:T(8,128)(2,1)S(1)} %get-tuple-element.46.refs_0_, bf16[128,2048]{1,0:T(8,128)(2,1)S(1)} %copy-done.7, ...), custom_call_target="tpu_custom_call" | custom-call | flops 671088640 | bytes 3670016 | tf_op jit(solution)/shard_map/pallas_call | solution.py:39
  56.2 8.3 %collective-permute-done.12.refs_2_ = bf16[128,2176]{1,0:T(8,128)(2,1)S(1)} collective-permute-done((bf16[128,2176]{1,0:T(8,128)(2,1)S(1)}, bf16[128,2176]{1,0:T(8,128)(2,1)S(1)}, u32[]{:S(2)}, u32[]{:S(2)}) %collective-permute-start.12) | collective-permute-done | bytes 557088 | tf_op jit(solution)/shard_map/ppermute | solution.py:307
  64.5 1.5 collective-permute-start.8
  66.0 1.5 collective-permute-start.9
  68.0 1.6 shard_map.89
  69.6 2.5 %shard_map.90 = (bf16[4,40,2048]{2,1,0:T(8,128)(2,1)S(1)}, bf16[4,40,2048]{2,1,0:T(8,128)(2,1)S(1)}, bf16[4,40,2048]{2,1,0:T(8,128)(2,1)S(1)}, bf16[4,40,2048]{2,1,0:T(8,128)(2,1)S(1)}) custom-call(bf16[640,256]{1,0:T(8,128)(2,1)S(1)} %get-tuple-element.55.refs_0_, bf16[128,2176]{1,0:T(8,128)(2,1)S(1)} %collective-permute-done.11.refs_1_, ...), custom_call_target="tpu_custom_call" | custom-call | flops 671088640 | bytes 3670016 | tf_op jit(solution)/shard_map/pallas_call | solution.py:39
  72.1 1.6 collective-permute-start.19
  75.0 14.2 %collective-permute-done.14.refs_2_ = bf16[128,2048]{1,0:T(8,128)(2,1)S(1)} collective-permute-done((bf16[128,2048]{1,0:T(8,128)(2,1)S(1)}, bf16[128,2048]{1,0:T(8,128)(2,1)S(1)}, u32[]{:S(2)}, u32[]{:S(2)}) %collective-permute-start.14) | collective-permute-done | bytes 524320 | tf_op jit(solution)/shard_map/ppermute | solution.py:307
  89.2 1.2 collective-permute-start.20
  90.4 1.4 collective-permute-start.21
  91.9 5.4 %collective-permute-done.10.refs_6_.refs_7_ = bf16[4,40,2048]{2,1,0:T(8,128)(2,1)S(1)} collective-permute-done((bf16[4,40,2048]{2,1,0:T(8,128)(2,1)S(1)}, bf16[4,40,2048]{2,1,0:T(8,128)(2,1)S(1)}, u32[]{:S(2)}, u32[]{:S(2)}) %collective-permute-start.10) | collective-permute-done | bytes 655392 | tf_op jit(solution)/shard_map/ppermute | solution.py:307
  97.2 2.9 %shard_map.91 = (bf16[4,40,2048]{2,1,0:T(8,128)(2,1)S(1)}, bf16[4,40,2048]{2,1,0:T(8,128)(2,1)}, bf16[4,40,2048]{2,1,0:T(8,128)(2,1)S(1)}, bf16[4,40,2048]{2,1,0:T(8,128)(2,1)S(1)}) custom-call(bf16[640,256]{1,0:T(8,128)(2,1)S(1)} %get-tuple-element.55.refs_0_, bf16[128,2048]{1,0:T(8,128)(2,1)S(1)} %collective-permute-done.13.refs_1_, ...), custom_call_target="tpu_custom_call" | custom-call | flops 671088640 | bytes 3670016 | tf_op jit(solution)/shard_map/pallas_call | solution.py:39
  100.2 1.4 collective-permute-start.22
  102.1 8.2 %collective-permute-done.19.refs_1_ = bf16[4,40,2048]{2,1,0:T(8,128)(2,1)S(1)} collective-permute-done((bf16[4,40,2048]{2,1,0:T(8,128)(2,1)S(1)}, bf16[4,40,2048]{2,1,0:T(8,128)(2,1)S(1)}, u32[]{:S(2)}, u32[]{:S(2)}) %collective-permute-start.19) | collective-permute-done | bytes 655392 | tf_op jit(solution)/shard_map/ppermute | solution.py:307
  110.3 2.4 %collective-permute-start.24 = (bf16[4,40,2048]{2,1,0:T(8,128)(2,1)S(1)}, bf16[4,40,2048]{2,1,0:T(8,128)(2,1)S(1)}, u32[]{:S(2)}, u32[]{:S(2)}) collective-permute-start(bf16[4,40,2048]{2,1,0:T(8,128)(2,1)S(1)} %get-tuple-element.71), channel_id=1, source_target_pairs={{0,6},{1,7},{2,4},{3,5},{4,2},{5,3},{6,0},{7,1},{8,14},{9,15},{10,... | collective-permute-start | bytes 1966088 | tf_op jit(solution)/shard_map/ppermute | solution.py:307
  112.7 23.2 %shard_map.92 = (bf16[4,40,2048]{2,1,0:T(8,128)(2,1)S(1)}, bf16[4,40,2048]{2,1,0:T(8,128)(2,1)S(1)}, bf16[4,40,2048]{2,1,0:T(8,128)(2,1)S(1)}, bf16[4,40,2048]{2,1,0:T(8,128)(2,1)S(1)}, f32[4,160,1]{2,1,0:T(8,128)S(1)}) custom-call(bf16[4,40,2048]{2,1,0:T(8,128)(2,1)S(1)} %get-tuple-element.47.refs_3_.refs_0_, ...), custom_call_target="tpu_custom_call" | custom-call | flops 10066329600 | bytes 45613056 | tf_op jit(solution)/shard_map/pallas_call | solution.py:39
  137.1 1.3 collective-permute-done.22.refs_5_
  138.4 2.4 %collective-permute-start.17 = (bf16[4,40,2048]{2,1,0:T(8,128)(2,1)S(1)}, bf16[4,40,2048]{2,1,0:T(8,128)(2,1)S(1)}, u32[]{:S(2)}, u32[]{:S(2)}) collective-permute-start(bf16[4,40,2048]{2,1,0:T(8,128)(2,1)S(1)} %get-tuple-element.61), channel_id=1, source_target_pairs={{0,6},{1,7},{2,4},{3,5},{4,2},{5,3},{6,0},{7,1},{8,14},{9,15},{10,... | collective-permute-start | bytes 1966088 | tf_op jit(solution)/shard_map/ppermute | solution.py:307
  140.9 8.1 %collective-permute-done.23.refs_6_ = bf16[4,40,2048]{2,1,0:T(8,128)(2,1)S(1)} collective-permute-done((bf16[4,40,2048]{2,1,0:T(8,128)(2,1)S(1)}, bf16[4,40,2048]{2,1,0:T(8,128)(2,1)S(1)}, u32[]{:S(2)}, u32[]{:S(2)}) %collective-permute-start.23) | collective-permute-done | bytes 655392 | tf_op jit(solution)/shard_map/ppermute | solution.py:307
  149.0 4.5 %collective-permute-done.24.refs_7_ = bf16[4,40,2048]{2,1,0:T(8,128)(2,1)S(1)} collective-permute-done((bf16[4,40,2048]{2,1,0:T(8,128)(2,1)S(1)}, bf16[4,40,2048]{2,1,0:T(8,128)(2,1)S(1)}, u32[]{:S(2)}, u32[]{:S(2)}) %collective-permute-start.24) | collective-permute-done | bytes 655392 | tf_op jit(solution)/shard_map/ppermute | solution.py:307
  153.5 22.1 %shard_map.94 = (bf16[4,40,1024]{2,1,0:T(8,128)(2,1)S(1)}, bf16[4,40,1024]{2,1,0:T(8,128)(2,1)}, bf16[4,40,1024]{2,1,0:T(8,128)(2,1)}, bf16[4,40,1024]{2,1,0:T(8...) custom-call(bf16[4,40,2048]{2,1,0:T(8,128)(2,1)S(1)} %get-tuple-elem, ...), custom_call_target="tpu_custom_call" | custom-call | flops 10066329600 | bytes 45613056 | tf_op jit(solution)/shard_map/pallas_call | solution.py:39
  175.6 1.5 collective-permute-start.25
  177.7 3.9 %collective-permute-done.17 = bf16[4,40,2048]{2,1,0:T(8,128)(2,1)S(1)} collective-permute-done((bf16[4,40,2048]{2,1,0:T(8,128)(2,1)S(1)}, bf16[4,40,2048]{2,1,0:T(8,128)(2,1)S(1)}, u32[]{:S(2)}, u32[]{:S(2)}) %collective-permute-start.17) | collective-permute-done | bytes 655392 | tf_op jit(solution)/shard_map/ppermute | solution.py:307
  181.6 3.7 %shard_map.93 = (f32[128,2048]{1,0:T(8,128)S(1)}, bf16[128,2048]{1,0:T(8,128)(2,1)}) custom-call(bf16[256,640]{1,0:T(8,128)(2,1)S(1)} %copy-done.9, bf16[256,640]{1,0:T(8,128)(2,1)S(1)} %copy-done.11, bf16[160,2048]{1,0:T(8,128)(2,1)S(1)} %bitcast.31, bf16[160,2048]{1,0:T(8,128)(2,1)S(1)} %bitcast.32, bf16[160,2048]{1,0:T(8,128)(2,1)S(1)} %bitcast.33, ...), custom_call_target="tpu_custom_call" | custom-call | flops 1342177280 | bytes 4718592 | tf_op jit(solution)/shard_map/pallas_call | solution.py:39
  186.7 1.5 collective-permute-start.27
  188.2 1.7 collective-permute-start.30
  190.2 1.4 collective-permute-start.32
  192.0 1.2 reduce.1
  195.2 4.1 %all-to-all-start = ((f32[16,1,80]{2,1,0:T(1,128)}), f32[16,1,80]{2,1,0:T(1,128)S(1)}, u32[]{:S(2)}, u32[]{:S(2)}) async-start(f32[16,1,80]{2,1,0:T(1,128)} %bitcast.19), calls=%async_computation | async-start | bytes 16384 | tf_op jit(solution)/shard_map/all_to_all | solution.py:355
  199.3 3.1 %shard_map.95 = (bf16[128,1024]{1,0:T(8,128)(2,1)S(1)}, bf16[128,1024]{1,0:T(8,128)(2,1)}) custom-call(bf16[256,640]{1,0:T(8,128)(2,1)S(1)} %get-tuple-element.64.refs_0_, bf16[256,640]{1,0:T(8,128)(2,1)S(1)} %get-tuple-element.65.refs_1_, bf16[160,1024]{1,0:T(8,128)(2,1)S(1)} %bitcast.27, bf16[160,1024]{1,0:T(8,128)(2,1)S(1)} %bitcast.28, ...), custom_call_target="tpu_custom_call" | custom-call | flops 671088640 | bytes 2359296 | tf_op jit(solution)/shard_map/pallas_call | solution.py:39
  202.3 1.9 collective-permute-start.29
  204.3 2.4 collective-permute-start.28
  206.6 3.3 %all-to-all-done = f32[16,1,80]{2,1,0:T(1,128)S(1)} async-done(((f32[16,1,80]{2,1,0:T(1,128)}), f32[16,1,80]{2,1,0:T(1,128)S(1)}, u32[]{:S(2)}, u32[]{:S(2)}) %all-to-all-start) | async-done | bytes 5152 | tf_op jit(solution)/shard_map/all_to_all | solution.py:355
  210.9 2.6 %shard_map.99 = (bf16[128,1024]{1,0:T(8,128)(2,1)S(1)}, bf16[128,1024]{1,0:T(8,128)(2,1)S(1)}) custom-call(bf16[256,640]{1,0:T(8,128)(2,1)S(1)} %get-tuple-element.64.refs_0_, bf16[256,640]{1,0:T(8,128)(2,1)S(1)} %get-tuple-element.65.refs_1_, bf16[160,1024]{1,0:T(8,128)(2,1)S(1)} %bitcast.35, bf16[160,1024]{1,0:T(8,128)(2,1)} %bitcast.12.refs_3_, ...), custom_call_target="tpu_custom_call" | custom-call | flops 671088640 | bytes 2359296 | tf_op jit(solution)/shard_map/pallas_call | solution.py:39
  215.9 1.7 shard_map.100
  218.2 13.6 %collective-permute-done.28 = bf16[128,1024]{1,0:T(8,128)(2,1)} collective-permute-done((bf16[128,1024]{1,0:T(8,128)(2,1)S(1)}, bf16[128,1024]{1,0:T(8,128)(2,1)}, u32[]{:S(2)}, u32[]{:S(2)}) %collective-permute-start.28) | collective-permute-done | bytes 262176 | tf_op jit(solution)/shard_map/ppermute | solution.py:307
  231.8 5.5 %collective-permute-done.33 = bf16[128,1024]{1,0:T(8,128)(2,1)S(1)} collective-permute-done((bf16[128,1024]{1,0:T(8,128)(2,1)S(1)}, bf16[128,1024]{1,0:T(8,128)(2,1)S(1)}, u32[]{:S(2)}, u32[]{:S(2)}) %collective-permute-start.33) | collective-permute-done | bytes 262176 | tf_op jit(solution)/shard_map/ppermute | solution.py:307
  237.2 1.3 convert_add_fusion.1
  (103 shorter events, 19.6 us)
Async XLA Ops:
  0.6 27.8 %collective-permute-start.1 = (bf16[2,2048,768]{2,1,0:T(8,128)(2,1)}, bf16[2,2048,768]{2,1,0:T(8,128)(2,1)}, u32[]{:S(2)}, u32[]{:S(2)}) collective-permute-start(bf16[2,2048,768]{2,1,0:T(8,128)(2,1)} %refs_8_.3), channel_id=1, source_target_pairs={{0,1},{1,0},{2,3},{3,2},{4,5},{5,4},{6,7},{7,6},{8,9},{9,8},{10,11... | collective-permute-start | bytes 18874376 | tf_op jit(solution)/shard_map/ppermute | solution.py:307
  1.1 27.3 %collective-permute-start.2 = (bf16[2,2048,768]{2,1,0:T(8,128)(2,1)}, bf16[2,2048,768]{2,1,0:T(8,128)(2,1)}, u32[]{:S(2)}, u32[]{:S(2)}) collective-permute-start(bf16[2,2048,768]{2,1,0:T(8,128)(2,1)} %refs_9_.3), channel_id=1, source_target_pairs={{0,1},{1,0},{2,3},{3,2},{4,5},{5,4},{6,7},{7,6},{8,9},{9,8},{10,11... | collective-permute-start | bytes 18874376 | tf_op jit(solution)/shard_map/ppermute | solution.py:307
  1.2 28.0 %collective-permute-start.3 = (bf16[2,768,2048]{2,1,0:T(8,128)(2,1)}, bf16[2,768,2048]{2,1,0:T(8,128)(2,1)}, u32[]{:S(2)}, u32[]{:S(2)}) collective-permute-start(bf16[2,768,2048]{2,1,0:T(8,128)(2,1)} %refs_10_.3), channel_id=1, source_target_pairs={{0,1},{1,0},{2,3},{3,2},{4,5},{5,4},{6,7},{7,6},{8,9},{9,8},{10,11... | collective-permute-start | bytes 18874376 | tf_op jit(solution)/shard_map/ppermute | solution.py:307
  6.1 17.9 %collective-permute-start = (bf16[128,2176]{1,0:T(8,128)(2,1)S(1)}, bf16[128,2176]{1,0:T(8,128)(2,1)S(1)}, u32[]{:S(2)}, u32[]{:S(2)}) collective-permute-start(bf16[128,2176]{1,0:T(8,128)(2,1)S(1)} %concatenate.9.refs_1_), channel_id=1, source_target_pairs={{0,8},{1,9},{2,10},{3,11},{4,12},{5,13},{6,14},{7,15},{8,16},{9,17... | collective-permute-start | bytes 1671176 | tf_op jit(solution)/shard_map/ppermute | solution.py:307
  24.0 17.3 %collective-permute-start.11 = (bf16[128,2176]{1,0:T(8,128)(2,1)S(1)}, bf16[128,2176]{1,0:T(8,128)(2,1)S(1)}, u32[]{:S(2)}, u32[]{:S(2)}) collective-permute-start(bf16[128,2176]{1,0:T(8,128)(2,1)S(1)} %collective-permute-done.refs_2_), channel_id=1, source_target_pairs={{0,8},{1,9},{2,10},{3,11},{4,12},{5,13},{6,14},{7,15},{8,16},{9,17... | collective-permute-start | bytes 1671176 | tf_op jit(solution)/shard_map/ppermute | solution.py:307
  24.0 28.6 %collective-permute-start.7 = (bf16[128,2048]{1,0:T(8,128)(2,1)}, bf16[128,2048]{1,0:T(8,128)(2,1)}, u32[]{:S(2)}, u32[]{:S(2)}) collective-permute-start(bf16[128,2048]{1,0:T(8,128)(2,1)} %refs_1_.1), channel_id=1, source_target_pairs={{0,8},{1,9},{2,10},{3,11},{4,12},{5,13},{6,14},{7,15},{8,16},{9,17... | collective-permute-start | bytes 1572872 | tf_op jit(solution)/shard_map/ppermute | solution.py:307
  29.3 23.4 %copy-start.7 = (bf16[128,2048]{1,0:T(8,128)(2,1)S(1)}, bf16[128,2048]{1,0:T(8,128)(2,1)}, u32[]{:S(2)}) copy-start(bf16[128,2048]{1,0:T(8,128)(2,1)} %refs_1_.1) | copy-start | bytes 1572868
  31.7 34.3 %collective-permute-start.4 = (bf16[4,40,2048]{2,1,0:T(8,128)(2,1)S(1)}, bf16[4,40,2048]{2,1,0:T(8,128)(2,1)S(1)}, u32[]{:S(2)}, u32[]{:S(2)}) collective-permute-start(bf16[4,40,2048]{2,1,0:T(8,128)(2,1)S(1)} %get-tuple-element.48), channel_id=1, source_target_pairs={{0,2},{1,3},{2,0},{3,1},{4,6},{5,7},{6,4},{7,5},{8,10},{9,11},{10,... | collective-permute-start | bytes 1966088 | tf_op jit(solution)/shard_map/ppermute | solution.py:307
  34.6 32.9 %collective-permute-start.5 = (bf16[4,40,2048]{2,1,0:T(8,128)(2,1)S(1)}, bf16[4,40,2048]{2,1,0:T(8,128)(2,1)S(1)}, u32[]{:S(2)}, u32[]{:S(2)}) collective-permute-start(bf16[4,40,2048]{2,1,0:T(8,128)(2,1)S(1)} %get-tuple-element.49), channel_id=1, source_target_pairs={{0,4},{1,5},{2,6},{3,7},{4,0},{5,1},{6,2},{7,3},{8,12},{9,13},{10,... | collective-permute-start | bytes 1966088 | tf_op jit(solution)/shard_map/ppermute | solution.py:307
  36.2 33.5 %collective-permute-start.6 = (bf16[4,40,2048]{2,1,0:T(8,128)(2,1)S(1)}, bf16[4,40,2048]{2,1,0:T(8,128)(2,1)S(1)}, u32[]{:S(2)}, u32[]{:S(2)}) collective-permute-start(bf16[4,40,2048]{2,1,0:T(8,128)(2,1)S(1)} %get-tuple-element.50), channel_id=1, source_target_pairs={{0,6},{1,7},{2,4},{3,5},{4,2},{5,3},{6,0},{7,1},{8,14},{9,15},{10,... | collective-permute-start | bytes 1966088 | tf_op jit(solution)/shard_map/ppermute | solution.py:307
  41.3 23.2 %collective-permute-start.12 = (bf16[128,2176]{1,0:T(8,128)(2,1)S(1)}, bf16[128,2176]{1,0:T(8,128)(2,1)S(1)}, u32[]{:S(2)}, u32[]{:S(2)}) collective-permute-start(bf16[128,2176]{1,0:T(8,128)(2,1)S(1)} %collective-permute-done.11.refs_1_), channel_id=1, source_target_pairs={{0,8},{1,9},{2,10},{3,11},{4,12},{5,13},{6,14},{7,15},{8,16},{9,17... | collective-permute-start | bytes 1671176 | tf_op jit(solution)/shard_map/ppermute | solution.py:307
  52.7 21.9 %collective-permute-start.13 = (bf16[128,2048]{1,0:T(8,128)(2,1)}, bf16[128,2048]{1,0:T(8,128)(2,1)S(1)}, u32[]{:S(2)}, u32[]{:S(2)}) collective-permute-start(bf16[128,2048]{1,0:T(8,128)(2,1)} %collective-permute-done.7.refs_2_), channel_id=1, source_target_pairs={{0,8},{1,9},{2,10},{3,11},{4,12},{5,13},{6,14},{7,15},{8,16},{9,17... | collective-permute-start | bytes 1572872 | tf_op jit(solution)/shard_map/ppermute | solution.py:307
  64.5 25.9 %collective-permute-start.8 = (bf16[4,40,2048]{2,1,0:T(8,128)(2,1)S(1)}, bf16[4,40,2048]{2,1,0:T(8,128)(2,1)S(1)}, u32[]{:S(2)}, u32[]{:S(2)}) collective-permute-start(bf16[4,40,2048]{2,1,0:T(8,128)(2,1)S(1)} %get-tuple-element.52), channel_id=1, source_target_pairs={{0,2},{1,3},{2,0},{3,1},{4,6},{5,7},{6,4},{7,5},{8,10},{9,11},{10,... | collective-permute-start | bytes 1966088 | tf_op jit(solution)/shard_map/ppermute | solution.py:307
  66.0 25.9 %collective-permute-start.9 = (bf16[4,40,2048]{2,1,0:T(8,128)(2,1)S(1)}, bf16[4,40,2048]{2,1,0:T(8,128)(2,1)S(1)}, u32[]{:S(2)}, u32[]{:S(2)}) collective-permute-start(bf16[4,40,2048]{2,1,0:T(8,128)(2,1)S(1)} %get-tuple-element.53), channel_id=1, source_target_pairs={{0,4},{1,5},{2,6},{3,7},{4,0},{5,1},{6,2},{7,3},{8,12},{9,13},{10,... | collective-permute-start | bytes 1966088 | tf_op jit(solution)/shard_map/ppermute | solution.py:307
  67.5 29.7 %collective-permute-start.10 = (bf16[4,40,2048]{2,1,0:T(8,128)(2,1)S(1)}, bf16[4,40,2048]{2,1,0:T(8,128)(2,1)S(1)}, u32[]{:S(2)}, u32[]{:S(2)}) collective-permute-start(bf16[4,40,2048]{2,1,0:T(8,128)(2,1)S(1)} %get-tuple-element.54), channel_id=1, source_target_pairs={{0,6},{1,7},{2,4},{3,5},{4,2},{5,3},{6,0},{7,1},{8,14},{9,15},{10,... | collective-permute-start | bytes 1966088 | tf_op jit(solution)/shard_map/ppermute | solution.py:307
  72.1 38.2 %collective-permute-start.19 = (bf16[4,40,2048]{2,1,0:T(8,128)(2,1)S(1)}, bf16[4,40,2048]{2,1,0:T(8,128)(2,1)S(1)}, u32[]{:S(2)}, u32[]{:S(2)}) collective-permute-start(bf16[4,40,2048]{2,1,0:T(8,128)(2,1)S(1)} %get-tuple-element.66), channel_id=1, source_target_pairs={{0,2},{1,3},{2,0},{3,1},{4,6},{5,7},{6,4},{7,5},{8,10},{9,11},{10,... | collective-permute-start | bytes 1966088 | tf_op jit(solution)/shard_map/ppermute | solution.py:307
  74.6 14.6 %collective-permute-start.14 = (bf16[128,2048]{1,0:T(8,128)(2,1)S(1)}, bf16[128,2048]{1,0:T(8,128)(2,1)S(1)}, u32[]{:S(2)}, u32[]{:S(2)}) collective-permute-start(bf16[128,2048]{1,0:T(8,128)(2,1)S(1)} %collective-permute-done.13.refs_1_), channel_id=1, source_target_pairs={{0,8},{1,9},{2,10},{3,11},{4,12},{5,13},{6,14},{7,15},{8,16},{9,17... | collective-permute-start | bytes 1572872 | tf_op jit(solution)/shard_map/ppermute | solution.py:307
  89.2 46.8 %collective-permute-start.20 = (bf16[4,40,2048]{2,1,0:T(8,128)(2,1)S(1)}, bf16[4,40,2048]{2,1,0:T(8,128)(2,1)S(1)}, u32[]{:S(2)}, u32[]{:S(2)}) collective-permute-start(bf16[4,40,2048]{2,1,0:T(8,128)(2,1)S(1)} %get-tuple-element.67), channel_id=1, source_target_pairs={{0,4},{1,5},{2,6},{3,7},{4,0},{5,1},{6,2},{7,3},{8,12},{9,13},{10,... | collective-permute-start | bytes 1966088 | tf_op jit(solution)/shard_map/ppermute | solution.py:307
  90.4 46.2 %collective-permute-start.21 = (bf16[4,40,2048]{2,1,0:T(8,128)(2,1)S(1)}, bf16[4,40,2048]{2,1,0:T(8,128)(2,1)S(1)}, u32[]{:S(2)}, u32[]{:S(2)}) collective-permute-start(bf16[4,40,2048]{2,1,0:T(8,128)(2,1)S(1)} %get-tuple-element.68), channel_id=1, source_target_pairs={{0,6},{1,7},{2,4},{3,5},{4,2},{5,3},{6,0},{7,1},{8,14},{9,15},{10,... | collective-permute-start | bytes 1966088 | tf_op jit(solution)/shard_map/ppermute | solution.py:307
  97.2 56.3 %slice-start = ((s8[6291456]{0:T(1024)(128)(4,1)}), s8[4194304]{0:T(1024)(128)(4,1)S(1)}, s32[]{:S(2)}) async-start(s8[6291456]{0:T(1024)(128)(4,1)} %bitcast.25), calls=%async_computation.1 | async-start | bytes 8388608
  100.2 38.3 %collective-permute-start.22 = (bf16[4,40,2048]{2,1,0:T(8,128)(2,1)}, bf16[4,40,2048]{2,1,0:T(8,128)(2,1)S(1)}, u32[]{:S(2)}, u32[]{:S(2)}) collective-permute-start(bf16[4,40,2048]{2,1,0:T(8,128)(2,1)} %get-tuple-element.69), channel_id=1, source_target_pairs={{0,2},{1,3},{2,0},{3,1},{4,6},{5,7},{6,4},{7,5},{8,10},{9,11},{10,... | collective-permute-start | bytes 1966088 | tf_op jit(solution)/shard_map/ppermute | solution.py:307
  101.6 47.4 %collective-permute-start.23 = (bf16[4,40,2048]{2,1,0:T(8,128)(2,1)S(1)}, bf16[4,40,2048]{2,1,0:T(8,128)(2,1)S(1)}, u32[]{:S(2)}, u32[]{:S(2)}) collective-permute-start(bf16[4,40,2048]{2,1,0:T(8,128)(2,1)S(1)} %get-tuple-element.70), channel_id=1, source_target_pairs={{0,4},{1,5},{2,6},{3,7},{4,0},{5,1},{6,2},{7,3},{8,12},{9,13},{10,... | collective-permute-start | bytes 1966088 | tf_op jit(solution)/shard_map/ppermute | solution.py:307
  110.3 43.2 %collective-permute-start.24 = (bf16[4,40,2048]{2,1,0:T(8,128)(2,1)S(1)}, bf16[4,40,2048]{2,1,0:T(8,128)(2,1)S(1)}, u32[]{:S(2)}, u32[]{:S(2)}) collective-permute-start(bf16[4,40,2048]{2,1,0:T(8,128)(2,1)S(1)} %get-tuple-element.71), channel_id=1, source_target_pairs={{0,6},{1,7},{2,4},{3,5},{4,2},{5,3},{6,0},{7,1},{8,14},{9,15},{10,... | collective-permute-start | bytes 1966088 | tf_op jit(solution)/shard_map/ppermute | solution.py:307
  112.7 40.8 %slice-start.1 = ((s8[6291456]{0:T(1024)(128)(4,1)}), s8[2097152]{0:T(1024)(128)(4,1)S(1)}, s32[]{:S(2)}) async-start(s8[6291456]{0:T(1024)(128)(4,1)} %bitcast.25), calls=%async_computation.2 | async-start | bytes 4194304
  136.0 41.7 %collective-permute-start.15 = (bf16[4,40,2048]{2,1,0:T(8,128)(2,1)S(1)}, bf16[4,40,2048]{2,1,0:T(8,128)(2,1)S(1)}, u32[]{:S(2)}, u32[]{:S(2)}) collective-permute-start(bf16[4,40,2048]{2,1,0:T(8,128)(2,1)S(1)} %get-tuple-element.59), channel_id=1, source_target_pairs={{0,2},{1,3},{2,0},{3,1},{4,6},{5,7},{6,4},{7,5},{8,10},{9,11},{10,... | collective-permute-start | bytes 1966088 | tf_op jit(solution)/shard_map/ppermute | solution.py:307
  136.6 41.0 %collective-permute-start.16 = (bf16[4,40,2048]{2,1,0:T(8,128)(2,1)S(1)}, bf16[4,40,2048]{2,1,0:T(8,128)(2,1)S(1)}, u32[]{:S(2)}, u32[]{:S(2)}) collective-permute-start(bf16[4,40,2048]{2,1,0:T(8,128)(2,1)S(1)} %get-tuple-element.60), channel_id=1, source_target_pairs={{0,4},{1,5},{2,6},{3,7},{4,0},{5,1},{6,2},{7,3},{8,12},{9,13},{10,... | collective-permute-start | bytes 1966088 | tf_op jit(solution)/shard_map/ppermute | solution.py:307
  138.4 43.2 %copy-start.9 = (bf16[256,640]{1,0:T(8,128)(2,1)S(1)}, bf16[256,640]{1,0:T(8,128)(2,1)}, u32[]{:S(2)}) copy-start(bf16[256,640]{1,0:T(8,128)(2,1)} %copy-done.8) | copy-start | bytes 983044
  138.4 43.2 %copy-start.11 = (bf16[256,640]{1,0:T(8,128)(2,1)S(1)}, bf16[256,640]{1,0:T(8,128)(2,1)}, u32[]{:S(2)}) copy-start(bf16[256,640]{1,0:T(8,128)(2,1)} %copy-done.10) | copy-start | bytes 983044
  138.4 43.2 %collective-permute-start.17 = (bf16[4,40,2048]{2,1,0:T(8,128)(2,1)S(1)}, bf16[4,40,2048]{2,1,0:T(8,128)(2,1)S(1)}, u32[]{:S(2)}, u32[]{:S(2)}) collective-permute-start(bf16[4,40,2048]{2,1,0:T(8,128)(2,1)S(1)} %get-tuple-element.61), channel_id=1, source_target_pairs={{0,6},{1,7},{2,4},{3,5},{4,2},{5,3},{6,0},{7,1},{8,14},{9,15},{10,... | collective-permute-start | bytes 1966088 | tf_op jit(solution)/shard_map/ppermute | solution.py:307
  175.6 9.8 %copy-start.2 = (f32[4,160,1]{2,1,0:T(8,128)}, f32[4,160,1]{2,1,0:T(8,128)S(1)}, u32[]{:S(2)}) copy-start(f32[4,160,1]{2,1,0:T(8,128)S(1)} %get-tuple-element.83) | copy-start | bytes 7684
  175.6 10.8 %copy-start.3 = (bf16[4,40,1024]{2,1,0:T(8,128)(2,1)}, bf16[4,40,1024]{2,1,0:T(8,128)(2,1)S(1)}, u32[]{:S(2)}) copy-start(bf16[4,40,1024]{2,1,0:T(8,128)(2,1)S(1)} %get-tuple-element.81.refs_0_) | copy-start | bytes 983044
  175.6 11.0 %copy-start.4 = (bf16[4,40,1024]{2,1,0:T(8,128)(2,1)}, bf16[4,40,1024]{2,1,0:T(8,128)(2,1)S(1)}, u32[]{:S(2)}) copy-start(bf16[4,40,1024]{2,1,0:T(8,128)(2,1)S(1)} %get-tuple-element.80.refs_0_) | copy-start | bytes 983044
  175.6 11.0 %copy-start.5 = (bf16[4,40,1024]{2,1,0:T(8,128)(2,1)}, bf16[4,40,1024]{2,1,0:T(8,128)(2,1)S(1)}, u32[]{:S(2)}) copy-start(bf16[4,40,1024]{2,1,0:T(8,128)(2,1)S(1)} %get-tuple-element.79.refs_0_) | copy-start | bytes 983044
  175.6 11.0 %copy-start.12 = (bf16[4,40,1024]{2,1,0:T(8,128)(2,1)}, bf16[4,40,1024]{2,1,0:T(8,128)(2,1)S(1)}, u32[]{:S(2)}) copy-start(bf16[4,40,1024]{2,1,0:T(8,128)(2,1)S(1)} %get-tuple-element.78) | copy-start | bytes 983044
  175.6 14.3 %collective-permute-start.25 = (bf16[4,40,1024]{2,1,0:T(8,128)(2,1)}, bf16[4,40,1024]{2,1,0:T(8,128)(2,1)S(1)}, u32[]{:S(2)}, u32[]{:S(2)}) collective-permute-start(bf16[4,40,1024]{2,1,0:T(8,128)(2,1)} %get-tuple-element.73), channel_id=1, source_target_pairs={{0,2},{1,3},{2,0},{3,1},{4,6},{5,7},{6,4},{7,5},{8,10},{9,11},{10,... | collective-permute-start | bytes 983048 | tf_op jit(solution)/shard_map/ppermute | solution.py:307
  177.1 13.1 %collective-permute-start.26 = (bf16[4,40,1024]{2,1,0:T(8,128)(2,1)}, bf16[4,40,1024]{2,1,0:T(8,128)(2,1)S(1)}, u32[]{:S(2)}, u32[]{:S(2)}) collective-permute-start(bf16[4,40,1024]{2,1,0:T(8,128)(2,1)} %get-tuple-element.74), channel_id=1, source_target_pairs={{0,4},{1,5},{2,6},{3,7},{4,0},{5,1},{6,2},{7,3},{8,12},{9,13},{10,... | collective-permute-start | bytes 983048 | tf_op jit(solution)/shard_map/ppermute | solution.py:307
  186.3 12.9 %copy-start.1 = (f32[128,2048]{1,0:T(8,128)S(1)}, f32[128,2048]{1,0:T(8,128)}, u32[]{:S(2)}) copy-start(f32[128,2048]{1,0:T(8,128)} %copy-done) | copy-start | bytes 3145732
  186.4 12.9 %collective-permute-start.18 = (bf16[128,2048]{1,0:T(8,128)(2,1)}, bf16[128,2048]{1,0:T(8,128)(2,1)S(1)}, u32[]{:S(2)}, u32[]{:S(2)}) collective-permute-start(bf16[128,2048]{1,0:T(8,128)(2,1)} %get-tuple-element.63), channel_id=1, source_target_pairs={{0,24},{1,25},{2,26},{3,27},{4,28},{5,29},{6,30},{7,31},{8,0},{9,1... | collective-permute-start | bytes 1572872 | tf_op jit(solution)/shard_map/ppermute | solution.py:307
  186.7 12.6 %collective-permute-start.27 = (bf16[4,40,1024]{2,1,0:T(8,128)(2,1)}, bf16[4,40,1024]{2,1,0:T(8,128)(2,1)}, u32[]{:S(2)}, u32[]{:S(2)}) collective-permute-start(bf16[4,40,1024]{2,1,0:T(8,128)(2,1)} %get-tuple-element.75), channel_id=1, source_target_pairs={{0,6},{1,7},{2,4},{3,5},{4,2},{5,3},{6,0},{7,1},{8,14},{9,15},{10,... | collective-permute-start | bytes 983048 | tf_op jit(solution)/shard_map/ppermute | solution.py:307
  188.2 21.8 %collective-permute-start.30 = (bf16[4,40,1024]{2,1,0:T(8,128)(2,1)}, bf16[4,40,1024]{2,1,0:T(8,128)(2,1)}, u32[]{:S(2)}, u32[]{:S(2)}) collective-permute-start(bf16[4,40,1024]{2,1,0:T(8,128)(2,1)} %shard_map.96), channel_id=1, source_target_pairs={{0,2},{1,3},{2,0},{3,1},{4,6},{5,7},{6,4},{7,5},{8,10},{9,11},{10,... | collective-permute-start | bytes 983048 | tf_op jit(solution)/shard_map/ppermute | solution.py:307
  189.9 20.1 %collective-permute-start.31 = (bf16[4,40,1024]{2,1,0:T(8,128)(2,1)}, bf16[4,40,1024]{2,1,0:T(8,128)(2,1)}, u32[]{:S(2)}, u32[]{:S(2)}) collective-permute-start(bf16[4,40,1024]{2,1,0:T(8,128)(2,1)} %shard_map.97), channel_id=1, source_target_pairs={{0,4},{1,5},{2,6},{3,7},{4,0},{5,1},{6,2},{7,3},{8,12},{9,13},{10,... | collective-permute-start | bytes 983048 | tf_op jit(solution)/shard_map/ppermute | solution.py:307
  190.2 19.7 %collective-permute-start.32 = (bf16[4,40,1024]{2,1,0:T(8,128)(2,1)}, bf16[4,40,1024]{2,1,0:T(8,128)(2,1)}, u32[]{:S(2)}, u32[]{:S(2)}) collective-permute-start(bf16[4,40,1024]{2,1,0:T(8,128)(2,1)} %shard_map.98), channel_id=1, source_target_pairs={{0,6},{1,7},{2,4},{3,5},{4,2},{5,3},{6,0},{7,1},{8,14},{9,15},{10,... | collective-permute-start | bytes 983048 | tf_op jit(solution)/shard_map/ppermute | solution.py:307
  191.9 24.0 %copy-start.6 = (f32[128,8]{1,0:T(8,128)S(1)}, f32[128,8]{1,0:T(8,128)}, u32[]{:S(2)}) copy-start(f32[128,8]{1,0:T(8,128)} %get-tuple-element.97.refs_0_) | copy-start | bytes 12292
  195.2 14.8 %all-to-all-start = ((f32[16,1,80]{2,1,0:T(1,128)}), f32[16,1,80]{2,1,0:T(1,128)S(1)}, u32[]{:S(2)}, u32[]{:S(2)}) async-start(f32[16,1,80]{2,1,0:T(1,128)} %bitcast.19), calls=%async_computation | async-start | bytes 16384 | tf_op jit(solution)/shard_map/all_to_all | solution.py:355
  202.3 15.9 %collective-permute-start.29 = (bf16[128,1024]{1,0:T(8,128)(2,1)}, bf16[128,1024]{1,0:T(8,128)(2,1)S(1)}, u32[]{:S(2)}, u32[]{:S(2)}) collective-permute-start(bf16[128,1024]{1,0:T(8,128)(2,1)} %get-tuple-element.77), channel_id=1, source_target_pairs={{0,8},{1,9},{2,10},{3,11},{4,12},{5,13},{6,14},{7,15},{8,16},{9,17... | collective-permute-start | bytes 786440 | tf_op jit(solution)/shard_map/ppermute | solution.py:307
  204.3 27.5 %collective-permute-start.28 = (bf16[128,1024]{1,0:T(8,128)(2,1)S(1)}, bf16[128,1024]{1,0:T(8,128)(2,1)}, u32[]{:S(2)}, u32[]{:S(2)}) collective-permute-start(bf16[128,1024]{1,0:T(8,128)(2,1)S(1)} %get-tuple-element.76.refs_6_), channel_id=1, source_target_pairs={{0,16},{1,17},{2,18},{3,19},{4,20},{5,21},{6,22},{7,23},{8,24},{9,... | collective-permute-start | bytes 786440 | tf_op jit(solution)/shard_map/ppermute | solution.py:307
  213.5 18.3 %collective-permute-start.34 = (bf16[128,1024]{1,0:T(8,128)(2,1)S(1)}, bf16[128,1024]{1,0:T(8,128)(2,1)S(1)}, u32[]{:S(2)}, u32[]{:S(2)}) collective-permute-start(bf16[128,1024]{1,0:T(8,128)(2,1)S(1)} %get-tuple-element.85), channel_id=1, source_target_pairs={{0,8},{1,9},{2,10},{3,11},{4,12},{5,13},{6,14},{7,15},{8,16},{9,17... | collective-permute-start | bytes 786440 | tf_op jit(solution)/shard_map/ppermute | solution.py:307
  213.6 23.6 %collective-permute-start.33 = (bf16[128,1024]{1,0:T(8,128)(2,1)S(1)}, bf16[128,1024]{1,0:T(8,128)(2,1)S(1)}, u32[]{:S(2)}, u32[]{:S(2)}) collective-permute-start(bf16[128,1024]{1,0:T(8,128)(2,1)S(1)} %get-tuple-element.84), channel_id=1, source_target_pairs={{0,16},{1,17},{2,18},{3,19},{4,20},{5,21},{6,22},{7,23},{8,24},{9,... | collective-permute-start | bytes 786440 | tf_op jit(solution)/shard_map/ppermute | solution.py:307
  (4 other events, 3.4 us)

commit v4 on v3

--- a/solution.py
+++ b/solution.py
@@ -287,6 +287,34 @@
     )(ids, gate)
 
 
+def home_kernel(counts, pieces, *refs):
+    out = refs[-1]
+    step = out.shape[1] // pieces
+    for j in range(pieces):
+        columns = slice(j * step, (j + 1) * step)
+        total, first = None, 0
+        for count in counts:
+            value = refs[first + j][...] if count > 1 else refs[first][:, columns]
+            value = value.astype(F32)
+            total = value if total is None else total + value
+            first += count
+        out[:, columns] = total
+
+
+def sums_home(layers_rows, width, pieces):
+    flat = [rows for layer_rows in layers_rows for rows in layer_rows]
+    tokens = flat[0].shape[0]
+    return call(
+        functools.partial(home_kernel, [len(layer_rows) for layer_rows in layers_rows], pieces),
+        jax.ShapeDtypeStruct((tokens, width), F32),
+        (),
+        [pl.BlockSpec(memory_space=pltpu.VMEM)] * len(flat),
+        pl.BlockSpec(memory_space=pltpu.VMEM),
+        len(layers_rows) * tokens * width,
+        4 * tokens * width,
+    )(*flat)
+
+
 def local(tokens, cotangent, routing, expert_ids, gate_weight, up_weight, down_weight):
     count_ep = lax.axis_size("ep")
     owned = gate_weight.shape[0]
@@ -375,17 +403,7 @@
                 if chunk is chunks[0] and by:
                     waits.append(back)
 
-    columns = []
-    step = width // tail_pieces
-    for j in range(tail_pieces):
-        total = None
-        for by in range(layers):
-            rows = home[by]
-            value = rows[j] if len(rows) > 1 else rows[0][:, j * step : (j + 1) * step]
-            value = value.astype(F32)
-            total = value if total is None else total + value
-        columns.append(total)
-    input_grad = jnp.concatenate(columns, axis=1)
+    input_grad = sums_home([home[by] for by in range(layers)], width, tail_pieces)
     if lax.axis_size("hid") > 1:
         input_grad = lax.psum_scatter(input_grad, "hid", scatter_dimension=1, tiled=True)
         gate_grad = lax.psum(gate_grad, "hid")

time: 240 us -> 268 us (1.12)
  waiting for transfers between devices: 110 us -> 131 us
  starting transfers between devices: 42.3 us -> 48.5 us
    ppermute x35, waiting for transfers between devices: 106 us -> 130 us  [permute(): return lax.ppermute(value, 'ep', [(i, target(i)) for i in range(count_ep)])]
    ppermute x35, starting transfers between devices: 38.3 us -> 42.6 us  [permute(): return lax.ppermute(value, 'ep', [(i, target(i)) for i in range(count_ep)])]
    all_to_all x1, waiting for transfers between devices: 3.34 us -> 0.58 us  [local(): lax.all_to_all(gate_slots, 'ep', 0, 0, tiled=True, axis_index_groups=same...]
    unnamed x35 -> x37, local copies, waits for them, and re-layouts: 5.66 us -> 7.81 us
    pallas_call x12 -> x13, Pallas kernels: 70.8 us -> 71.8 us  [call(): return lambda *args: run(*args, *waits)]
  transfers between devices with their start and end apart: 36 -> 36, of which waited for: 16 -> 16; matrix products, arithmetic and copies ran while one was open for 4% -> 3% of each run, Pallas kernels for 30% -> 26%
where the time goes in v4:
time: 268 us
  waiting for transfers between devices  131 us (49%)
  Pallas kernels  71.8 us (27%)
  starting transfers between devices  48.5 us (18%)
  local copies, waits for them, and re-layouts  11.9 us (4%)
  other arithmetic  3.59 us (1%)
    ppermute x35, waiting for transfers between devices, permute(): return lax.ppermute(value, 'ep', [(i, target(i)) for i in range(count_ep)])  130 us
    pallas_call x13, Pallas kernels, call(): return lambda *args: run(*args, *waits)  71.8 us
    ppermute x35, starting transfers between devices, permute(): return lax.ppermute(value, 'ep', [(i, target(i)) for i in range(count_ep)])  42.6 us
    unnamed x37, local copies, waits for them, and re-layouts  7.81 us
    all_to_all x1, starting transfers between devices, local(): lax.all_to_all(gate_slots, 'ep', 0, 0, tiled=True, axis_index_groups=same...  5.92 us
  transfers between devices with their start and end apart: 36, of which 16 were waited for; matrix products, arithmetic and copies ran while one was open for 3% of the time, Pallas kernels for 26%

profile of v4, /device:TPU:0, one launch (start us, length us, event | category | flops | bytes accessed | tf_op | source)
XLA Modules:
  0.0 267.5 jit_solution(3193741625541784901)
XLA Ops:
  4.9 1.2 concatenate.6.refs_1_
  6.1 2.7 %collective-permute-start = (bf16[128,2176]{1,0:T(8,128)(2,1)S(1)}, bf16[128,2176]{1,0:T(8,128)(2,1)S(1)}, u32[]{:S(2)}, u32[]{:S(2)}) collective-permute-start(bf16[128,2176]{1,0:T(8,128)(2,1)S(1)} %concatenate.6.refs_1_), channel_id=1, source_target_pairs={{0,8},{1,9},{2,10},{3,11},{4,12},{5,13},{6,14},{7,15},{8,16},{9,17... | collective-permute-start | bytes 1671176 | tf_op jit(solution)/shard_map/ppermute | solution.py:335
  8.8 15.2 %collective-permute-done.refs_2_ = bf16[128,2176]{1,0:T(8,128)(2,1)S(1)} collective-permute-done((bf16[128,2176]{1,0:T(8,128)(2,1)S(1)}, bf16[128,2176]{1,0:T(8,128)(2,1)S(1)}, u32[]{:S(2)}, u32[]{:S(2)}) %collective-permute-start) | collective-permute-done | bytes 557088 | tf_op jit(solution)/shard_map/ppermute | solution.py:335
  24.0 1.3 collective-permute-start.7
  25.4 1.6 shard_map.86
  29.3 2.4 shard_map.87
  31.7 2.9 %collective-permute-start.4 = (bf16[4,40,2048]{2,1,0:T(8,128)(2,1)S(1)}, bf16[4,40,2048]{2,1,0:T(8,128)(2,1)S(1)}, u32[]{:S(2)}, u32[]{:S(2)}) collective-permute-start(bf16[4,40,2048]{2,1,0:T(8,128)(2,1)S(1)} %get-tuple-element.48), channel_id=1, source_target_pairs={{0,2},{1,3},{2,0},{3,1},{4,6},{5,7},{6,4},{7,5},{8,10},{9,11},{10,... | collective-permute-start | bytes 1966088 | tf_op jit(solution)/shard_map/ppermute | solution.py:335
  34.6 6.7 %collective-permute-done.11.refs_1_ = bf16[128,2176]{1,0:T(8,128)(2,1)S(1)} collective-permute-done((bf16[128,2176]{1,0:T(8,128)(2,1)S(1)}, bf16[128,2176]{1,0:T(8,128)(2,1)S(1)}, u32[]{:S(2)}, u32[]{:S(2)}) %collective-permute-start.11) | collective-permute-done | bytes 557088 | tf_op jit(solution)/shard_map/ppermute | solution.py:335
  41.3 11.3 %collective-permute-done.7.refs_2_ = bf16[128,2048]{1,0:T(8,128)(2,1)} collective-permute-done((bf16[128,2048]{1,0:T(8,128)(2,1)}, bf16[128,2048]{1,0:T(8,128)(2,1)}, u32[]{:S(2)}, u32[]{:S(2)}) %collective-permute-start.7) | collective-permute-done | bytes 524320 | tf_op jit(solution)/shard_map/ppermute | solution.py:335
  52.7 1.5 collective-permute-start.5
  54.2 1.4 collective-permute-start.6
  55.7 3.5 %shard_map.88 = (bf16[4,40,2048]{2,1,0:T(8,128)(2,1)S(1)}, bf16[4,40,2048]{2,1,0:T(8,128)(2,1)S(1)}, bf16[4,40,2048]{2,1,0:T(8,128)(2,1)S(1)}, bf16[4,40,2048]{2,1,0:T(8,128)(2,1)S(1)}) custom-call(bf16[640,256]{1,0:T(8,128)(2,1)S(1)} %get-tuple-element.46.refs_0_, bf16[128,2048]{1,0:T(8,128)(2,1)S(1)} %copy-done.7, ...), custom_call_target="tpu_custom_call" | custom-call | flops 671088640 | bytes 3670016 | tf_op jit(solution)/shard_map/pallas_call | solution.py:39
  59.1 15.5 %collective-permute-done.13.refs_1_ = bf16[128,2048]{1,0:T(8,128)(2,1)S(1)} collective-permute-done((bf16[128,2048]{1,0:T(8,128)(2,1)}, bf16[128,2048]{1,0:T(8,128)(2,1)S(1)}, u32[]{:S(2)}, u32[]{:S(2)}) %collective-permute-start.13) | collective-permute-done | bytes 524320 | tf_op jit(solution)/shard_map/ppermute | solution.py:335
  74.6 2.3 collective-permute-start.10
  78.1 19.1 %collective-permute-done.5.refs_5_.refs_2_ = bf16[4,40,2048]{2,1,0:T(8,128)(2,1)S(1)} collective-permute-done((bf16[4,40,2048]{2,1,0:T(8,128)(2,1)S(1)}, bf16[4,40,2048]{2,1,0:T(8,128)(2,1)S(1)}, u32[]{:S(2)}, u32[]{:S(2)}) %collective-permute-start.5) | collective-permute-done | bytes 655392 | tf_op jit(solution)/shard_map/ppermute | solution.py:335
  97.3 1.6 shard_map.89
  98.9 2.5 shard_map.90
  101.4 7.6 %collective-permute-done.14.refs_2_ = bf16[128,2048]{1,0:T(8,128)(2,1)S(1)} collective-permute-done((bf16[128,2048]{1,0:T(8,128)(2,1)S(1)}, bf16[128,2048]{1,0:T(8,128)(2,1)S(1)}, u32[]{:S(2)}, u32[]{:S(2)}) %collective-permute-start.14) | collective-permute-done | bytes 524320 | tf_op jit(solution)/shard_map/ppermute | solution.py:335
  109.3 2.2 shard_map.91
  111.5 1.3 collective-permute-start.22
  112.8 2.0 collective-permute-start.23
  115.1 1.2 collective-permute-start.19
  116.3 2.0 collective-permute-start.20
  118.2 11.0 %collective-permute-done.22.refs_5_ = bf16[4,40,2048]{2,1,0:T(8,128)(2,1)S(1)} collective-permute-done((bf16[4,40,2048]{2,1,0:T(8,128)(2,1)S(1)}, bf16[4,40,2048]{2,1,0:T(8,128)(2,1)S(1)}, u32[]{:S(2)}, u32[]{:S(2)}) %collective-permute-start.22) | collective-permute-done | bytes 655392 | tf_op jit(solution)/shard_map/ppermute | solution.py:335
  129.3 2.6 collective-permute-start.21
  131.9 23.2 %shard_map.92 = (bf16[4,40,2048]{2,1,0:T(8,128)(2,1)S(1)}, bf16[4,40,2048]{2,1,0:T(8,128)(2,1)S(1)}, bf16[4,40,2048]{2,1,0:T(8,128)(2,1)S(1)}, bf16[4,40,2048]{2,1,0:T(8,128)(2,1)S(1)}, f32[4,160,1]{2,1,0:T(8,128)S(1)}) custom-call(bf16[4,40,2048]{2,1,0:T(8,128)(2,1)S(1)} %get-tuple-element.47.refs_3_.refs_0_, ...), custom_call_target="tpu_custom_call" | custom-call | flops 10066329600 | bytes 45613056 | tf_op jit(solution)/shard_map/pallas_call | solution.py:39
  156.1 1.3 collective-permute-done.19.refs_1_
  157.4 2.6 collective-permute-start.17
  160.0 12.6 %collective-permute-done.20.refs_2_ = bf16[4,40,2048]{2,1,0:T(8,128)(2,1)S(1)} collective-permute-done((bf16[4,40,2048]{2,1,0:T(8,128)(2,1)S(1)}, bf16[4,40,2048]{2,1,0:T(8,128)(2,1)S(1)}, u32[]{:S(2)}, u32[]{:S(2)}) %collective-permute-start.20) | collective-permute-done | bytes 655392 | tf_op jit(solution)/shard_map/ppermute | solution.py:335
  172.6 22.0 %shard_map.94 = (bf16[4,40,1024]{2,1,0:T(8,128)(2,1)S(1)}, bf16[4,40,1024]{2,1,0:T(8,128)(2,1)}, bf16[4,40,1024]{2,1,0:T(8,128)(2,1)S(1)}, bf16[4,40,1024]{2,1,0...) custom-call(bf16[4,40,2048]{2,1,0:T(8,128)(2,1)S(1)} %get-tuple-elem, ...), custom_call_target="tpu_custom_call" | custom-call | flops 10066329600 | bytes 45613056 | tf_op jit(solution)/shard_map/pallas_call | solution.py:39
  196.8 1.6 collective-permute-start.27
  198.4 1.8 collective-permute-start.25
  200.2 1.2 collective-permute-done.16
  201.5 3.7 %shard_map.93 = (f32[128,2048]{1,0:T(8,128)S(1)}, bf16[128,2048]{1,0:T(8,128)(2,1)}) custom-call(bf16[256,640]{1,0:T(8,128)(2,1)S(1)} %copy-done.9, bf16[256,640]{1,0:T(8,128)(2,1)S(1)} %copy-done.11, bf16[160,2048]{1,0:T(8,128)(2,1)S(1)} %bitcast.31, bf16[160,2048]{1,0:T(8,128)(2,1)S(1)} %bitcast.32, bf16[160,2048]{1,0:T(8,128)(2,1)S(1)} %bitcast.33, ...), custom_call_target="tpu_custom_call" | custom-call | flops 1342177280 | bytes 4718592 | tf_op jit(solution)/shard_map/pallas_call | solution.py:39
  206.2 3.5 %collective-permute-start.18 = (bf16[128,2048]{1,0:T(8,128)(2,1)}, bf16[128,2048]{1,0:T(8,128)(2,1)S(1)}, u32[]{:S(2)}, u32[]{:S(2)}) collective-permute-start(bf16[128,2048]{1,0:T(8,128)(2,1)} %get-tuple-element.63), channel_id=1, source_target_pairs={{0,24},{1,25},{2,26},{3,27},{4,28},{5,29},{6,30},{7,31},{8,0},{9,1... | collective-permute-start | bytes 1572872 | tf_op jit(solution)/shard_map/ppermute | solution.py:335
  209.8 1.6 collective-permute-start.31
  211.8 1.5 collective-permute-start.29
  213.3 1.5 collective-permute-done.25
  214.9 1.3 collective-permute-start.26
  216.5 1.2 reduce.1
  219.7 5.9 %all-to-all-start = ((f32[16,1,80]{2,1,0:T(1,128)}), f32[16,1,80]{2,1,0:T(1,128)S(1)}, u32[]{:S(2)}, u32[]{:S(2)}) async-start(f32[16,1,80]{2,1,0:T(1,128)} %bitcast.19), calls=%async_computation | async-start | bytes 16384 | tf_op jit(solution)/shard_map/all_to_all | solution.py:383
  225.6 3.8 %collective-permute-done.26 = bf16[4,40,1024]{2,1,0:T(8,128)(2,1)} collective-permute-done((bf16[4,40,1024]{2,1,0:T(8,128)(2,1)}, bf16[4,40,1024]{2,1,0:T(8,128)(2,1)}, u32[]{:S(2)}, u32[]{:S(2)}) %collective-permute-start.26) | collective-permute-done | bytes 327712 | tf_op jit(solution)/shard_map/ppermute | solution.py:335
  229.4 3.0 %shard_map.95 = (bf16[128,1024]{1,0:T(8,128)(2,1)}, bf16[128,1024]{1,0:T(8,128)(2,1)S(1)}) custom-call(bf16[256,640]{1,0:T(8,128)(2,1)S(1)} %get-tuple-element.64.refs_0_, bf16[256,640]{1,0:T(8,128)(2,1)S(1)} %get-tuple-element.65.refs_1_, bf16[160,1024]{1,0:T(8,128)(2,1)S(1)} %bitcast.27, bf16[160,1024]{1,0:T(8,128)(2,1)S(1)} %bitcast.29, ...), custom_call_target="tpu_custom_call" | custom-call | flops 671088640 | bytes 2359296 | tf_op jit(solution)/shard_map/pallas_call | solution.py:39
  233.9 3.1 %shard_map.99 = (bf16[128,1024]{1,0:T(8,128)(2,1)}, bf16[128,1024]{1,0:T(8,128)(2,1)S(1)}) custom-call(bf16[256,640]{1,0:T(8,128)(2,1)S(1)} %get-tuple-element.64.refs_0_, bf16[256,640]{1,0:T(8,128)(2,1)S(1)} %get-tuple-element.65.refs_1_, bf16[160,1024]{1,0:T(8,128)(2,1)S(1)} %bitcast.35, bf16[160,1024]{1,0:T(8,128)(2,1)} %bitcast.12.refs_3_, ...), custom_call_target="tpu_custom_call" | custom-call | flops 671088640 | bytes 2359296 | tf_op jit(solution)/shard_map/pallas_call | solution.py:39
  237.1 2.4 collective-permute-start.32
  241.9 1.7 shard_map.101
  244.2 22.1 %collective-permute-done.32.refs_3_ = bf16[128,1024]{1,0:T(8,128)(2,1)S(1)} collective-permute-done((bf16[128,1024]{1,0:T(8,128)(2,1)}, bf16[128,1024]{1,0:T(8,128)(2,1)S(1)}, u32[]{:S(2)}, u32[]{:S(2)}) %collective-permute-start.32) | collective-permute-done | bytes 262176 | tf_op jit(solution)/shard_map/ppermute | solution.py:335
  266.3 1.2 shard_map.100
  (104 shorter events, 19.9 us)
Async XLA Ops:
  0.6 27.8 %collective-permute-start.1 = (bf16[2,2048,768]{2,1,0:T(8,128)(2,1)}, bf16[2,2048,768]{2,1,0:T(8,128)(2,1)}, u32[]{:S(2)}, u32[]{:S(2)}) collective-permute-start(bf16[2,2048,768]{2,1,0:T(8,128)(2,1)} %refs_8_.3), channel_id=1, source_target_pairs={{0,1},{1,0},{2,3},{3,2},{4,5},{5,4},{6,7},{7,6},{8,9},{9,8},{10,11... | collective-permute-start | bytes 18874376 | tf_op jit(solution)/shard_map/ppermute | solution.py:335
  1.1 27.3 %collective-permute-start.2 = (bf16[2,2048,768]{2,1,0:T(8,128)(2,1)}, bf16[2,2048,768]{2,1,0:T(8,128)(2,1)}, u32[]{:S(2)}, u32[]{:S(2)}) collective-permute-start(bf16[2,2048,768]{2,1,0:T(8,128)(2,1)} %refs_9_.3), channel_id=1, source_target_pairs={{0,1},{1,0},{2,3},{3,2},{4,5},{5,4},{6,7},{7,6},{8,9},{9,8},{10,11... | collective-permute-start | bytes 18874376 | tf_op jit(solution)/shard_map/ppermute | solution.py:335
  1.2 28.0 %collective-permute-start.3 = (bf16[2,768,2048]{2,1,0:T(8,128)(2,1)}, bf16[2,768,2048]{2,1,0:T(8,128)(2,1)}, u32[]{:S(2)}, u32[]{:S(2)}) collective-permute-start(bf16[2,768,2048]{2,1,0:T(8,128)(2,1)} %refs_10_.3), channel_id=1, source_target_pairs={{0,1},{1,0},{2,3},{3,2},{4,5},{5,4},{6,7},{7,6},{8,9},{9,8},{10,11... | collective-permute-start | bytes 18874376 | tf_op jit(solution)/shard_map/ppermute | solution.py:335
  6.1 17.9 %collective-permute-start = (bf16[128,2176]{1,0:T(8,128)(2,1)S(1)}, bf16[128,2176]{1,0:T(8,128)(2,1)S(1)}, u32[]{:S(2)}, u32[]{:S(2)}) collective-permute-start(bf16[128,2176]{1,0:T(8,128)(2,1)S(1)} %concatenate.6.refs_1_), channel_id=1, source_target_pairs={{0,8},{1,9},{2,10},{3,11},{4,12},{5,13},{6,14},{7,15},{8,16},{9,17... | collective-permute-start | bytes 1671176 | tf_op jit(solution)/shard_map/ppermute | solution.py:335
  24.0 17.3 %collective-permute-start.11 = (bf16[128,2176]{1,0:T(8,128)(2,1)S(1)}, bf16[128,2176]{1,0:T(8,128)(2,1)S(1)}, u32[]{:S(2)}, u32[]{:S(2)}) collective-permute-start(bf16[128,2176]{1,0:T(8,128)(2,1)S(1)} %collective-permute-done.refs_2_), channel_id=1, source_target_pairs={{0,8},{1,9},{2,10},{3,11},{4,12},{5,13},{6,14},{7,15},{8,16},{9,17... | collective-permute-start | bytes 1671176 | tf_op jit(solution)/shard_map/ppermute | solution.py:335
  24.0 28.6 %collective-permute-start.7 = (bf16[128,2048]{1,0:T(8,128)(2,1)}, bf16[128,2048]{1,0:T(8,128)(2,1)}, u32[]{:S(2)}, u32[]{:S(2)}) collective-permute-start(bf16[128,2048]{1,0:T(8,128)(2,1)} %refs_1_.1), channel_id=1, source_target_pairs={{0,8},{1,9},{2,10},{3,11},{4,12},{5,13},{6,14},{7,15},{8,16},{9,17... | collective-permute-start | bytes 1572872 | tf_op jit(solution)/shard_map/ppermute | solution.py:335
  29.3 26.4 %copy-start.7 = (bf16[128,2048]{1,0:T(8,128)(2,1)S(1)}, bf16[128,2048]{1,0:T(8,128)(2,1)}, u32[]{:S(2)}) copy-start(bf16[128,2048]{1,0:T(8,128)(2,1)} %refs_1_.1) | copy-start | bytes 1572868
  31.7 45.7 %collective-permute-start.4 = (bf16[4,40,2048]{2,1,0:T(8,128)(2,1)S(1)}, bf16[4,40,2048]{2,1,0:T(8,128)(2,1)S(1)}, u32[]{:S(2)}, u32[]{:S(2)}) collective-permute-start(bf16[4,40,2048]{2,1,0:T(8,128)(2,1)S(1)} %get-tuple-element.48), channel_id=1, source_target_pairs={{0,2},{1,3},{2,0},{3,1},{4,6},{5,7},{6,4},{7,5},{8,10},{9,11},{10,... | collective-permute-start | bytes 1966088 | tf_op jit(solution)/shard_map/ppermute | solution.py:335
  41.3 35.6 %collective-permute-start.12 = (bf16[128,2176]{1,0:T(8,128)(2,1)S(1)}, bf16[128,2176]{1,0:T(8,128)(2,1)S(1)}, u32[]{:S(2)}, u32[]{:S(2)}) collective-permute-start(bf16[128,2176]{1,0:T(8,128)(2,1)S(1)} %collective-permute-done.11.refs_1_), channel_id=1, source_target_pairs={{0,8},{1,9},{2,10},{3,11},{4,12},{5,13},{6,14},{7,15},{8,16},{9,17... | collective-permute-start | bytes 1671176 | tf_op jit(solution)/shard_map/ppermute | solution.py:335
  52.7 21.9 %collective-permute-start.13 = (bf16[128,2048]{1,0:T(8,128)(2,1)}, bf16[128,2048]{1,0:T(8,128)(2,1)S(1)}, u32[]{:S(2)}, u32[]{:S(2)}) collective-permute-start(bf16[128,2048]{1,0:T(8,128)(2,1)} %collective-permute-done.7.refs_2_), channel_id=1, source_target_pairs={{0,8},{1,9},{2,10},{3,11},{4,12},{5,13},{6,14},{7,15},{8,16},{9,17... | collective-permute-start | bytes 1572872 | tf_op jit(solution)/shard_map/ppermute | solution.py:335
  52.7 44.6 %collective-permute-start.5 = (bf16[4,40,2048]{2,1,0:T(8,128)(2,1)S(1)}, bf16[4,40,2048]{2,1,0:T(8,128)(2,1)S(1)}, u32[]{:S(2)}, u32[]{:S(2)}) collective-permute-start(bf16[4,40,2048]{2,1,0:T(8,128)(2,1)S(1)} %get-tuple-element.49), channel_id=1, source_target_pairs={{0,4},{1,5},{2,6},{3,7},{4,0},{5,1},{6,2},{7,3},{8,12},{9,13},{10,... | collective-permute-start | bytes 1966088 | tf_op jit(solution)/shard_map/ppermute | solution.py:335
  54.2 44.7 %collective-permute-start.6 = (bf16[4,40,2048]{2,1,0:T(8,128)(2,1)S(1)}, bf16[4,40,2048]{2,1,0:T(8,128)(2,1)S(1)}, u32[]{:S(2)}, u32[]{:S(2)}) collective-permute-start(bf16[4,40,2048]{2,1,0:T(8,128)(2,1)S(1)} %get-tuple-element.50), channel_id=1, source_target_pairs={{0,6},{1,7},{2,4},{3,5},{4,2},{5,3},{6,0},{7,1},{8,14},{9,15},{10,... | collective-permute-start | bytes 1966088 | tf_op jit(solution)/shard_map/ppermute | solution.py:335
  74.6 34.4 %collective-permute-start.10 = (bf16[4,40,2048]{2,1,0:T(8,128)(2,1)S(1)}, bf16[4,40,2048]{2,1,0:T(8,128)(2,1)S(1)}, u32[]{:S(2)}, u32[]{:S(2)}) collective-permute-start(bf16[4,40,2048]{2,1,0:T(8,128)(2,1)S(1)} %get-tuple-element.54), channel_id=1, source_target_pairs={{0,6},{1,7},{2,4},{3,5},{4,2},{5,3},{6,0},{7,1},{8,14},{9,15},{10,... | collective-permute-start | bytes 1966088 | tf_op jit(solution)/shard_map/ppermute | solution.py:335
  76.9 32.1 %collective-permute-start.8 = (bf16[4,40,2048]{2,1,0:T(8,128)(2,1)S(1)}, bf16[4,40,2048]{2,1,0:T(8,128)(2,1)S(1)}, u32[]{:S(2)}, u32[]{:S(2)}) collective-permute-start(bf16[4,40,2048]{2,1,0:T(8,128)(2,1)S(1)} %get-tuple-element.52), channel_id=1, source_target_pairs={{0,2},{1,3},{2,0},{3,1},{4,6},{5,7},{6,4},{7,5},{8,10},{9,11},{10,... | collective-permute-start | bytes 1966088 | tf_op jit(solution)/shard_map/ppermute | solution.py:335
  77.5 31.8 %collective-permute-start.9 = (bf16[4,40,2048]{2,1,0:T(8,128)(2,1)S(1)}, bf16[4,40,2048]{2,1,0:T(8,128)(2,1)S(1)}, u32[]{:S(2)}, u32[]{:S(2)}) collective-permute-start(bf16[4,40,2048]{2,1,0:T(8,128)(2,1)S(1)} %get-tuple-element.53), channel_id=1, source_target_pairs={{0,4},{1,5},{2,6},{3,7},{4,0},{5,1},{6,2},{7,3},{8,12},{9,13},{10,... | collective-permute-start | bytes 1966088 | tf_op jit(solution)/shard_map/ppermute | solution.py:335
  97.3 11.7 %collective-permute-start.14 = (bf16[128,2048]{1,0:T(8,128)(2,1)S(1)}, bf16[128,2048]{1,0:T(8,128)(2,1)S(1)}, u32[]{:S(2)}, u32[]{:S(2)}) collective-permute-start(bf16[128,2048]{1,0:T(8,128)(2,1)S(1)} %collective-permute-done.13.refs_1_), channel_id=1, source_target_pairs={{0,8},{1,9},{2,10},{3,11},{4,12},{5,13},{6,14},{7,15},{8,16},{9,17... | collective-permute-start | bytes 1572872 | tf_op jit(solution)/shard_map/ppermute | solution.py:335
  109.3 63.3 %slice-start = ((s8[6291456]{0:T(1024)(128)(4,1)}), s8[4194304]{0:T(1024)(128)(4,1)S(1)}, s32[]{:S(2)}) async-start(s8[6291456]{0:T(1024)(128)(4,1)} %bitcast.25), calls=%async_computation.1 | async-start | bytes 8388608
  111.5 17.7 %collective-permute-start.22 = (bf16[4,40,2048]{2,1,0:T(8,128)(2,1)S(1)}, bf16[4,40,2048]{2,1,0:T(8,128)(2,1)S(1)}, u32[]{:S(2)}, u32[]{:S(2)}) collective-permute-start(bf16[4,40,2048]{2,1,0:T(8,128)(2,1)S(1)} %get-tuple-element.69), channel_id=1, source_target_pairs={{0,2},{1,3},{2,0},{3,1},{4,6},{5,7},{6,4},{7,5},{8,10},{9,11},{10,... | collective-permute-start | bytes 1966088 | tf_op jit(solution)/shard_map/ppermute | solution.py:335
  112.8 42.3 %collective-permute-start.23 = (bf16[4,40,2048]{2,1,0:T(8,128)(2,1)S(1)}, bf16[4,40,2048]{2,1,0:T(8,128)(2,1)S(1)}, u32[]{:S(2)}, u32[]{:S(2)}) collective-permute-start(bf16[4,40,2048]{2,1,0:T(8,128)(2,1)S(1)} %get-tuple-element.70), channel_id=1, source_target_pairs={{0,4},{1,5},{2,6},{3,7},{4,0},{5,1},{6,2},{7,3},{8,12},{9,13},{10,... | collective-permute-start | bytes 1966088 | tf_op jit(solution)/shard_map/ppermute | solution.py:335
  114.7 40.7 %collective-permute-start.24 = (bf16[4,40,2048]{2,1,0:T(8,128)(2,1)S(1)}, bf16[4,40,2048]{2,1,0:T(8,128)(2,1)S(1)}, u32[]{:S(2)}, u32[]{:S(2)}) collective-permute-start(bf16[4,40,2048]{2,1,0:T(8,128)(2,1)S(1)} %get-tuple-element.71), channel_id=1, source_target_pairs={{0,6},{1,7},{2,4},{3,5},{4,2},{5,3},{6,0},{7,1},{8,14},{9,15},{10,... | collective-permute-start | bytes 1966088 | tf_op jit(solution)/shard_map/ppermute | solution.py:335
  115.1 42.3 %collective-permute-start.19 = (bf16[4,40,2048]{2,1,0:T(8,128)(2,1)S(1)}, bf16[4,40,2048]{2,1,0:T(8,128)(2,1)S(1)}, u32[]{:S(2)}, u32[]{:S(2)}) collective-permute-start(bf16[4,40,2048]{2,1,0:T(8,128)(2,1)S(1)} %get-tuple-element.66), channel_id=1, source_target_pairs={{0,2},{1,3},{2,0},{3,1},{4,6},{5,7},{6,4},{7,5},{8,10},{9,11},{10,... | collective-permute-start | bytes 1966088 | tf_op jit(solution)/shard_map/ppermute | solution.py:335
  116.3 56.3 %collective-permute-start.20 = (bf16[4,40,2048]{2,1,0:T(8,128)(2,1)S(1)}, bf16[4,40,2048]{2,1,0:T(8,128)(2,1)S(1)}, u32[]{:S(2)}, u32[]{:S(2)}) collective-permute-start(bf16[4,40,2048]{2,1,0:T(8,128)(2,1)S(1)} %get-tuple-element.67), channel_id=1, source_target_pairs={{0,4},{1,5},{2,6},{3,7},{4,0},{5,1},{6,2},{7,3},{8,12},{9,13},{10,... | collective-permute-start | bytes 1966088 | tf_op jit(solution)/shard_map/ppermute | solution.py:335
  129.3 43.3 %collective-permute-start.21 = (bf16[4,40,2048]{2,1,0:T(8,128)(2,1)S(1)}, bf16[4,40,2048]{2,1,0:T(8,128)(2,1)S(1)}, u32[]{:S(2)}, u32[]{:S(2)}) collective-permute-start(bf16[4,40,2048]{2,1,0:T(8,128)(2,1)S(1)} %get-tuple-element.68), channel_id=1, source_target_pairs={{0,6},{1,7},{2,4},{3,5},{4,2},{5,3},{6,0},{7,1},{8,14},{9,15},{10,... | collective-permute-start | bytes 1966088 | tf_op jit(solution)/shard_map/ppermute | solution.py:335
  131.9 40.7 %slice-start.1 = ((s8[6291456]{0:T(1024)(128)(4,1)}), s8[2097152]{0:T(1024)(128)(4,1)S(1)}, s32[]{:S(2)}) async-start(s8[6291456]{0:T(1024)(128)(4,1)} %bitcast.25), calls=%async_computation.2 | async-start | bytes 4194304
  155.1 45.1 %collective-permute-start.15 = (bf16[4,40,2048]{2,1,0:T(8,128)(2,1)S(1)}, bf16[4,40,2048]{2,1,0:T(8,128)(2,1)S(1)}, u32[]{:S(2)}, u32[]{:S(2)}) collective-permute-start(bf16[4,40,2048]{2,1,0:T(8,128)(2,1)S(1)} %get-tuple-element.59), channel_id=1, source_target_pairs={{0,2},{1,3},{2,0},{3,1},{4,6},{5,7},{6,4},{7,5},{8,10},{9,11},{10,... | collective-permute-start | bytes 1966088 | tf_op jit(solution)/shard_map/ppermute | solution.py:335
  155.4 46.0 %collective-permute-start.16 = (bf16[4,40,2048]{2,1,0:T(8,128)(2,1)S(1)}, bf16[4,40,2048]{2,1,0:T(8,128)(2,1)S(1)}, u32[]{:S(2)}, u32[]{:S(2)}) collective-permute-start(bf16[4,40,2048]{2,1,0:T(8,128)(2,1)S(1)} %get-tuple-element.60), channel_id=1, source_target_pairs={{0,4},{1,5},{2,6},{3,7},{4,0},{5,1},{6,2},{7,3},{8,12},{9,13},{10,... | collective-permute-start | bytes 1966088 | tf_op jit(solution)/shard_map/ppermute | solution.py:335
  157.4 44.1 %copy-start.9 = (bf16[256,640]{1,0:T(8,128)(2,1)S(1)}, bf16[256,640]{1,0:T(8,128)(2,1)}, u32[]{:S(2)}) copy-start(bf16[256,640]{1,0:T(8,128)(2,1)} %copy-done.8) | copy-start | bytes 983044
  157.4 44.1 %copy-start.11 = (bf16[256,640]{1,0:T(8,128)(2,1)S(1)}, bf16[256,640]{1,0:T(8,128)(2,1)}, u32[]{:S(2)}) copy-start(bf16[256,640]{1,0:T(8,128)(2,1)} %copy-done.10) | copy-start | bytes 983044
  157.4 44.1 %collective-permute-start.17 = (bf16[4,40,2048]{2,1,0:T(8,128)(2,1)S(1)}, bf16[4,40,2048]{2,1,0:T(8,128)(2,1)S(1)}, u32[]{:S(2)}, u32[]{:S(2)}) collective-permute-start(bf16[4,40,2048]{2,1,0:T(8,128)(2,1)S(1)} %get-tuple-element.61), channel_id=1, source_target_pairs={{0,6},{1,7},{2,4},{3,5},{4,2},{5,3},{6,0},{7,1},{8,14},{9,15},{10,... | collective-permute-start | bytes 1966088 | tf_op jit(solution)/shard_map/ppermute | solution.py:335
  196.8 8.4 %copy-start.2 = (f32[4,160,1]{2,1,0:T(8,128)}, f32[4,160,1]{2,1,0:T(8,128)S(1)}, u32[]{:S(2)}) copy-start(f32[4,160,1]{2,1,0:T(8,128)S(1)} %get-tuple-element.82) | copy-start | bytes 7684
  196.8 9.4 %copy-start.3 = (bf16[4,40,1024]{2,1,0:T(8,128)(2,1)}, bf16[4,40,1024]{2,1,0:T(8,128)(2,1)S(1)}, u32[]{:S(2)}) copy-start(bf16[4,40,1024]{2,1,0:T(8,128)(2,1)S(1)} %get-tuple-element.78.refs_0_) | copy-start | bytes 983044
  196.8 12.9 %copy-start.12 = (bf16[4,40,1024]{2,1,0:T(8,128)(2,1)}, bf16[4,40,1024]{2,1,0:T(8,128)(2,1)S(1)}, u32[]{:S(2)}) copy-start(bf16[4,40,1024]{2,1,0:T(8,128)(2,1)S(1)} %get-tuple-element.77) | copy-start | bytes 983044
  196.8 15.0 %collective-permute-start.27 = (bf16[4,40,1024]{2,1,0:T(8,128)(2,1)}, bf16[4,40,1024]{2,1,0:T(8,128)(2,1)S(1)}, u32[]{:S(2)}, u32[]{:S(2)}) collective-permute-start(bf16[4,40,1024]{2,1,0:T(8,128)(2,1)} %get-tuple-element.75), channel_id=1, source_target_pairs={{0,6},{1,7},{2,4},{3,5},{4,2},{5,3},{6,0},{7,1},{8,14},{9,15},{10,... | collective-permute-start | bytes 983048 | tf_op jit(solution)/shard_map/ppermute | solution.py:335
  198.4 16.4 %collective-permute-start.25 = (bf16[4,40,1024]{2,1,0:T(8,128)(2,1)}, bf16[4,40,1024]{2,1,0:T(8,128)(2,1)S(1)}, u32[]{:S(2)}, u32[]{:S(2)}) collective-permute-start(bf16[4,40,1024]{2,1,0:T(8,128)(2,1)} %get-tuple-element.73), channel_id=1, source_target_pairs={{0,2},{1,3},{2,0},{3,1},{4,6},{5,7},{6,4},{7,5},{8,10},{9,11},{10,... | collective-permute-start | bytes 983048 | tf_op jit(solution)/shard_map/ppermute | solution.py:335
  205.2 1.0 copy-start
  206.2 23.2 %copy-start.1 = (f32[128,2048]{1,0:T(8,128)S(1)}, f32[128,2048]{1,0:T(8,128)}, u32[]{:S(2)}) copy-start(f32[128,2048]{1,0:T(8,128)} %copy-done) | copy-start | bytes 3145732
  206.2 23.2 %collective-permute-start.18 = (bf16[128,2048]{1,0:T(8,128)(2,1)}, bf16[128,2048]{1,0:T(8,128)(2,1)S(1)}, u32[]{:S(2)}, u32[]{:S(2)}) collective-permute-start(bf16[128,2048]{1,0:T(8,128)(2,1)} %get-tuple-element.63), channel_id=1, source_target_pairs={{0,24},{1,25},{2,26},{3,27},{4,28},{5,29},{6,30},{7,31},{8,0},{9,1... | collective-permute-start | bytes 1572872 | tf_op jit(solution)/shard_map/ppermute | solution.py:335
  209.8 23.2 %collective-permute-start.31 = (bf16[4,40,1024]{2,1,0:T(8,128)(2,1)}, bf16[4,40,1024]{2,1,0:T(8,128)(2,1)}, u32[]{:S(2)}, u32[]{:S(2)}) collective-permute-start(bf16[4,40,1024]{2,1,0:T(8,128)(2,1)} %shard_map.98), channel_id=1, source_target_pairs={{0,6},{1,7},{2,4},{3,5},{4,2},{5,3},{6,0},{7,1},{8,14},{9,15},{10,... | collective-permute-start | bytes 983048 | tf_op jit(solution)/shard_map/ppermute | solution.py:335
  211.4 21.6 %collective-permute-start.30 = (bf16[4,40,1024]{2,1,0:T(8,128)(2,1)}, bf16[4,40,1024]{2,1,0:T(8,128)(2,1)}, u32[]{:S(2)}, u32[]{:S(2)}) collective-permute-start(bf16[4,40,1024]{2,1,0:T(8,128)(2,1)} %shard_map.97), channel_id=1, source_target_pairs={{0,4},{1,5},{2,6},{3,7},{4,0},{5,1},{6,2},{7,3},{8,12},{9,13},{10,... | collective-permute-start | bytes 983048 | tf_op jit(solution)/shard_map/ppermute | solution.py:335
  211.8 21.1 %collective-permute-start.29 = (bf16[4,40,1024]{2,1,0:T(8,128)(2,1)}, bf16[4,40,1024]{2,1,0:T(8,128)(2,1)}, u32[]{:S(2)}, u32[]{:S(2)}) collective-permute-start(bf16[4,40,1024]{2,1,0:T(8,128)(2,1)} %shard_map.96), channel_id=1, source_target_pairs={{0,2},{1,3},{2,0},{3,1},{4,6},{5,7},{6,4},{7,5},{8,10},{9,11},{10,... | collective-permute-start | bytes 983048 | tf_op jit(solution)/shard_map/ppermute | solution.py:335
  214.9 14.5 %collective-permute-start.26 = (bf16[4,40,1024]{2,1,0:T(8,128)(2,1)}, bf16[4,40,1024]{2,1,0:T(8,128)(2,1)}, u32[]{:S(2)}, u32[]{:S(2)}) collective-permute-start(bf16[4,40,1024]{2,1,0:T(8,128)(2,1)} %copy-done.14), channel_id=1, source_target_pairs={{0,4},{1,5},{2,6},{3,7},{4,0},{5,1},{6,2},{7,3},{8,12},{9,13},{10,... | collective-permute-start | bytes 983048 | tf_op jit(solution)/shard_map/ppermute | solution.py:335
  216.4 25.5 %copy-start.6 = (f32[128,8]{1,0:T(8,128)S(1)}, f32[128,8]{1,0:T(8,128)}, u32[]{:S(2)}) copy-start(f32[128,8]{1,0:T(8,128)} %get-tuple-element.97.refs_0_) | copy-start | bytes 12292
  219.7 13.3 %all-to-all-start = ((f32[16,1,80]{2,1,0:T(1,128)}), f32[16,1,80]{2,1,0:T(1,128)S(1)}, u32[]{:S(2)}, u32[]{:S(2)}) async-start(f32[16,1,80]{2,1,0:T(1,128)} %bitcast.19), calls=%async_computation | async-start | bytes 16384 | tf_op jit(solution)/shard_map/all_to_all | solution.py:383
  232.4 34.0 %collective-permute-start.28 = (bf16[128,1024]{1,0:T(8,128)(2,1)}, bf16[128,1024]{1,0:T(8,128)(2,1)S(1)}, u32[]{:S(2)}, u32[]{:S(2)}) collective-permute-start(bf16[128,1024]{1,0:T(8,128)(2,1)} %get-tuple-element.76.refs_6_), channel_id=1, source_target_pairs={{0,16},{1,17},{2,18},{3,19},{4,20},{5,21},{6,22},{7,23},{8,24},{9,... | collective-permute-start | bytes 786440 | tf_op jit(solution)/shard_map/ppermute | solution.py:335
  233.0 1.0 copy-start.13
  237.1 29.2 %collective-permute-start.32 = (bf16[128,1024]{1,0:T(8,128)(2,1)}, bf16[128,1024]{1,0:T(8,128)(2,1)S(1)}, u32[]{:S(2)}, u32[]{:S(2)}) collective-permute-start(bf16[128,1024]{1,0:T(8,128)(2,1)} %get-tuple-element.83), channel_id=1, source_target_pairs={{0,16},{1,17},{2,18},{3,19},{4,20},{5,21},{6,22},{7,23},{8,24},{9,... | collective-permute-start | bytes 786440 | tf_op jit(solution)/shard_map/ppermute | solution.py:335
  239.4 26.9 %collective-permute-start.34 = (bf16[128,1024]{1,0:T(8,128)(2,1)S(1)}, bf16[128,1024]{1,0:T(8,128)(2,1)S(1)}, u32[]{:S(2)}, u32[]{:S(2)}) collective-permute-start(bf16[128,1024]{1,0:T(8,128)(2,1)S(1)} %get-tuple-element.85), channel_id=1, source_target_pairs={{0,8},{1,9},{2,10},{3,11},{4,12},{5,13},{6,14},{7,15},{8,16},{9,17... | collective-permute-start | bytes 786440 | tf_op jit(solution)/shard_map/ppermute | solution.py:335
  239.4 26.9 %collective-permute-start.33 = (bf16[128,1024]{1,0:T(8,128)(2,1)S(1)}, bf16[128,1024]{1,0:T(8,128)(2,1)S(1)}, u32[]{:S(2)}, u32[]{:S(2)}) collective-permute-start(bf16[128,1024]{1,0:T(8,128)(2,1)S(1)} %get-tuple-element.84), channel_id=1, source_target_pairs={{0,8},{1,9},{2,10},{3,11},{4,12},{5,13},{6,14},{7,15},{8,16},{9,17... | collective-permute-start | bytes 786440 | tf_op jit(solution)/shard_map/ppermute | solution.py:335
  (5 other events, 3.6 us)
